TPU v7x, 32 devices: a whole 2x2x4 slice. The times are simulated.
32 devices in a mesh: wide: 8 (over z, x), narrow: 4 (over y, core).
Axes of the slice: x: 2, y: 2, z: 4, core: 2. Of those that a mesh axis runs over, the one named last changes fastest.
Arguments:
- token_ids: int32 [2, 32, 256], P(None, ('wide', 'narrow')), may hold values from 0 to 50256
- doc_ids: int32 [2, 32, 256], P(None, ('wide', 'narrow')), may hold values from 0 to 7, never falling along the last dimension, each value on 1 to 128 neighbouring positions
- loss_positions: int32 [2, 32, 32], P(None, ('wide', 'narrow')), may hold values from 0 to 254
- tied_table_master: float32 [50304, 1024], P(('wide', 'narrow')), may hold values from -0.375 to 0.375
- qkv_master: float32 [1024, 3072], P(('wide', 'narrow')), may hold values from -0.1875 to 0.1875
- out_master: float32 [1024, 1024], P(('wide', 'narrow')), may hold values from -0.75 to 0.75
- up_master: float32 [1024, 4096], P(('wide', 'narrow')), may hold values from -0.1875 to 0.1875
- down_master: float32 [4096, 1024], P(('wide', 'narrow')), may hold values from -0.09375 to 0.09375
- norm_master: float32 [1024, 6], P(('wide', 'narrow')), may hold values from -1 to 1.5, as said below
- table_first_moment: float32 [50304, 1024], P(('wide', 'narrow')), may hold values from -8.34465e-07 to 8.34465e-07
- first_qkv: float32 [1024, 3072], P(('wide', 'narrow')), may hold values from -8.34465e-07 to 8.34465e-07
- first_out: float32 [1024, 1024], P(('wide', 'narrow')), may hold values from -8.34465e-07 to 8.34465e-07
- first_up: float32 [1024, 4096], P(('wide', 'narrow')), may hold values from -8.34465e-07 to 8.34465e-07
- first_down: float32 [4096, 1024], P(('wide', 'narrow')), may hold values from -8.34465e-07 to 8.34465e-07
- first_norms: float32 [1024, 6], P(('wide', 'narrow')), may hold values from -3.33786e-06 to 3.33786e-06
- table_second_moment: float32 [50304, 1024], P(('wide', 'narrow')), may hold values from 1.5600538e-15 to 6.2402154e-15
- second_qkv: float32 [1024, 3072], P(('wide', 'narrow')), may hold values from 1.5600538e-15 to 6.2402154e-15
- second_out: float32 [1024, 1024], P(('wide', 'narrow')), may hold values from 1.5600538e-15 to 6.2402154e-15
- second_up: float32 [1024, 4096], P(('wide', 'narrow')), may hold values from 1.5600538e-15 to 6.2402154e-15
- second_down: float32 [4096, 1024], P(('wide', 'narrow')), may hold values from 1.5600538e-15 to 6.2402154e-15
- second_norms: float32 [1024, 6], P(('wide', 'narrow')), may hold values from 2.4960862e-14 to 9.9843446e-14
Outputs:
- loss_value: float32 [], replicated
- grad_norm: float32 [], replicated
- matrix_norms: float32 [3, 6], replicated
- new_table: float32 [50304, 1024], P(('wide', 'narrow'))
- new_qkv: float32 [1024, 3072], P(('wide', 'narrow'))
- new_out: float32 [1024, 1024], P(('wide', 'narrow'))
- new_up: float32 [1024, 4096], P(('wide', 'narrow'))
- new_down: float32 [4096, 1024], P(('wide', 'narrow'))
- new_norms: float32 [1024, 6], P(('wide', 'narrow'))
- new_first_table: float32 [50304, 1024], P(('wide', 'narrow'))
- new_first_qkv: float32 [1024, 3072], P(('wide', 'narrow'))
- new_first_out: float32 [1024, 1024], P(('wide', 'narrow'))
- new_first_up: float32 [1024, 4096], P(('wide', 'narrow'))
- new_first_down: float32 [4096, 1024], P(('wide', 'narrow'))
- new_first_norms: float32 [1024, 6], P(('wide', 'narrow'))
- new_second_table: float32 [50304, 1024], P(('wide', 'narrow'))
- new_second_qkv: float32 [1024, 3072], P(('wide', 'narrow'))
- new_second_out: float32 [1024, 1024], P(('wide', 'narrow'))
- new_second_up: float32 [1024, 4096], P(('wide', 'narrow'))
- new_second_down: float32 [4096, 1024], P(('wide', 'narrow'))
- new_second_norms: float32 [1024, 6], P(('wide', 'narrow'))
Inputs may be any that keep to these rules, and one draw needn't show every extreme that they name: `doc_ids`: within a sequence document numbers never fall. `norm_master`: columns 0, 2 and 4 are gains, columns 1, 3 and 5 shifts.
All inputs are finite; a program needn't handle non-finite values.
Results may differ from a plain program's by a relative error of at most 0.0095.
The roundings to bfloat16 on the way count: a program that leaves them out, or rounds other values in their place, can miss the bound.
Values may be sent and summed in bfloat16 or wider, within the bound.
No kernel may reach another device: no remote copies, remote signals or barrier semaphores. Data moves between devices by JAX's collectives and lax.ppermute only.
A program may use at most 384 MiB of HBM per device.

v0:
```python
import jax
import jax.numpy as jnp
from jax import lax
from jax.sharding import PartitionSpec as P

HEAD_DIM = 64
VOCAB = 50257


neg_fill = -1e30
beta_first = 0.9
beta_second = 0.999
adam_epsilon = 1e-12
decay_rates = (0.01, 0.01, 0.01, 0.01, 0.01, 0.0)
learn_rate = 0.5
clip_limit = 0.01
norm_epsilon = 1e-05
step_count = 5.0
query_rows = 512


def layer_norm(values, gain_row, offset):
    centered = values - jnp.mean(values, axis=-1, keepdims=True)
    spread = jnp.mean(centered * centered, axis=-1, keepdims=True)
    return centered * lax.rsqrt(spread + norm_epsilon) * gain_row + offset


def norm_backward(values, gain_row, offset, grad_output):
    unused, pullback = jax.vjp(layer_norm, values, gain_row, offset)
    return pullback(grad_output)


def gelu_tanh(values):
    return jax.nn.gelu(values, approximate=True)


def matmul(left_side, right_side):
    return jnp.dot(left_side, right_side, preferred_element_type=jnp.float32)


def contract_rows(left_side, right_side):
    return lax.dot_general(
        left_side, right_side, (((0,), (0,)), ((), ())), preferred_element_type=jnp.float32
    )


def contract_cols(left_side, right_side):
    return lax.dot_general(
        left_side, right_side, (((1,), (1,)), ((), ())), preferred_element_type=jnp.float32
    )


def gather_layer(layer_shards):
    qkv_part, out_part, up_part, down_part, gain_part = [
        weight_shard.astype(jnp.bfloat16) for weight_shard in layer_shards
    ]
    return (
        lax.all_gather(qkv_part, ("wide", "narrow"), axis=0, tiled=True),
        lax.all_gather(out_part, ("wide", "narrow"), axis=0, tiled=True),
        lax.all_gather(up_part, ("wide", "narrow"), axis=0, tiled=True),
        lax.all_gather(down_part, ("wide", "narrow"), axis=0, tiled=True),
        lax.all_gather(gain_part, ("wide", "narrow"), axis=0, tiled=True),
    )


def block_scores(query_part, keys_all, docs_query, documents, row_start):
    scores = jnp.einsum(
        "qhd,khd->hqk", query_part, keys_all, preferred_element_type=jnp.float32
    ) * HEAD_DIM ** (-0.5)
    query_place = row_start + jnp.arange(query_part.shape[0])
    key_place = jnp.arange(keys_all.shape[0])
    allowed = (key_place[None, :] <= query_place[:, None]) & (
        documents[None, :] == docs_query[:, None]
    )
    return jnp.where(allowed[None], scores, neg_fill)


def attention_forward(queries, keys_all, values_all, documents):
    length = queries.shape[0]
    block_rows = min(query_rows, length)

    def one_block(block_index):
        row_start = block_index * block_rows
        scores = block_scores(queries, keys_all, documents, documents, row_start)
        top_score = jnp.max(scores, axis=-1, keepdims=True)
        exp_scores = jnp.exp(scores - top_score)
        exp_total = jnp.sum(exp_scores, axis=-1, keepdims=True)
        prob_low = (exp_scores / exp_total).astype(jnp.bfloat16)
        context = jnp.einsum(
            "hqk,khd->qhd", prob_low, values_all, preferred_element_type=jnp.float32
        )
        return (context, top_score[..., 0] + jnp.log(exp_total[..., 0]))

    contexts, log_totals = lax.map(one_block, jnp.arange(length // block_rows))
    return (contexts.reshape(length, -1), log_totals)


def attention_backward(queries, keys_all, values_all, documents, log_totals, grad_context):
    length = queries.shape[0]
    block_rows = min(query_rows, length)

    def one_block(carried, block_index):
        key_grad, value_grad = carried
        row_start = block_index * block_rows
        scores = block_scores(queries, keys_all, documents, documents, row_start)
        probs = jnp.exp(scores - log_totals[block_index][..., None])
        prob_low = probs.astype(jnp.bfloat16)
        grad_probs = jnp.einsum(
            "qhd,khd->hqk", grad_context, values_all, preferred_element_type=jnp.float32
        )
        inner = jnp.sum(probs * grad_probs, axis=-1, keepdims=True)
        grad_scores = (probs * (grad_probs - inner)).astype(jnp.bfloat16)
        query_grad = jnp.einsum(
            "hqk,khd->qhd", grad_scores, keys_all, preferred_element_type=jnp.float32
        ) * HEAD_DIM ** (-0.5)
        key_grad = key_grad + jnp.einsum(
            "hqk,qhd->khd", grad_scores, queries, preferred_element_type=jnp.float32
        ) * HEAD_DIM ** (-0.5)
        value_grad = value_grad + jnp.einsum(
            "hqk,qhd->khd", prob_low, grad_context, preferred_element_type=jnp.float32
        )
        return ((key_grad, value_grad), query_grad)

    zero_grad = jnp.zeros(keys_all.shape, jnp.float32)
    (key_grad, value_grad), query_grads = lax.scan(
        one_block, (zero_grad, zero_grad), jnp.arange(length // block_rows)
    )
    return (query_grads.reshape(keys_all.shape), key_grad, value_grad)


def layer_forward(x_embed, weights, documents):
    qkv_weight, out_weight, up_weight, down_weight, gain_table = weights
    gain_entries = gain_table.astype(jnp.float32)
    length = x_embed.shape[0]
    head_count = x_embed.shape[1] // HEAD_DIM
    normed_one = layer_norm(x_embed, gain_entries[:, 0], gain_entries[:, 1]).astype(jnp.bfloat16)
    qkv_all = (
        matmul(normed_one, qkv_weight).astype(jnp.bfloat16).reshape(length, 3, head_count, HEAD_DIM)
    )
    context, log_totals = attention_forward(qkv_all[:, 0], qkv_all[:, 1], qkv_all[:, 2], documents)
    context = context.astype(jnp.bfloat16)
    x_attn = x_embed + matmul(context, out_weight)
    normed_two = layer_norm(x_attn, gain_entries[:, 2], gain_entries[:, 3]).astype(jnp.bfloat16)
    up_value = matmul(normed_two, up_weight)
    activated = gelu_tanh(up_value).astype(jnp.bfloat16)
    x_out = x_attn + matmul(activated, down_weight)
    return (
        x_out,
        (
            x_embed,
            normed_one,
            qkv_all,
            context,
            log_totals,
            x_attn,
            normed_two,
            up_value,
            activated,
        ),
    )


def layer_backward(grad_output, kept, weights, documents):
    x_embed, normed_one, qkv_all, context, log_totals, x_attn, normed_two, up_value, activated = (
        kept
    )
    qkv_weight, out_weight, up_weight, down_weight, gain_table = weights
    gain_entries = gain_table.astype(jnp.float32)
    length = x_embed.shape[0]
    grad_mlp = grad_output.astype(jnp.bfloat16)
    grad_down = contract_rows(activated, grad_mlp)
    grad_act = contract_cols(grad_mlp, down_weight)
    unused, gelu_pull = jax.vjp(gelu_tanh, up_value)
    grad_up_low = gelu_pull(grad_act)[0].astype(jnp.bfloat16)
    grad_up = contract_rows(normed_two, grad_up_low)
    grad_normed_two = contract_cols(grad_up_low, up_weight)
    grad_x_attn, gain_two, shift_two = norm_backward(
        x_attn, gain_entries[:, 2], gain_entries[:, 3], grad_normed_two
    )
    grad_x_attn = grad_output + grad_x_attn
    grad_attn_low = grad_x_attn.astype(jnp.bfloat16)
    grad_out_weight = contract_rows(context, grad_attn_low)
    grad_context = (
        contract_cols(grad_attn_low, out_weight).astype(jnp.bfloat16).reshape(qkv_all[:, 0].shape)
    )
    query_grad, key_grad, value_grad = attention_backward(
        qkv_all[:, 0], qkv_all[:, 1], qkv_all[:, 2], documents, log_totals, grad_context
    )
    grad_qkv_low = (
        jnp.stack([query_grad, key_grad, value_grad], axis=1)
        .reshape(length, -1)
        .astype(jnp.bfloat16)
    )
    grad_qkv = contract_rows(normed_one, grad_qkv_low)
    grad_normed_one = contract_cols(grad_qkv_low, qkv_weight)
    grad_x_embed, gain_one, shift_one = norm_backward(
        x_embed, gain_entries[:, 0], gain_entries[:, 1], grad_normed_one
    )
    gain_grads = jnp.stack([gain_one, shift_one, gain_two, shift_two], axis=1)
    return (grad_x_attn + grad_x_embed, (grad_qkv, grad_out_weight, grad_up, grad_down), gain_grads)


def add_lists(earlier, later):
    if earlier is None:
        return list(later)
    return [first_term + second_term for first_term, second_term in zip(earlier, later)]


def per_device(
    token_ids,
    doc_ids,
    loss_positions,
    tied_table_master,
    qkv_master,
    out_master,
    up_master,
    down_master,
    norm_master,
    table_first_moment,
    first_qkv,
    first_out,
    first_up,
    first_down,
    first_norms,
    table_second_moment,
    second_qkv,
    second_out,
    second_up,
    second_down,
    second_norms,
):
    micro_count = token_ids.shape[0]
    picked_count = loss_positions.shape[2]
    narrow_count = lax.axis_size("narrow")
    wide_count = lax.axis_size("wide")
    count_all = micro_count * wide_count * narrow_count * picked_count
    block_size = tied_table_master.shape[0]
    narrow_place = lax.axis_index("narrow")
    local_place = jnp.arange(block_size * wide_count)
    columns = (
        local_place // block_size * narrow_count + narrow_place
    ) * block_size + local_place % block_size
    valid_cols = columns < VOCAB
    table_low = tied_table_master.astype(jnp.bfloat16)
    table_full = lax.all_gather(table_low, "wide", axis=0, tiled=True)
    group_tokens, group_picks = (
        lax.all_gather(token_ids, "narrow", axis=1, tiled=True),
        lax.all_gather(loss_positions, "narrow", axis=1, tiled=True),
    )
    id_block = group_tokens // block_size
    inside = id_block % narrow_count == narrow_place
    row_index = jnp.where(
        inside, id_block // narrow_count * block_size + group_tokens % block_size, 0
    )
    layer_shards = (qkv_master, out_master, up_master, down_master, norm_master)
    grad_table = jnp.zeros(table_full.shape, jnp.float32)
    loss_local = jnp.zeros((), jnp.float32)
    summed_grads = None
    for micro_index in range(micro_count):
        forward_weights = gather_layer(layer_shards)
        looked = jnp.where(
            inside[micro_index][..., None], table_full[row_index[micro_index]], 0.0
        ).astype(jnp.float32)
        x_embed = lax.psum_scatter(
            looked.astype(jnp.bfloat16), "narrow", scatter_dimension=0, tiled=True
        ).astype(jnp.float32)[0]
        documents = doc_ids[micro_index, 0]
        x_out, kept = layer_forward(x_embed, forward_weights, documents)
        gain_entries = forward_weights[4].astype(jnp.float32)
        final_norm = layer_norm(x_out, gain_entries[:, 4], gain_entries[:, 5])
        own_picks = loss_positions[micro_index, 0]
        picked_low = final_norm[own_picks].astype(jnp.bfloat16)
        head_rows = lax.all_gather(picked_low, "narrow", axis=0, tiled=True)
        logits = contract_cols(head_rows, table_full)
        logits = jnp.where(valid_cols[None, :], logits, neg_fill)
        targets = jnp.take_along_axis(
            group_tokens[micro_index], group_picks[micro_index] + 1, axis=1
        ).reshape(-1)
        target_hits = targets[:, None] == columns[None, :]
        own_target = jnp.sum(jnp.where(target_hits, logits, 0.0), axis=1)
        local_top = jnp.max(logits, axis=1)
        top_logit = lax.pmax(local_top, "narrow")
        local_total = jnp.sum(jnp.exp(logits - top_logit[:, None]), axis=1)
        exp_total = lax.psum(local_total, "narrow")
        log_total = top_logit + jnp.log(exp_total)
        own_log = jnp.sum(
            lax.dynamic_slice_in_dim(log_total, narrow_place * picked_count, picked_count, 0)
        )
        loss_local = loss_local + own_log - jnp.sum(own_target)
        grad_logits = (
            (jnp.exp(logits - log_total[:, None]) - target_hits.astype(jnp.float32)) / count_all
        ).astype(jnp.bfloat16)
        grad_micro = contract_rows(grad_logits, head_rows)
        grad_picked = lax.psum_scatter(
            matmul(grad_logits, table_full), "narrow", scatter_dimension=0, tiled=True
        )
        grad_final = jnp.zeros_like(final_norm).at[own_picks].add(grad_picked)
        grad_x_out, gain_last, shift_last = norm_backward(
            x_out, gain_entries[:, 4], gain_entries[:, 5], grad_final
        )
        backward_weights = gather_layer(layer_shards)
        grad_embed, weight_grads, gain_grads = layer_backward(
            grad_x_out, kept, backward_weights, documents
        )
        gain_grads = jnp.concatenate(
            [gain_grads, jnp.stack([gain_last, shift_last], axis=1)], axis=1
        )
        grad_group = lax.all_gather(grad_embed[None], "narrow", axis=0, tiled=True)
        masked_grad = jnp.where(inside[micro_index][..., None], grad_group, 0.0)
        grad_micro = grad_micro.at[row_index[micro_index]].add(masked_grad)
        new_terms = list(weight_grads) + [gain_grads]
        grad_table = grad_table + grad_micro
        summed_grads = add_lists(summed_grads, new_terms)
    reduced = (
        lax.psum_scatter(summed_grads[0], ("wide", "narrow"), scatter_dimension=0, tiled=True),
        lax.psum_scatter(summed_grads[1], ("wide", "narrow"), scatter_dimension=0, tiled=True),
        lax.psum_scatter(summed_grads[2], ("wide", "narrow"), scatter_dimension=0, tiled=True),
        lax.psum_scatter(summed_grads[3], ("wide", "narrow"), scatter_dimension=0, tiled=True),
        lax.psum_scatter(summed_grads[4], ("wide", "narrow"), scatter_dimension=0, tiled=True),
    )
    table_grad = lax.psum_scatter(grad_table, "wide", scatter_dimension=0, tiled=True)
    all_grads = (table_grad,) + tuple(reduced)
    masters = (tied_table_master, qkv_master, out_master, up_master, down_master, norm_master)
    firsts = (table_first_moment, first_qkv, first_out, first_up, first_down, first_norms)
    seconds = (table_second_moment, second_qkv, second_out, second_up, second_down, second_norms)
    grad_squares = jnp.stack([jnp.sum(gradient * gradient) for gradient in all_grads])
    weight_squares = jnp.stack([jnp.sum(weight * weight) for weight in masters])
    grad_total, weight_total, loss_total = lax.psum(
        (grad_squares, weight_squares, loss_local), ("wide", "narrow")
    )
    grad_norm = jnp.sqrt(jnp.sum(grad_total))
    factor = jnp.minimum(1.0, clip_limit / grad_norm)
    new_firsts = []
    new_seconds = []
    directions = []
    for group_index in range(6):
        clipped = factor * all_grads[group_index]
        first_new = beta_first * firsts[group_index] + (1.0 - beta_first) * clipped
        second_new = beta_second * seconds[group_index] + (1.0 - beta_second) * clipped * clipped
        direction = (
            first_new
            / (1.0 - beta_first**step_count)
            / (jnp.sqrt(second_new / (1.0 - beta_second**step_count)) + adam_epsilon)
            + decay_rates[group_index] * masters[group_index]
        )
        new_firsts.append(first_new)
        new_seconds.append(second_new)
        directions.append(direction)
    update_total = lax.psum(
        jnp.stack([jnp.sum(direction * direction) for direction in directions]), ("wide", "narrow")
    )
    weight_norms = jnp.sqrt(weight_total)
    update_norms = jnp.sqrt(update_total)
    new_weights = [
        masters[group_index]
        - learn_rate
        * (weight_norms[group_index] / update_norms[group_index])
        * directions[group_index]
        for group_index in range(6)
    ]
    matrix_norms = jnp.stack([factor * jnp.sqrt(grad_total), weight_norms, update_norms])
    return (
        loss_total / count_all,
        grad_norm,
        matrix_norms,
        new_weights[0],
        new_weights[1],
        new_weights[2],
        new_weights[3],
        new_weights[4],
        new_weights[5],
        new_firsts[0],
        new_firsts[1],
        new_firsts[2],
        new_firsts[3],
        new_firsts[4],
        new_firsts[5],
        new_seconds[0],
        new_seconds[1],
        new_seconds[2],
        new_seconds[3],
        new_seconds[4],
        new_seconds[5],
    )


def solution(mesh):
    return jax.shard_map(
        per_device,
        mesh=mesh,
        in_specs=(
            P(None, ("wide", "narrow"), None),
            P(None, ("wide", "narrow"), None),
            P(None, ("wide", "narrow"), None),
            P(("wide", "narrow"), None),
            P(("wide", "narrow"), None),
            P(("wide", "narrow"), None),
            P(("wide", "narrow"), None),
            P(("wide", "narrow"), None),
            P(("wide", "narrow"), None),
            P(("wide", "narrow"), None),
            P(("wide", "narrow"), None),
            P(("wide", "narrow"), None),
            P(("wide", "narrow"), None),
            P(("wide", "narrow"), None),
            P(("wide", "narrow"), None),
            P(("wide", "narrow"), None),
            P(("wide", "narrow"), None),
            P(("wide", "narrow"), None),
            P(("wide", "narrow"), None),
            P(("wide", "narrow"), None),
            P(("wide", "narrow"), None),
        ),
        out_specs=(
            P(),
            P(),
            P(),
            P(("wide", "narrow"), None),
            P(("wide", "narrow"), None),
            P(("wide", "narrow"), None),
            P(("wide", "narrow"), None),
            P(("wide", "narrow"), None),
            P(("wide", "narrow"), None),
            P(("wide", "narrow"), None),
            P(("wide", "narrow"), None),
            P(("wide", "narrow"), None),
            P(("wide", "narrow"), None),
            P(("wide", "narrow"), None),
            P(("wide", "narrow"), None),
            P(("wide", "narrow"), None),
            P(("wide", "narrow"), None),
            P(("wide", "narrow"), None),
            P(("wide", "narrow"), None),
            P(("wide", "narrow"), None),
            P(("wide", "narrow"), None),
        ),
        check_vma=False,
    )
```

profile of v0, /device:TPU:0, one launch (start us, length us, event | category | flops | bytes accessed | tf_op | source)
XLA Modules:
  0.0 2729.1 jit_solution(12251236713326640974)
XLA Ops:
  21.2 487.5 %all-gather.24.cloned.1.call-done = bf16[8,1572,1024]{2,1,0:T(8,128)(2,1)} async-done(((bf16[1,1572,1024]{2,1,0:T(8,128)(2,1)}), bf16[8,1572,1024]{2,1,0:T(8,128)(2,1)}) %all-gather.24.cloned.1.call-update) | async-done | bytes 25755664 | tf_op jit(solution)/shard_map/all_gather | solution.py:245
  508.7 27.2 reshape.705
  535.9 16.6 gather_fusion.2
  559.0 41.2 %all-gather.3 = bf16[32,32,6]{1,2,0:T(8,128)(2,1)S(1)} all-gather(bf16[1,32,6]{1,2,0:T(8,128)(2,1)S(1)} %convert_bitcast_fusion.3), channel_id=1, replica_groups=mesh['wide'=8,'narrow'=4] {'wide','narrow'}, dimensions={0}, use_global_device_ids=true | all-gather | bytes 12672 | tf_op jit(solution)/shard_map/all_gather | solution.py:62
  611.3 16.8 gather_fusion
  645.5 41.4 %all-gather.14.cloned.1.call-done = bf16[1024,1024]{1,0:T(8,128)(2,1)} async-done(((bf16[32,1024]{1,0:T(8,128)(2,1)}), bf16[1024,1024]{1,0:T(8,128)(2,1)}) %all-gather.14.cloned.1.call-update) | async-done | bytes 2097168 | tf_op jit(solution)/shard_map/all_gather | solution.py:59
  689.9 76.9 %all-gather.16.cloned.1.call-done = bf16[1024,4096]{1,0:T(8,128)(2,1)} async-done(((bf16[32,4096]{1,0:T(8,128)(2,1)}), bf16[1024,4096]{1,0:T(8,128)(2,1)}) %all-gather.16.cloned.1.call-update) | async-done | bytes 8388624 | tf_op jit(solution)/shard_map/all_gather | solution.py:60
  774.6 71.9 %all-gather.18.cloned.1.call-done = bf16[4096,1024]{1,0:T(8,128)(2,1)} async-done(((bf16[128,1024]{1,0:T(8,128)(2,1)}), bf16[4096,1024]{1,0:T(8,128)(2,1)}) %all-gather.18.cloned.1.call-update) | async-done | bytes 8388624 | tf_op jit(solution)/shard_map/all_gather | solution.py:61
  896.0 15.5 fusion.186
  911.6 15.4 fusion.185
  950.5 14.8 fusion.151
  965.5 14.8 fusion.154
  988.4 22.1 reduce-scatter.18.cloned.1.call-done
  1109.4 10.9 fusion.143
  1120.3 12.0 convolution_add_fusion.1
  1148.7 21.7 fusion.156
  1170.5 35.2 %convolution_add_fusion = f32[12576,1024]{1,0:T(8,128)} fusion(f32[12576,1024]{1,0:T(8,128)} %fusion.156, bf16[128,1024]{1,0:T(8,128)(2,1)S(1)} %copy-done.50, f32[128,12576]{0,1:T(8,128)} %get-tuple-element.258, f32[128]{0:T(128)S(1)} %copy-done.124, s32[128]{0:T(128)S(1)} %copy-done.108, s32[12576]{0:T(1024)S(1)} %copy-done.46), kind=kOutput, calls=%fused_computation.9 | convolution fusion | flops 3319259136 | bytes 109774976 | tf_op jit(solution)/shard_map/dot_general | solution.py:42
  1217.9 51.9 %scatter_fusion = f32[12576,1024]{1,0:T(8,128)} fusion(f32[12576,1024]{1,0:T(8,128)} %convolution_add_fusion, s32[2048]{0:T(1024)S(1)} %bitcast.350, f32[2048,1024]{1,0:T(8,128)} %bitcast.297), kind=kCustom, calls=%fused_computation.8 | custom fusion | flops 2097152 | bytes 25174016 | tf_op jit(solution)/shard_map/add | solution.py:312
  1269.8 1151.0 %fusion = f32[1584,1024]{1,0:T(8,128)} fusion(f32[12576,1024]{1,0:T(8,128)} %scatter_fusion), kind=kCustom, calls=%all-reduce-scatter | all-reduce-scatter fusion | flops 12976129 | bytes 57999872
  2434.9 18.3 concatenate.24
  2463.6 101.7 %reduce-scatter.26.cloned.1.call-done = f32[32,4096]{1,0:T(8,128)} async-done(((f32[1024,4096]{1,0:T(8,128)}), f32[32,4096]{1,0:T(8,128)}) %reduce-scatter.26.cloned.1.call-update) | async-done | bytes 524304 | tf_op jit(solution)/shard_map/reduce_scatter | solution.py:317
  2571.7 48.3 %psum.45 = f32[6]{0:T(128)S(1)} all-reduce(f32[6]{0:T(128)S(1)} %stack.153), channel_id=1, replica_groups=mesh['wide'=8,'narrow'=4] {'wide','narrow'}, use_global_device_ids=true, to_apply=%region_74.76 | all-reduce | flops 6 | bytes 48 | tf_op jit(solution)/shard_map/psum | solution.py:328
  2622.1 14.8 multiply_reduce_fusion.1
  2652.4 39.0 %all-reduce.2 = (f32[]{:T(128)}, f32[6]{0:T(128)}, f32[6]{0:T(128)}) all-reduce(f32[]{:T(128)S(6)} %sub.262, f32[6]{0:T(128)} %stack.169, f32[6]{0:T(128)} %stack.161), channel_id=1, replica_groups=mesh['wide'=8,'narrow'=4] {'wide','narrow'}, use_global_device_ids=true, to_apply=%region_30.32 | all-reduce | flops 13 | bytes 104 | tf_op jit(solution)/shard_map/psum | solution.py:328
  (559 shorter events, 328.6 us)
Async XLA Ops:
  8.0 500.7 %all-gather.24.cloned.1.call-start = ((), (), s32[]{:S(2)}) async-start(), calls=%async_computation.23 | async-start | bytes 29048832 | tf_op jit(solution)/shard_map/all_gather | solution.py:245
  13.1 616.9 %reduce-scatter.16.cloned.1.call-start = ((), (), s32[]{:S(2)}) async-start(), calls=%async_computation.14 | async-start | bytes 2621440 | tf_op jit(solution)/shard_map/reduce_scatter | solution.py:264
  20.6 590.3 %copy-start.97 = (s32[4,256,1]{1,2,0:T(1,128)}, s32[4,256,1]{1,2,0:T(1,128)S(1)}, u32[]{:S(2)}) copy-start(s32[4,256,1]{1,2,0:T(1,128)S(1)} %get-tuple-element.202) | copy-start | bytes 12292
  554.9 77.7 %all-gather.12.cloned.1.call-start = ((), (), s32[]{:S(2)}) async-start(), calls=%async_computation.10 | async-start | bytes 6488064 | tf_op jit(solution)/shard_map/all_gather | solution.py:58
  555.7 131.3 %all-gather.14.cloned.1.call-start = ((), (), s32[]{:S(2)}) async-start(), calls=%async_computation.11 | async-start | bytes 2162688 | tf_op jit(solution)/shard_map/all_gather | solution.py:59
  557.3 209.5 %all-gather.16.cloned.1.call-start = ((), (), s32[]{:S(2)}) async-start(), calls=%async_computation.12 | async-start | bytes 8650752 | tf_op jit(solution)/shard_map/all_gather | solution.py:60
  558.1 288.4 %all-gather.18.cloned.1.call-start = ((), (), s32[]{:S(2)}) async-start(), calls=%async_computation.13 | async-start | bytes 8650752 | tf_op jit(solution)/shard_map/all_gather | solution.py:61
  559.0 296.0 %reduce-scatter.14.cloned.1.call-start = ((), (), s32[]{:S(2)}) async-start(), calls=%async_computation.9 | async-start | bytes 2621440 | tf_op jit(solution)/shard_map/reduce_scatter | solution.py:264
  611.0 261.7 %copy-start.77 = (f32[1024,1]{0,1:T(1,128)}, f32[1024,1]{0,1:T(1,128)S(1)}, u32[]{:S(2)}) copy-start(f32[1024,1]{0,1:T(1,128)S(1)} %get-tuple-element.193) | copy-start | bytes 12292
  611.1 268.1 %copy-start.91 = (f32[1024,1]{0,1:T(1,128)}, f32[1024,1]{0,1:T(1,128)S(1)}, u32[]{:S(2)}) copy-start(f32[1024,1]{0,1:T(1,128)S(1)} %get-tuple-element.191) | copy-start | bytes 12292
  611.1 354.3 %copy-start.45 = (s32[12576]{0:T(1024)}, s32[12576]{0:T(1024)S(1)}, u32[]{:S(2)}) copy-start(s32[12576]{0:T(1024)S(1)} %fusion.129) | copy-start | bytes 150916
  629.8 356.0 %reduce-scatter.20.cloned.1.call-start = ((), (), s32[]{:S(2)}) async-start(), calls=%async_computation.16 | async-start | bytes 655360 | tf_op jit(solution)/shard_map/reduce_scatter | solution.py:294
  965.3 45.2 %reduce-scatter.18.cloned.1.call-start = ((), (), s32[]{:S(2)}) async-start(), calls=%async_computation.15 | async-start | bytes 655360 | tf_op jit(solution)/shard_map/reduce_scatter | solution.py:294
  980.4 225.4 %all-gather.20.cloned.1.call-start = ((), (), s32[]{:S(2)}) async-start(), calls=%async_computation.21 | async-start | bytes 5242880 | tf_op jit(solution)/shard_map/all_gather | solution.py:308
  1085.5 124.8 %all-gather.22.cloned.1.call-start = ((), (), s32[]{:S(2)}) async-start(), calls=%async_computation.22 | async-start | bytes 5242880 | tf_op jit(solution)/shard_map/all_gather | solution.py:308
  1086.3 1341.4 %reduce-scatter.30.cloned.1.call-start = ((), (), s32[]{:S(2)}) async-start(), calls=%async_computation.24 | async-start | bytes 540672
  1091.7 1366.8 %reduce-scatter.24.cloned.1.call-start = ((), (), s32[]{:S(2)}) async-start(), calls=%async_computation.18 | async-start | bytes 4325376 | tf_op jit(solution)/shard_map/reduce_scatter | solution.py:316
  1097.4 1362.7 %reduce-scatter.22.cloned.1.call-start = ((), (), s32[]{:S(2)}) async-start(), calls=%async_computation.17 | async-start | bytes 12976128 | tf_op jit(solution)/shard_map/reduce_scatter | solution.py:315
  1108.2 1353.6 %reduce-scatter.28.cloned.1.call-start = ((), (), s32[]{:S(2)}) async-start(), calls=%async_computation.20 | async-start | bytes 17301504 | tf_op jit(solution)/shard_map/reduce_scatter | solution.py:318
  1132.4 1432.9 %reduce-scatter.26.cloned.1.call-start = ((), (), s32[]{:S(2)}) async-start(), calls=%async_computation.19 | async-start | bytes 17301504 | tf_op jit(solution)/shard_map/reduce_scatter | solution.py:317
  1269.8 1153.3 %copy-start.156 = (u32[32]{0:T(128)S(1)}, u32[32]{0:T(128)}, u32[]{:S(2)}) copy-start(u32[32]{0:T(128)} %constant.342) | copy-start | bytes 388
  2421.8 13.1 collective-permute-start
  2453.3 168.1 %copy-start.149 = (f32[32,6]{0,1:T(8,128)S(1)}, f32[32,6]{0,1:T(8,128)}, u32[]{:S(2)}) copy-start(f32[32,6]{0,1:T(8,128)} %param.37) | copy-start | bytes 2308
  2453.3 168.1 %copy-start.150 = (f32[32,6]{0,1:T(8,128)S(1)}, f32[32,6]{0,1:T(8,128)}, u32[]{:S(2)}) copy-start(f32[32,6]{0,1:T(8,128)} %param.43) | copy-start | bytes 2308
  (159 other events, 2257.5 us)
Sparse Core Ops, SparseCore 0:
  13.3 495.4 all-gather.23
  555.0 31.6 reduce-scatter.15
  629.9 27.5 reduce-scatter.13
  965.4 20.2 reduce-scatter.19
  988.8 21.6 reduce-scatter.17
  1085.7 34.6 all-gather.19
  1121.9 34.8 all-gather.21
Sparse Core Ops, SparseCore 1:
  558.9 69.3 all-gather.11
  631.9 55.0 all-gather.13
  690.7 76.0 all-gather.15
  770.7 75.8 all-gather.17
  1091.8 159.6 reduce-scatter.29
  1253.8 261.4 reduce-scatter.23
  1522.2 264.5 reduce-scatter.21
  1789.0 480.1 reduce-scatter.27
  2271.3 293.9 reduce-scatter.25
where the time goes:
time: 2740 us; the launch traced here: 2730 us
  blocking collectives  1320 us (48%)
  waiting for transfers between devices  814 us (30%)
  matrix products  271 us (10%)
  other arithmetic  164 us (6%)
  local copies, waits for them, and re-layouts  129 us (5%)
  between operations  33.2 us (1%)
    unnamed x1, blocking collectives  1150 us
    all_gather x1, waiting for transfers between devices, per_device(): table_full = lax.all_gather(table_low, 'wide', axis=0, tiled=True)  487 us
    dot_general x10, matrix products, contract_rows(): lax.dot_general(left_side, right_side, (((0,), (0,)), ((), ())), preferre...  114 us
    reduce_scatter x1, waiting for transfers between devices, per_device(): lax.psum_scatter(summed_grads[2], ('wide', 'narrow'), scatter_dimension=0...  102 us
    psum x2, blocking collectives, per_device(): lax.psum((grad_squares, weight_squares, loss_local), ('wide', 'narrow'))  87.3 us
    all_gather x1, waiting for transfers between devices, gather_layer(): lax.all_gather(up_part, ('wide', 'narrow'), axis=0, tiled=True)  76.9 us
    all_gather x1, waiting for transfers between devices, gather_layer(): lax.all_gather(down_part, ('wide', 'narrow'), axis=0, tiled=True)  71.9 us
    dot_general x10, matrix products, contract_cols(): lax.dot_general(left_side, right_side, (((1,), (1,)), ((), ())), preferre...  68 us
  transfers between devices with their start and end apart: 17, of which 8 were waited for; matrix products, arithmetic and copies ran while one was open for 53% of the time, Pallas kernels for 0%

commit v1 on v0

v1 whole, which is shorter than its diff:
```python
import math

import jax
import jax.numpy as jnp
from jax import lax
from jax.sharding import PartitionSpec as P

HEAD_DIM = 64
VOCAB = 50257

neg_fill = -1e30
beta_first = 0.9
beta_second = 0.999
adam_epsilon = 1e-12
decay_rates = (0.01, 0.01, 0.01, 0.01, 0.01, 0.0)
learn_rate = 0.5
clip_limit = 0.01
norm_epsilon = 1e-05
step_count = 5.0
bf16 = jnp.bfloat16
f32 = jnp.float32


def layer_norm(values, gain_row, offset):
    centered = values - jnp.mean(values, axis=-1, keepdims=True)
    spread = jnp.mean(centered * centered, axis=-1, keepdims=True)
    return centered * lax.rsqrt(spread + norm_epsilon) * gain_row + offset


def norm_backward(values, gain_row, offset, grad_output):
    unused, pullback = jax.vjp(layer_norm, values, gain_row, offset)
    return pullback(grad_output)


def gelu_tanh(values):
    return jax.nn.gelu(values, approximate=True)


def matmul(left_side, right_side):
    return jnp.dot(left_side, right_side, preferred_element_type=f32)


def contract_rows(left_side, right_side):
    return lax.dot_general(
        left_side, right_side, (((0,), (0,)), ((), ())), preferred_element_type=f32
    )


def contract_cols(left_side, right_side):
    return lax.dot_general(
        left_side, right_side, (((1,), (1,)), ((), ())), preferred_element_type=f32
    )


class Links:
    def __init__(self):
        self.wide = lax.axis_size("wide")
        self.narrow = lax.axis_size("narrow")
        self.depth = self.wide // 2
        wide_place = lax.axis_index("wide")
        narrow_place = lax.axis_index("narrow")
        self.device = wide_place * self.narrow + narrow_place
        self.z = wide_place // 2
        self.place = {"x": wide_place % 2, "y": narrow_place // 2, "c": narrow_place % 2}

    def swap(self, values, axis):
        if axis == "x":
            return lax.ppermute(values, "wide", [(i, i ^ 1) for i in range(self.wide)])
        step = 2 if axis == "y" else 1
        return lax.ppermute(values, "narrow", [(i, i ^ step) for i in range(self.narrow)])

    def shift(self, values, step):
        pairs = [(i, (i // 2 + step) % self.depth * 2 + i % 2) for i in range(self.wide)]
        return lax.ppermute(values, "wide", pairs)

    def exchange(self, values, combine):
        for step in (1, 2):
            other = lax.ppermute(values, "narrow", [(i, i ^ step) for i in range(self.narrow)])
            values = combine(values, other)
        step = 1
        while step < self.wide:
            other = lax.ppermute(values, "wide", [(i, i ^ step) for i in range(self.wide)])
            values = combine(values, other)
            step *= 2
        return values

    def total(self, values):
        return self.exchange(values, jnp.add)

    def gather(self, shard, order):
        rows, width = shard.shape
        zero = jnp.zeros((), jnp.int32)
        whole = jnp.zeros((self.depth, 1, 1, 1, rows, width), shard.dtype)
        for step in range(self.depth):
            part = shard if step == 0 else self.shift(shard, step)
            spot = (self.z - step) % self.depth
            whole = lax.dynamic_update_slice(
                whole, part[None, None, None, None], (spot, zero, zero, zero, zero, zero)
            )
        for axis in order:
            dim = " xyc".index(axis)
            other = self.swap(whole, axis)
            shape = list(whole.shape)
            shape[dim] = 2
            both = jnp.zeros(shape, shard.dtype)
            for block, spot in ((whole, self.place[axis]), (other, 1 - self.place[axis])):
                start = [zero] * 6
                start[dim] = spot
                both = lax.dynamic_update_slice(both, block, start)
            whole = both
        return whole.reshape(-1, width)

    def scatter_sum(self, terms, order):
        parts = [
            term.reshape(self.depth, 2, 2, 2, -1, term.shape[-1]) for term in terms
        ]
        widths = [term.shape[-1] for term in terms]
        for axis in order:
            dim = " xyc".index(axis)

            def side(spot):
                picked = [lax.dynamic_slice_in_dim(part, spot, 1, dim) for part in parts]
                return picked[0] if len(picked) == 1 else jnp.concatenate(picked, axis=-1)

            other = self.swap(side(1 - self.place[axis]), axis)
            mine = side(self.place[axis])
            parts = [(mine.astype(f32) + other.astype(f32)).astype(bf16)]
        stacked = parts[0][:, 0, 0, 0]
        summed = lax.dynamic_index_in_dim(stacked, self.z, 0, keepdims=False).astype(f32)
        for step in range(1, self.depth):
            block = lax.dynamic_index_in_dim(
                stacked, (self.z + step) % self.depth, 0, keepdims=False
            )
            summed = summed + self.shift(block, step).astype(f32)
        pieces = []
        start = 0
        for width in widths:
            pieces.append(summed[:, start : start + width])
            start += width
        return pieces


def per_device(
    token_ids,
    doc_ids,
    loss_positions,
    tied_table_master,
    qkv_master,
    out_master,
    up_master,
    down_master,
    norm_master,
    table_first_moment,
    first_qkv,
    first_out,
    first_up,
    first_down,
    first_norms,
    table_second_moment,
    second_qkv,
    second_out,
    second_up,
    second_down,
    second_norms,
):
    links = Links()
    devices = links.wide * links.narrow
    micro_count, unused, length = token_ids.shape
    picked_count = loss_positions.shape[2]
    token_count = micro_count * length
    pick_total = micro_count * picked_count
    model_width = tied_table_master.shape[1]
    head_count = model_width // HEAD_DIM
    block_size = tied_table_master.shape[0]
    count_all = devices * pick_total
    shard_rows = qkv_master.shape[0]

    tokens = token_ids.reshape(token_count)
    picks = loss_positions.reshape(micro_count, picked_count)
    documents = doc_ids.reshape(micro_count, length)
    mean_load = token_count / devices
    slots = int(math.ceil((mean_load + 6.0 * math.sqrt(mean_load)) / 8.0)) * 8
    owner = tokens // block_size
    local_row = tokens % block_size
    token_place = jnp.arange(token_count)
    earlier = (owner[:, None] == owner[None, :]) & (token_place[None, :] < token_place[:, None])
    rank = jnp.sum(earlier.astype(jnp.int32), axis=1)
    most = jnp.max(rank) + 1
    slot_place = jnp.arange(devices * slots)
    line = -(-(slots + 1 + pick_total) // 128) * 128

    pick_hits = picks[:, :, None] == jnp.arange(length)[None, None, :]
    next_hits = picks[:, :, None] + 1 == jnp.arange(length)[None, None, :]
    own_targets = jnp.sum(
        jnp.where(next_hits, token_ids.reshape(micro_count, 1, length), 0), axis=2
    ).reshape(-1)
    pick_docs = jnp.sum(jnp.where(pick_hits, documents[:, None, :], 0), axis=2)

    def slot_of(round_index):
        inside = (rank >= round_index * slots) & (rank < (round_index + 1) * slots)
        return jnp.where(inside, owner * slots + rank - round_index * slots, -1)

    def ask(round_index):
        slot = slot_of(round_index)
        wanted = jnp.sum(
            jnp.where(slot[None, :] == slot_place[:, None], local_row[None, :] + 1, 0), axis=1
        ) - 1
        wanted = wanted.reshape(devices, slots)
        message = jnp.concatenate(
            [
                wanted,
                jnp.broadcast_to(most, (devices, 1)),
                jnp.broadcast_to(own_targets[None, :], (devices, pick_total)),
                jnp.zeros((devices, line - slots - 1 - pick_total), jnp.int32),
            ],
            axis=1,
        )
        answer = lax.all_to_all(message, ("wide", "narrow"), 0, 0, tiled=True)
        asked = answer[:, :slots].reshape(-1)
        return slot, asked, answer

    def fetch(slot, asked):
        row_hits = (asked[:, None] == jnp.arange(block_size)[None, :]).astype(bf16)
        found = matmul(row_hits, table_low).astype(bf16)
        landed = lax.all_to_all(found, ("wide", "narrow"), 0, 0, tiled=True)
        token_hits = (slot[:, None] == slot_place[None, :]).astype(bf16)
        return matmul(token_hits, landed).astype(bf16)

    def give_back(slot, asked, grad_low):
        token_hits = (slot[:, None] == slot_place[None, :]).astype(bf16)
        sent = contract_rows(token_hits, grad_low).astype(bf16)
        landed = lax.all_to_all(sent, ("wide", "narrow"), 0, 0, tiled=True)
        row_hits = (asked[None, :] == jnp.arange(block_size)[:, None]).astype(bf16)
        return matmul(row_hits, landed)

    table_low = tied_table_master.astype(bf16)
    slot_first, asked_first, answer = ask(0)
    rounds = (jnp.max(answer[:, slots]) + slots - 1) // slots
    targets = answer[:, slots + 1 : slots + 1 + pick_total].reshape(-1)

    gain_width = 128
    gain_shard = jnp.pad(norm_master, ((0, 0), (0, gain_width - norm_master.shape[1])))
    first_shard = jnp.concatenate([qkv_master, gain_shard, out_master], axis=1).astype(bf16)
    first_whole = links.gather(first_shard, "xyc")
    up_weight = links.gather(up_master.astype(bf16), "xyc")
    down_weight = links.gather(down_master.astype(bf16), "yxc")
    qkv_width = qkv_master.shape[1]
    qkv_weight = first_whole[:, :qkv_width]
    gain_entries = first_whole[:, qkv_width : qkv_width + 6].astype(f32).T
    out_weight = first_whole[:, qkv_width + gain_width :]

    def more_rows(state):
        round_index, embedded = state
        slot, asked, unused_answer = ask(round_index)
        return (round_index + 1, embedded + fetch(slot, asked))

    unused_round, x_low = lax.while_loop(
        lambda state: state[0] < rounds,
        more_rows,
        (jnp.ones((), jnp.int32), fetch(slot_first, asked_first)),
    )

    x_embed = x_low.astype(f32)
    normed_one = layer_norm(x_embed, gain_entries[0], gain_entries[1]).astype(bf16)
    qkv_all = matmul(normed_one, qkv_weight).astype(bf16)
    pick_rows = (
        pick_hits[:, :, None, :] & jnp.eye(micro_count, dtype=bool)[:, None, :, None]
    ).reshape(pick_total, token_count).astype(bf16)
    picked_both = matmul(
        pick_rows, jnp.concatenate([qkv_all[:, :model_width], x_low], axis=1)
    ).astype(bf16)
    heads_picked = (micro_count, picked_count, head_count, HEAD_DIM)
    heads_all = (micro_count, length, head_count, HEAD_DIM)
    queries = picked_both[:, :model_width].reshape(heads_picked)
    x_embed_picked = picked_both[:, model_width:].astype(f32)
    keys_all = qkv_all[:, model_width : 2 * model_width].reshape(heads_all)
    values_all = qkv_all[:, 2 * model_width :].reshape(heads_all)
    allowed = (jnp.arange(length)[None, None, :] <= picks[:, :, None]) & (
        documents[:, None, :] == pick_docs[:, :, None]
    )
    scale = HEAD_DIM ** (-0.5)
    scores = (
        jnp.einsum("mjhd,muhd->mhju", queries, keys_all, preferred_element_type=f32) * scale
    )
    scores = jnp.where(allowed[:, None], scores, neg_fill)
    exp_scores = jnp.exp(scores - jnp.max(scores, axis=-1, keepdims=True))
    probs = exp_scores / jnp.sum(exp_scores, axis=-1, keepdims=True)
    prob_low = probs.astype(bf16)
    context = (
        jnp.einsum("mhju,muhd->mjhd", prob_low, values_all, preferred_element_type=f32)
        .reshape(pick_total, model_width)
        .astype(bf16)
    )
    x_attn = x_embed_picked + matmul(context, out_weight)
    normed_two = layer_norm(x_attn, gain_entries[2], gain_entries[3]).astype(bf16)
    up_value = matmul(normed_two, up_weight)
    activated = gelu_tanh(up_value).astype(bf16)
    x_out = x_attn + matmul(activated, down_weight)
    picked_low = layer_norm(x_out, gain_entries[4], gain_entries[5]).astype(bf16)

    head_rows = links.gather(picked_low, "xyc")
    columns = links.device * block_size + jnp.arange(block_size)
    logits = contract_cols(head_rows, table_low)
    logits = jnp.where((columns < VOCAB)[None, :], logits, neg_fill)
    target_hits = targets[:, None] == columns[None, :]
    target_sum = jnp.sum(jnp.where(target_hits, logits, 0.0))
    local_top = jnp.max(logits, axis=1)
    local_sum = jnp.sum(jnp.exp(logits - local_top[:, None]), axis=1)

    def merge_totals(first, second):
        top = jnp.maximum(first[0], second[0])
        total = first[1] * jnp.exp(first[0] - top) + second[1] * jnp.exp(second[0] - top)
        return jnp.stack([top, total])

    merged = links.exchange(jnp.stack([local_top, local_sum]), merge_totals)
    log_total = merged[0] + jnp.log(merged[1])
    grad_logits = (
        (jnp.exp(logits - log_total[:, None]) - target_hits.astype(f32)) / count_all
    ).astype(bf16)
    (grad_picked,) = links.scatter_sum([matmul(grad_logits, table_low).astype(bf16)], "cyx")
    table_head = contract_rows(grad_logits, head_rows)

    grad_x_out, gain_last, shift_last = norm_backward(
        x_out, gain_entries[4], gain_entries[5], grad_picked
    )
    grad_mlp = grad_x_out.astype(bf16)
    grad_down = contract_rows(activated, grad_mlp).astype(bf16)
    unused, gelu_pull = jax.vjp(gelu_tanh, up_value)
    grad_up_low = gelu_pull(contract_cols(grad_mlp, down_weight))[0].astype(bf16)
    grad_up = contract_rows(normed_two, grad_up_low).astype(bf16)
    grad_x_attn, gain_two, shift_two = norm_backward(
        x_attn, gain_entries[2], gain_entries[3], contract_cols(grad_up_low, up_weight)
    )
    grad_x_attn = grad_x_out + grad_x_attn
    grad_attn_low = grad_x_attn.astype(bf16)
    grad_out_weight = contract_rows(context, grad_attn_low).astype(bf16)
    grad_context = contract_cols(grad_attn_low, out_weight).astype(bf16).reshape(heads_picked)
    grad_values = jnp.einsum(
        "mhju,mjhd->muhd", prob_low, grad_context, preferred_element_type=f32
    )
    grad_probs = jnp.einsum(
        "mjhd,muhd->mhju", grad_context, values_all, preferred_element_type=f32
    )
    inner = jnp.sum(probs * grad_probs, axis=-1, keepdims=True)
    grad_scores = (probs * (grad_probs - inner)).astype(bf16)
    grad_queries = (
        jnp.einsum("mhju,muhd->mjhd", grad_scores, keys_all, preferred_element_type=f32) * scale
    ).reshape(pick_total, model_width)
    grad_keys = (
        jnp.einsum("mhju,mjhd->muhd", grad_scores, queries, preferred_element_type=f32) * scale
    )
    grad_qkv_low = jnp.concatenate(
        [
            contract_rows(pick_rows, grad_queries.astype(bf16)).astype(bf16),
            grad_keys.reshape(token_count, model_width).astype(bf16),
            grad_values.reshape(token_count, model_width).astype(bf16),
        ],
        axis=1,
    )
    grad_qkv = contract_rows(normed_one, grad_qkv_low).astype(bf16)
    grad_x_one, gain_one, shift_one = norm_backward(
        x_embed, gain_entries[0], gain_entries[1], contract_cols(grad_qkv_low, qkv_weight)
    )
    grad_x_embed = grad_x_one + lax.dot_general(
        pick_rows.astype(f32),
        grad_x_attn,
        (((0,), (0,)), ((), ())),
        precision=lax.Precision.HIGHEST,
        preferred_element_type=f32,
    )
    grad_embed_low = grad_x_embed.astype(bf16)
    (down_grad,) = links.scatter_sum([grad_down], "cyx")
    up_grad, out_grad = links.scatter_sum([grad_up, grad_out_weight], "cxy")
    (qkv_grad,) = links.scatter_sum([grad_qkv], "cyx")
    gain_grads = links.total(
        jnp.stack([gain_one, shift_one, gain_two, shift_two, gain_last, shift_last])
    )
    gain_grad = lax.dynamic_slice_in_dim(gain_grads, links.device * shard_rows, shard_rows, 1).T

    def more_grads(state):
        round_index, earlier_grad = state
        slot, asked, unused_answer = ask(round_index)
        return (round_index + 1, earlier_grad + give_back(slot, asked, grad_embed_low))

    unused_round, table_grad = lax.while_loop(
        lambda state: state[0] < rounds,
        more_grads,
        (
            jnp.ones((), jnp.int32),
            table_head + give_back(slot_first, asked_first, grad_embed_low),
        ),
    )

    all_grads = (table_grad, qkv_grad, out_grad, up_grad, down_grad, gain_grad)
    masters = (tied_table_master, qkv_master, out_master, up_master, down_master, norm_master)
    firsts = (table_first_moment, first_qkv, first_out, first_up, first_down, first_norms)
    seconds = (table_second_moment, second_qkv, second_out, second_up, second_down, second_norms)
    squares = [jnp.sum(gradient * gradient) for gradient in all_grads]
    squares += [jnp.sum(weight * weight) for weight in masters]
    sums = links.total(jnp.stack(squares + [target_sum]).reshape(1, 13))[0]
    grad_total, weight_total, target_total = sums[:6], sums[6:12], sums[12]
    loss_value = (jnp.sum(log_total) - target_total) / count_all
    grad_norm = jnp.sqrt(jnp.sum(grad_total))
    factor = jnp.minimum(1.0, clip_limit / grad_norm)
    new_firsts = []
    new_seconds = []
    directions = []
    for group_index in range(6):
        clipped = factor * all_grads[group_index]
        first_new = beta_first * firsts[group_index] + (1.0 - beta_first) * clipped
        second_new = beta_second * seconds[group_index] + (1.0 - beta_second) * clipped * clipped
        direction = (
            first_new
            / (1.0 - beta_first**step_count)
            / (jnp.sqrt(second_new / (1.0 - beta_second**step_count)) + adam_epsilon)
            + decay_rates[group_index] * masters[group_index]
        )
        new_firsts.append(first_new)
        new_seconds.append(second_new)
        directions.append(direction)
    update_total = links.total(
        jnp.stack([jnp.sum(direction * direction) for direction in directions]).reshape(1, 6)
    )[0]
    weight_norms = jnp.sqrt(weight_total)
    update_norms = jnp.sqrt(update_total)
    new_weights = [
        masters[group_index]
        - learn_rate
        * (weight_norms[group_index] / update_norms[group_index])
        * directions[group_index]
        for group_index in range(6)
    ]
    matrix_norms = jnp.stack([factor * jnp.sqrt(grad_total), weight_norms, update_norms])
    return (
        loss_value,
        grad_norm,
        matrix_norms,
        *new_weights,
        *new_firsts,
        *new_seconds,
    )


def solution(mesh):
    rows = P(("wide", "narrow"), None)
    ids = P(None, ("wide", "narrow"), None)
    return jax.shard_map(
        per_device,
        mesh=mesh,
        in_specs=(ids,) * 3 + (rows,) * 18,
        out_specs=(P(),) * 3 + (rows,) * 18,
        check_vma=False,
    )
```

time: 2740 us -> 917 us (0.33)
  blocking collectives: 1320 us -> 0 us
  waiting for transfers between devices: 814 us -> 364 us
  matrix products: 271 us -> 128 us
  starting transfers between devices: 2.61 us -> 115 us
  other arithmetic: 164 us -> 122 us
  local copies, waits for them, and re-layouts: 129 us -> 162 us
    unnamed x1 -> x0, blocking collectives: 1150 us -> none
    all_gather x7 -> x0, waiting for transfers between devices: 678 us -> none  [the longest x1 487 us: per_device(): table_full = lax.all_gather(table_low, 'wide', axis=0, tiled=True)]
    ppermute x0 -> x68, waiting for transfers between devices: none -> 352 us  [the longest x8 126 us: swap(): return lax.ppermute(values, 'wide', [(i, i ^ 1) for i in range(self.wide)])]
    reduce_scatter x8 -> x0, waiting for transfers between devices: 129 us -> none  [the longest x1 102 us: per_device(): lax.psum_scatter(summed_grads[2], ('wide', 'narrow'), scatter_dimension=0...]
    ppermute x0 -> x68, starting transfers between devices: none -> 94.8 us  [the longest x24 41.6 us: shift(): return lax.ppermute(values, 'wide', pairs)]
    psum x3 -> x0, blocking collectives: 93.2 us -> none  [the longest x2 87.3 us: per_device(): lax.psum((grad_squares, weight_squares, loss_local), ('wide', 'narrow'))]
    dot_general x10 -> x7, matrix products: 114 us -> 29.6 us  [contract_rows(): lax.dot_general(left_side, right_side, (((0,), (0,)), ((), ())), preferre...]
    all_gather x5 -> x0, blocking collectives: 64.2 us -> none  [the longest x1 41.2 us: gather_layer(): lax.all_gather(gain_part, ('wide', 'narrow'), axis=0, tiled=True)]
  transfers between devices with their start and end apart: 17 -> 71, of which waited for: 8 -> 41; matrix products, arithmetic and copies ran while one was open for 53% -> 22% of each run, Pallas kernels for 0% -> 0%
where the time goes in v1:
time: 917 us; the launch traced here: 908 us
  waiting for transfers between devices  364 us (40%)
  local copies, waits for them, and re-layouts  162 us (18%)
  matrix products  128 us (14%)
  other arithmetic  122 us (13%)
  starting transfers between devices  115 us (13%)
  between operations  16.7 us (2%)
    ppermute x8, waiting for transfers between devices, swap(): return lax.ppermute(values, 'wide', [(i, i ^ 1) for i in range(self.wide)])  126 us
    ppermute x16, waiting for transfers between devices, swap(): lax.ppermute(values, 'narrow', [(i, i ^ step) for i in range(self.narrow)])  101 us
    ppermute x24, waiting for transfers between devices, shift(): return lax.ppermute(values, 'wide', pairs)  62.7 us
    dot_general x9, matrix products, matmul(): return jnp.dot(left_side, right_side, preferred_element_type=f32)  49.1 us
    dynamic_update_slice x24, local copies, waits for them, and re-layouts, gather(): both = lax.dynamic_update_slice(both, block, start)  48.5 us
    ppermute x12, waiting for transfers between devices, exchange(): lax.ppermute(values, 'wide', [(i, i ^ step) for i in range(self.wide)])  46.9 us
    ppermute x24, starting transfers between devices, shift(): return lax.ppermute(values, 'wide', pairs)  41.6 us
    dot_general x5, matrix products, contract_cols(): lax.dot_general(left_side, right_side, (((1,), (1,)), ((), ())), preferre...  36 us
  transfers between devices with their start and end apart: 71, of which 41 were waited for; matrix products, arithmetic and copies ran while one was open for 22% of the time, Pallas kernels for 0%

profile of v1, /device:TPU:0, one launch (start us, length us, event | category | flops | bytes accessed | tf_op | source)
XLA Modules:
  0.0 908.0 jit_solution(14031769103513541721)
XLA Ops:
  21.8 8.7 multiply_reduce_fusion.1
  39.4 12.0 %all-to-all-done.4 = s32[32,1,128]{2,1,0:T(1,128)S(1)} async-done(((s32[32,1,128]{2,1,0:T(1,128)}), s32[32,1,128]{2,1,0:T(1,128)S(1)}, u32[]{:S(2)}, u32[]{:S(2)}) %all-to-all-start.4) | async-done | bytes 16416 | tf_op jit(solution)/shard_map/all_to_all | solution.py:218
  66.1 10.5 %collective-permute-done.12 = bf16[128,1024]{1,0:T(8,128)(2,1)S(1)} collective-permute-done((bf16[128,1024]{1,0:T(8,128)(2,1)S(1)}, bf16[128,1024]{1,0:T(8,128)(2,1)S(1)}, u32[]{:S(2)}, u32[]{:S(2)}) %collective-permute-start.12) | collective-permute-done | bytes 262176 | tf_op jit(solution)/shard_map/ppermute | solution.py:74
  78.4 9.3 %collective-permute-done.13 = bf16[128,1024]{1,0:T(8,128)(2,1)S(1)} collective-permute-done((bf16[128,1024]{1,0:T(8,128)(2,1)S(1)}, bf16[128,1024]{1,0:T(8,128)(2,1)S(1)}, u32[]{:S(2)}, u32[]{:S(2)}) %collective-permute-start.13) | collective-permute-done | bytes 262176 | tf_op jit(solution)/shard_map/ppermute | solution.py:74
  97.2 16.8 %collective-permute-done.9 = bf16[4,1,1,1,32,4096]{5,4,3,2,1,0:T(8,128)(2,1)S(1)} collective-permute-done((bf16[4,1,1,1,32,4096]{5,4,3,2,1,0:T(8,128)(2,1)}, bf16[4,1,1,1,32,4096]{5,4,3,2,1,0:T(8,128)(2,1)S(1)}, u32[]{:S(2)}, u32[]{:S(2)}) %collective-permute-start.9) | collective-permute-done | bytes 1048608 | tf_op jit(solution)/shard_map/ppermute | solution.py:68
  114.7 9.4 %all-to-all-start.5 = ((bf16[32,40,1024]{2,1,0:T(8,128)(2,1)}), bf16[32,40,1024]{2,1,0:T(8,128)(2,1)}, u32[]{:S(2)}, u32[]{:S(2)}) async-start(bf16[32,40,1024]{2,1,0:T(8,128)(2,1)} %bitcast.292), calls=%async_computation.5 | async-start | bytes 5242880 | tf_op jit(solution)/shard_map/all_to_all | solution.py:225
  133.0 16.8 %collective-permute-done.3 = bf16[4,1,1,1,32,4224]{5,4,3,2,1,0:T(8,128)(2,1)} collective-permute-done((bf16[4,1,1,1,32,4224]{5,4,3,2,1,0:T(8,128)(2,1)S(1)}, bf16[4,1,1,1,32,4224]{5,4,3,2,1,0:T(8,128)(2,1)}, u32[]{:S(2)}, u32[]{:S(2)}) %collective-permute-start.3) | collective-permute-done | bytes 1081376 | tf_op jit(solution)/shard_map/ppermute | solution.py:68
  159.3 28.2 %collective-permute-done.10 = bf16[4,2,1,1,32,4096]{5,4,3,2,1,0:T(8,128)(2,1)} collective-permute-done((bf16[4,2,1,1,32,4096]{5,4,3,2,1,0:T(8,128)(2,1)S(1)}, bf16[4,2,1,1,32,4096]{5,4,3,2,1,0:T(8,128)(2,1)}, u32[]{:S(2)}, u32[]{:S(2)}) %collective-permute-start.10) | collective-permute-done | bytes 2097184 | tf_op jit(solution)/shard_map/ppermute | solution.py:70
  190.6 17.1 %collective-permute-done.16 = bf16[4,1,2,1,128,1024]{5,4,3,2,1,0:T(8,128)(2,1)S(1)} collective-permute-done((bf16[4,1,2,1,128,1024]{5,4,3,2,1,0:T(8,128)(2,1)S(1)}, bf16[4,1,2,1,128,1024]{5,4,3,2,1,0:T(8,128)(2,1)S(1)}, u32[]{:S(2)}, u32[]{:S(2)}) %collective-permute-start.16) | collective-permute-done | bytes 2097184 | tf_op jit(solution)/shard_map/ppermute | solution.py:68
  325.0 12.3 %collective-permute-done.21 = bf16[4,1,1,1,64,1024]{5,4,3,2,1,0:T(8,128)(2,1)S(1)} collective-permute-done((bf16[4,1,1,1,64,1024]{5,4,3,2,1,0:T(8,128)(2,1)S(1)}, bf16[4,1,1,1,64,1024]{5,4,3,2,1,0:T(8,128)(2,1)S(1)}, u32[]{:S(2)}, u32[]{:S(2)}) %collective-permute-start.21) | collective-permute-done | bytes 524320 | tf_op jit(solution)/shard_map/ppermute | solution.py:68
  340.6 21.0 %collective-permute-done.22 = bf16[4,2,1,1,64,1024]{5,4,3,2,1,0:T(8,128)(2,1)S(1)} collective-permute-done((bf16[4,2,1,1,64,1024]{5,4,3,2,1,0:T(8,128)(2,1)S(1)}, bf16[4,2,1,1,64,1024]{5,4,3,2,1,0:T(8,128)(2,1)S(1)}, u32[]{:S(2)}, u32[]{:S(2)}) %collective-permute-start.22) | collective-permute-done | bytes 1048608 | tf_op jit(solution)/shard_map/ppermute | solution.py:70
  370.5 10.5 %select_reduce_fusion.2 = (f32[2048]{0:T(1024)S(1)}, f32[2048,1572]{0,1:T(8,128)S(1)}) fusion(pred[1572]{0:T(1024)(128)(4,1)S(1)} %broadcast_compare_fusion, bf16[2048,1024]{1,0:T(8,128)(2,1)S(1)} %bitcast.290, bf16[1572,1024]{1,0:T(8,128)(2,1)} %get-tuple-element.761), kind=kOutput, calls=%fused_computation.38 | convolution fusion | flops 6599882752 | bytes 20301348 | tf_op jit(solution)/shard_map/dot_general | solution.py:50
  408.1 12.0 %convolution_convert_fusion.4 = bf16[2048,1024]{1,0:T(8,128)(2,1)S(1)} fusion(bf16[1572,1024]{1,0:T(8,128)(2,1)} %get-tuple-element.761, f32[2048,1572]{0,1:T(8,128)S(1)} %get-tuple-element.544, s32[2048]{0:T(1024)S(1)} %copy-done.66, f32[2048]{0:T(1024)S(1)} %get-tuple-element.462, s32[1572]{0:T(1024)S(1)} %copy-done.68, ...), kind=kOutput, calls=%fused_computation.69 | convolution fusion | flops 6618079232 | bytes 20315828 | tf_op jit(solution)/shard_map/dot_general | solution.py:40
  426.5 24.6 %collective-permute-done.30 = bf16[4,2,1,1,64,1024]{5,4,3,2,1,0:T(8,128)(2,1)S(1)} collective-permute-done((bf16[4,2,1,1,64,1024]{5,4,3,2,1,0:T(8,128)(2,1)S(1)}, bf16[4,2,1,1,64,1024]{5,4,3,2,1,0:T(8,128)(2,1)S(1)}, u32[]{:S(2)}, u32[]{:S(2)}) %collective-permute-start.30) | collective-permute-done | bytes 1048608 | tf_op jit(solution)/shard_map/ppermute | solution.py:70
  530.2 9.3 %fusion.42 = (f32[1024]{0:T(1024)}, f32[512]{0:T(512)}, f32[1024]{0:T(1024)}, f32[512,1024]{1,0:T(8,128)}) fusion(bf16[512,1024]{1,0:T(8,128)(2,1)S(1)} %copy-done.8, f32[512]{0:T(512)} %copy-done.87, f32[512]{0:T(512)} %copy-done.74, f32[1024]{0:T(1024)} %copy-done.81, bf16[1024,4224]{1,0:T(8,128)(2,1)} %bitcast.13, bf16[512,1024]{1,0:T(8,128)(2,1)} %reshape.773, ...), kind=kOutput, calls=%fused_computation.91 | convolution fusion | flops 3235378688 | bytes 12601344 | tf_op jit(solution)/shard_map/dot_general | solution.py:50
  596.6 16.4 %collective-permute-done.56 = f32[6,1024]{1,0:T(8,128)S(1)} collective-permute-done((f32[6,1024]{1,0:T(8,128)S(1)}, f32[6,1024]{1,0:T(8,128)S(1)}, u32[]{:S(2)}, u32[]{:S(2)}) %collective-permute-start.56) | collective-permute-done | bytes 24608 | tf_op jit(solution)/shard_map/ppermute | solution.py:82
  620.4 10.2 %collective-permute-done.57 = f32[6,1024]{1,0:T(8,128)S(1)} collective-permute-done((f32[6,1024]{1,0:T(8,128)S(1)}, f32[6,1024]{1,0:T(8,128)S(1)}, u32[]{:S(2)}, u32[]{:S(2)}) %collective-permute-start.57) | collective-permute-done | bytes 24608 | tf_op jit(solution)/shard_map/ppermute | solution.py:82
  653.1 11.9 %convolution_add_fusion = f32[1572,1024]{1,0:T(8,128)} fusion(f32[1572,1024]{1,0:T(8,128)} %fusion.21, bf16[2048,1024]{1,0:T(8,128)(2,1)S(1)} %bitcast.291, f32[2048,1572]{0,1:T(8,128)S(1)} %bitcast.284, s32[2048]{0:T(1024)S(1)} %copy-done.67, f32[2048]{0:T(1024)S(1)} %copy-done.95, s32[1572]{0:T(1024)S(1)} %copy-done.69, pred[1572]{0:T(1024)(128)(4,1)S(1)} %copy-done.97), kind=kOutput, calls=%fused_computation.67 | convolution fusion | flops 6617591808 | bytes 29974196 | tf_op jit(solution)/shard_map/dot_general | solution.py:44
  689.0 45.9 %collective-permute-done.42 = bf16[4,1,2,1,32,5120]{5,4,3,2,1,0:T(8,128)(2,1)} collective-permute-done((bf16[4,1,2,1,32,5120]{5,4,3,2,1,0:T(8,128)(2,1)}, bf16[4,1,2,1,32,5120]{5,4,3,2,1,0:T(8,128)(2,1)}, u32[]{:S(2)}, u32[]{:S(2)}) %collective-permute-start.42) | collective-permute-done | bytes 2621472 | tf_op jit(solution)/shard_map/ppermute | solution.py:68
  756.9 8.6 collective-permute-done.43
  775.0 14.7 %collective-permute-done.51 = bf16[128,1024]{1,0:T(8,128)(2,1)S(1)} collective-permute-done((bf16[128,1024]{1,0:T(8,128)(2,1)S(1)}, bf16[128,1024]{1,0:T(8,128)(2,1)S(1)}, u32[]{:S(2)}, u32[]{:S(2)}) %collective-permute-start.51) | collective-permute-done | bytes 262176 | tf_op jit(solution)/shard_map/ppermute | solution.py:74
  791.3 13.7 %collective-permute-done.45 = bf16[32,5120]{1,0:T(8,128)(2,1)S(1)} collective-permute-done((bf16[32,5120]{1,0:T(8,128)(2,1)S(1)}, bf16[32,5120]{1,0:T(8,128)(2,1)S(1)}, u32[]{:S(2)}, u32[]{:S(2)}) %collective-permute-start.45) | collective-permute-done | bytes 327712 | tf_op jit(solution)/shard_map/ppermute | solution.py:74
  841.3 14.8 %multiply_reduce_fusion = (f32[]{:T(128)}, f32[1572,1024]{1,0:T(8,128)}, f32[1572,1024]{1,0:T(8,128)}) fusion(f32[1572,1024]{1,0:T(8,128)} %param.28, f32[1572,1024]{1,0:T(8,128)} %get-tuple-element.284, f32[]{:T(128)S(6)} %min.3, f32[1572,1024]{1,0:T(8,128)} %param.34, f32[1572,1024]{1,0:T(8,128)} %param.40), kind=kLoop, calls=%fused_computation.50 | loop fusion | flops 25755648 | bytes 38633480 | tf_op jit(solution)/shard_map/reduce_sum | solution.py:422
  895.3 10.0 %multiply_subtract_fusion = f32[1572,1024]{1,0:T(8,128)} fusion(f32[1572,1024]{1,0:T(8,128)} %param.28, f32[]{:T(128)} %bitcast.98, f32[1572,1024]{1,0:T(8,128)} %get-tuple-element.447, f32[1572,1024]{1,0:T(8,128)} %get-tuple-element.446), kind=kLoop, calls=%fused_computation.49 | loop fusion | flops 12877824 | bytes 25755652 | tf_op jit(solution)/shard_map/sub | solution.py:427
  (623 shorter events, 526.5 us)
Async XLA Ops:
  3.5 57.6 %collective-permute-start.6 = (bf16[32,4096]{1,0:T(8,128)(2,1)S(1)}, bf16[32,4096]{1,0:T(8,128)(2,1)S(1)}, u32[]{:S(2)}, u32[]{:S(2)}) collective-permute-start(bf16[32,4096]{1,0:T(8,128)(2,1)S(1)} %get-tuple-element.472), channel_id=1, source_target_pairs={{0,8},{4,12},{8,16},{12,20},{16,24},{20,28},{24,0},{28,4},{1,9},{5... | collective-permute-start | bytes 786440 | tf_op jit(solution)/shard_map/ppermute | solution.py:74
  6.6 57.0 %collective-permute-start.7 = (bf16[32,4096]{1,0:T(8,128)(2,1)S(1)}, bf16[32,4096]{1,0:T(8,128)(2,1)S(1)}, u32[]{:S(2)}, u32[]{:S(2)}) collective-permute-start(bf16[32,4096]{1,0:T(8,128)(2,1)S(1)} %get-tuple-element.472), channel_id=1, source_target_pairs={{0,16},{4,20},{8,24},{12,28},{16,0},{20,4},{24,8},{28,12},{1,17},{... | collective-permute-start | bytes 786440 | tf_op jit(solution)/shard_map/ppermute | solution.py:74
  9.2 55.5 %collective-permute-start.8 = (bf16[32,4096]{1,0:T(8,128)(2,1)S(1)}, bf16[32,4096]{1,0:T(8,128)(2,1)S(1)}, u32[]{:S(2)}, u32[]{:S(2)}) collective-permute-start(bf16[32,4096]{1,0:T(8,128)(2,1)S(1)} %get-tuple-element.472), channel_id=1, source_target_pairs={{0,24},{4,28},{8,0},{12,4},{16,8},{20,12},{24,16},{28,20},{1,25},{... | collective-permute-start | bytes 786440 | tf_op jit(solution)/shard_map/ppermute | solution.py:74
  15.5 78.0 %collective-permute-start = (bf16[32,4224]{1,0:T(8,128)(2,1)}, bf16[32,4224]{1,0:T(8,128)(2,1)}, u32[]{:S(2)}, u32[]{:S(2)}) collective-permute-start(bf16[32,4224]{1,0:T(8,128)(2,1)} %pad_maximum_fusion.4), channel_id=1, source_target_pairs={{0,8},{4,12},{8,16},{12,20},{16,24},{20,28},{24,0},{28,4},{1,9},{5... | collective-permute-start | bytes 811016 | tf_op jit(solution)/shard_map/ppermute | solution.py:74
  16.1 78.5 %collective-permute-start.1 = (bf16[32,4224]{1,0:T(8,128)(2,1)}, bf16[32,4224]{1,0:T(8,128)(2,1)}, u32[]{:S(2)}, u32[]{:S(2)}) collective-permute-start(bf16[32,4224]{1,0:T(8,128)(2,1)} %pad_maximum_fusion.4), channel_id=1, source_target_pairs={{0,16},{4,20},{8,24},{12,28},{16,0},{20,4},{24,8},{28,12},{1,17},{... | collective-permute-start | bytes 811016 | tf_op jit(solution)/shard_map/ppermute | solution.py:74
  61.2 34.5 %collective-permute-start.2 = (bf16[32,4224]{1,0:T(8,128)(2,1)}, bf16[32,4224]{1,0:T(8,128)(2,1)S(1)}, u32[]{:S(2)}, u32[]{:S(2)}) collective-permute-start(bf16[32,4224]{1,0:T(8,128)(2,1)} %pad_maximum_fusion.4), channel_id=1, source_target_pairs={{0,24},{4,28},{8,0},{12,4},{16,8},{20,12},{24,16},{28,20},{1,25},{... | collective-permute-start | bytes 811016 | tf_op jit(solution)/shard_map/ppermute | solution.py:74
  89.7 34.8 %collective-permute-start.15 = (bf16[4,1,1,1,128,1024]{5,4,3,2,1,0:T(8,128)(2,1)}, bf16[4,1,1,1,128,1024]{5,4,3,2,1,0:T(8,128)(2,1)}, u32[]{:S(2)}, u32[]{:S(2)}) collective-permute-start(bf16[4,1,1,1,128,1024]{5,4,3,2,1,0:T(8,128)(2,1)} %bitcast_dynamic-update-slice_fusion.3), channel_id=1, source_target_pairs={{0,2},{1,3},{2,0},{3,1},{4,6},{5,7},{6,4},{7,5},{8,10},{9,11},{10,... | collective-permute-start | bytes 3145736 | tf_op jit(solution)/shard_map/ppermute | solution.py:70
  95.7 54.1 %collective-permute-start.3 = (bf16[4,1,1,1,32,4224]{5,4,3,2,1,0:T(8,128)(2,1)S(1)}, bf16[4,1,1,1,32,4224]{5,4,3,2,1,0:T(8,128)(2,1)}, u32[]{:S(2)}, u32[]{:S(2)}) collective-permute-start(bf16[4,1,1,1,32,4224]{5,4,3,2,1,0:T(8,128)(2,1)S(1)} %bitcast_dynamic-update-slice_fusion), channel_id=1, source_target_pairs={{0,4},{4,0},{8,12},{12,8},{16,20},{20,16},{24,28},{28,24},{1,5},{5... | collective-permute-start | bytes 3244040 | tf_op jit(solution)/shard_map/ppermute | solution.py:68
  114.1 73.3 %collective-permute-start.10 = (bf16[4,2,1,1,32,4096]{5,4,3,2,1,0:T(8,128)(2,1)S(1)}, bf16[4,2,1,1,32,4096]{5,4,3,2,1,0:T(8,128)(2,1)}, u32[]{:S(2)}, u32[]{:S(2)}) collective-permute-start(bf16[4,2,1,1,32,4096]{5,4,3,2,1,0:T(8,128)(2,1)S(1)} %constant_dynamic-update-slice_fusion.16), channel_id=1, source_target_pairs={{0,2},{1,3},{2,0},{3,1},{4,6},{5,7},{6,4},{7,5},{8,10},{9,11},{10,... | collective-permute-start | bytes 6291464 | tf_op jit(solution)/shard_map/ppermute | solution.py:70
  114.7 127.4 %all-to-all-start.5 = ((bf16[32,40,1024]{2,1,0:T(8,128)(2,1)}), bf16[32,40,1024]{2,1,0:T(8,128)(2,1)}, u32[]{:S(2)}, u32[]{:S(2)}) async-start(bf16[32,40,1024]{2,1,0:T(8,128)(2,1)} %bitcast.292), calls=%async_computation.5 | async-start | bytes 5242880 | tf_op jit(solution)/shard_map/all_to_all | solution.py:225
  127.1 80.6 %collective-permute-start.16 = (bf16[4,1,2,1,128,1024]{5,4,3,2,1,0:T(8,128)(2,1)S(1)}, bf16[4,1,2,1,128,1024]{5,4,3,2,1,0:T(8,128)(2,1)S(1)}, u32[]{:S(2)}, u32[]{:S(2)}) collective-permute-start(bf16[4,1,2,1,128,1024]{5,4,3,2,1,0:T(8,128)(2,1)S(1)} %constant_dynamic-update-slice_fusion.10), channel_id=1, source_target_pairs={{0,4},{4,0},{8,12},{12,8},{16,20},{20,16},{24,28},{28,24},{1,5},{5... | collective-permute-start | bytes 6291464 | tf_op jit(solution)/shard_map/ppermute | solution.py:68
  151.2 80.7 %collective-permute-start.4 = (bf16[4,2,1,1,32,4224]{5,4,3,2,1,0:T(8,128)(2,1)S(1)}, bf16[4,2,1,1,32,4224]{5,4,3,2,1,0:T(8,128)(2,1)S(1)}, u32[]{:S(2)}, u32[]{:S(2)}) collective-permute-start(bf16[4,2,1,1,32,4224]{5,4,3,2,1,0:T(8,128)(2,1)S(1)} %constant_dynamic-update-slice_fusion.22), channel_id=1, source_target_pairs={{0,2},{1,3},{2,0},{3,1},{4,6},{5,7},{6,4},{7,5},{8,10},{9,11},{10,... | collective-permute-start | bytes 6488072 | tf_op jit(solution)/shard_map/ppermute | solution.py:70
  190.6 64.0 %collective-permute-start.11 = (bf16[4,2,2,1,32,4096]{5,4,3,2,1,0:T(8,128)(2,1)}, bf16[4,2,2,1,32,4096]{5,4,3,2,1,0:T(8,128)(2,1)}, u32[]{:S(2)}, u32[]{:S(2)}) collective-permute-start(bf16[4,2,2,1,32,4096]{5,4,3,2,1,0:T(8,128)(2,1)} %constant_dynamic-update-slice_fusion.14), channel_id=1, source_target_pairs={{0,1},{1,0},{2,3},{3,2},{4,5},{5,4},{6,7},{7,6},{8,9},{9,8},{10,11... | collective-permute-start | bytes 12582920 | tf_op jit(solution)/shard_map/ppermute | solution.py:70
  209.2 40.5 %collective-permute-start.17 = (bf16[4,2,2,1,128,1024]{5,4,3,2,1,0:T(8,128)(2,1)}, bf16[4,2,2,1,128,1024]{5,4,3,2,1,0:T(8,128)(2,1)}, u32[]{:S(2)}, u32[]{:S(2)}) collective-permute-start(bf16[4,2,2,1,128,1024]{5,4,3,2,1,0:T(8,128)(2,1)} %constant_dynamic-update-slice_fusion.8), channel_id=1, source_target_pairs={{0,1},{1,0},{2,3},{3,2},{4,5},{5,4},{6,7},{7,6},{8,9},{9,8},{10,11... | collective-permute-start | bytes 12582920 | tf_op jit(solution)/shard_map/ppermute | solution.py:70
  550.9 36.8 %collective-permute-start.35 = (bf16[4,2,2,1,32,3072]{5,4,3,2,1,0:T(8,128)(2,1)}, bf16[4,2,2,1,32,3072]{5,4,3,2,1,0:T(8,128)(2,1)}, u32[]{:S(2)}, u32[]{:S(2)}) collective-permute-start(bf16[4,2,2,1,32,3072]{5,4,3,2,1,0:T(8,128)(2,1)} %constant_dynamic-slice_fusion.12), channel_id=1, source_target_pairs={{0,1},{1,0},{2,3},{3,2},{4,5},{5,4},{6,7},{7,6},{8,9},{9,8},{10,11... | collective-permute-start | bytes 9437192 | tf_op jit(solution)/shard_map/ppermute | solution.py:70
  558.7 72.6 %collective-permute-start.47 = (bf16[4,2,2,1,128,1024]{5,4,3,2,1,0:T(8,128)(2,1)}, bf16[4,2,2,1,128,1024]{5,4,3,2,1,0:T(8,128)(2,1)}, u32[]{:S(2)}, u32[]{:S(2)}) collective-permute-start(bf16[4,2,2,1,128,1024]{5,4,3,2,1,0:T(8,128)(2,1)} %constant_dynamic-slice_fusion.3), channel_id=1, source_target_pairs={{0,1},{1,0},{2,3},{3,2},{4,5},{5,4},{6,7},{7,6},{8,9},{9,8},{10,11... | collective-permute-start | bytes 12582920 | tf_op jit(solution)/shard_map/ppermute | solution.py:70
  563.9 80.7 %all-to-all-start.6 = ((bf16[32,40,1024]{2,1,0:T(8,128)(2,1)}), bf16[32,40,1024]{2,1,0:T(8,128)(2,1)}, u32[]{:S(2)}, u32[]{:S(2)}) async-start(bf16[32,40,1024]{2,1,0:T(8,128)(2,1)} %bitcast.293), calls=%async_computation.6 | async-start | bytes 5242880 | tf_op jit(solution)/shard_map/all_to_all | solution.py:232
  593.1 47.7 %collective-permute-start.36 = (bf16[4,2,1,1,32,3072]{5,4,3,2,1,0:T(8,128)(2,1)}, bf16[4,2,1,1,32,3072]{5,4,3,2,1,0:T(8,128)(2,1)}, u32[]{:S(2)}, u32[]{:S(2)}) collective-permute-start(bf16[4,2,1,1,32,3072]{5,4,3,2,1,0:T(8,128)(2,1)} %constant_dynamic-slice_fusion.11), channel_id=1, source_target_pairs={{0,2},{1,3},{2,0},{3,1},{4,6},{5,7},{6,4},{7,5},{8,10},{9,11},{10,... | collective-permute-start | bytes 4718600 | tf_op jit(solution)/shard_map/ppermute | solution.py:70
  620.4 44.6 %collective-permute-start.41 = (bf16[4,2,2,1,32,5120]{5,4,3,2,1,0:T(8,128)(2,1)}, bf16[4,2,2,1,32,5120]{5,4,3,2,1,0:T(8,128)(2,1)}, u32[]{:S(2)}, u32[]{:S(2)}) collective-permute-start(bf16[4,2,2,1,32,5120]{5,4,3,2,1,0:T(8,128)(2,1)} %pad_maximum_fusion), channel_id=1, source_target_pairs={{0,1},{1,0},{2,3},{3,2},{4,5},{5,4},{6,7},{7,6},{8,9},{9,8},{10,11... | collective-permute-start | bytes 15728648 | tf_op jit(solution)/shard_map/ppermute | solution.py:70
  637.2 48.4 %collective-permute-start.48 = (bf16[4,2,1,1,128,1024]{5,4,3,2,1,0:T(8,128)(2,1)}, bf16[4,2,1,1,128,1024]{5,4,3,2,1,0:T(8,128)(2,1)}, u32[]{:S(2)}, u32[]{:S(2)}) collective-permute-start(bf16[4,2,1,1,128,1024]{5,4,3,2,1,0:T(8,128)(2,1)} %constant_dynamic-slice_fusion.2), channel_id=1, source_target_pairs={{0,2},{1,3},{2,0},{3,1},{4,6},{5,7},{6,4},{7,5},{8,10},{9,11},{10,... | collective-permute-start | bytes 6291464 | tf_op jit(solution)/shard_map/ppermute | solution.py:70
  644.2 94.7 %collective-permute-start.37 = (bf16[4,1,1,1,32,3072]{5,4,3,2,1,0:T(8,128)(2,1)}, bf16[4,1,1,1,32,3072]{5,4,3,2,1,0:T(8,128)(2,1)}, u32[]{:S(2)}, u32[]{:S(2)}) collective-permute-start(bf16[4,1,1,1,32,3072]{5,4,3,2,1,0:T(8,128)(2,1)} %constant_dynamic-slice_fusion.10), channel_id=1, source_target_pairs={{0,4},{4,0},{8,12},{12,8},{16,20},{20,16},{24,28},{28,24},{1,5},{5... | collective-permute-start | bytes 2359304 | tf_op jit(solution)/shard_map/ppermute | solution.py:68
  674.7 60.1 %collective-permute-start.42 = (bf16[4,1,2,1,32,5120]{5,4,3,2,1,0:T(8,128)(2,1)}, bf16[4,1,2,1,32,5120]{5,4,3,2,1,0:T(8,128)(2,1)}, u32[]{:S(2)}, u32[]{:S(2)}) collective-permute-start(bf16[4,1,2,1,32,5120]{5,4,3,2,1,0:T(8,128)(2,1)} %constant_dynamic-slice_fusion.5), channel_id=1, source_target_pairs={{0,4},{4,0},{8,12},{12,8},{16,20},{20,16},{24,28},{28,24},{1,5},{5... | collective-permute-start | bytes 7864328 | tf_op jit(solution)/shard_map/ppermute | solution.py:68
  688.3 67.4 %collective-permute-start.49 = (bf16[4,1,1,1,128,1024]{5,4,3,2,1,0:T(8,128)(2,1)S(1)}, bf16[4,1,1,1,128,1024]{5,4,3,2,1,0:T(8,128)(2,1)S(1)}, u32[]{:S(2)}, u32[]{:S(2)}) collective-permute-start(bf16[4,1,1,1,128,1024]{5,4,3,2,1,0:T(8,128)(2,1)S(1)} %constant_dynamic-slice_fusion.1), channel_id=1, source_target_pairs={{0,4},{4,0},{8,12},{12,8},{16,20},{20,16},{24,28},{28,24},{1,5},{5... | collective-permute-start | bytes 3145736 | tf_op jit(solution)/shard_map/ppermute | solution.py:68
  769.2 35.8 %collective-permute-start.45 = (bf16[32,5120]{1,0:T(8,128)(2,1)S(1)}, bf16[32,5120]{1,0:T(8,128)(2,1)S(1)}, u32[]{:S(2)}, u32[]{:S(2)}) collective-permute-start(bf16[32,5120]{1,0:T(8,128)(2,1)S(1)} %get-tuple-element.488), channel_id=1, source_target_pairs={{0,16},{4,20},{8,24},{12,28},{16,0},{20,4},{24,8},{28,12},{1,17},{... | collective-permute-start | bytes 983048 | tf_op jit(solution)/shard_map/ppermute | solution.py:74
  (171 other events, 2985.9 us)

commit v2 on v1

v2 whole, which is shorter than its diff:
```python
import math

import jax
import jax.numpy as jnp
from jax import lax
from jax.experimental import pallas as pl
from jax.experimental.pallas import tpu as pltpu
from jax.sharding import PartitionSpec as P

HEAD_DIM = 64
VOCAB = 50257

neg_fill = -1e30
beta_first = 0.9
beta_second = 0.999
adam_epsilon = 1e-12
decay_rates = (0.01, 0.01, 0.01, 0.01, 0.01, 0.0)
learn_rate = 0.5
clip_limit = 0.01
norm_epsilon = 1e-05
step_count = 5.0
bf16 = jnp.bfloat16
f32 = jnp.float32


def layer_norm(values, gain_row, offset):
    centered = values - jnp.mean(values, axis=-1, keepdims=True)
    spread = jnp.mean(centered * centered, axis=-1, keepdims=True)
    return centered * lax.rsqrt(spread + norm_epsilon) * gain_row + offset


def norm_backward(values, gain_row, offset, grad_output):
    unused, pullback = jax.vjp(layer_norm, values, gain_row, offset)
    return pullback(grad_output)


def gelu_tanh(values):
    return jax.nn.gelu(values, approximate=True)


def matmul(left_side, right_side):
    return jnp.dot(left_side, right_side, preferred_element_type=f32)


def contract_rows(left_side, right_side):
    return lax.dot_general(
        left_side, right_side, (((0,), (0,)), ((), ())), preferred_element_type=f32
    )


def contract_cols(left_side, right_side):
    return lax.dot_general(
        left_side, right_side, (((1,), (1,)), ((), ())), preferred_element_type=f32
    )


class Links:
    def __init__(self):
        self.wide = lax.axis_size("wide")
        self.narrow = lax.axis_size("narrow")
        self.depth = self.wide // 2
        wide_place = lax.axis_index("wide")
        narrow_place = lax.axis_index("narrow")
        self.device = wide_place * self.narrow + narrow_place
        self.z = wide_place // 2
        self.place = {"x": wide_place % 2, "y": narrow_place // 2, "c": narrow_place % 2}

    def swap(self, values, axis):
        if axis == "x":
            return lax.ppermute(values, "wide", [(i, i ^ 1) for i in range(self.wide)])
        step = 2 if axis == "y" else 1
        return lax.ppermute(values, "narrow", [(i, i ^ step) for i in range(self.narrow)])

    def cross(self, values, step):
        return lax.ppermute(values, "wide", [(i, i ^ (2 * step)) for i in range(self.wide)])

    def exchange(self, values, combine):
        for step in (1, 2):
            other = lax.ppermute(values, "narrow", [(i, i ^ step) for i in range(self.narrow)])
            values = combine(values, other)
        step = 1
        while step < self.wide:
            other = lax.ppermute(values, "wide", [(i, i ^ step) for i in range(self.wide)])
            values = combine(values, other)
            step *= 2
        return values

    def to_all(self, values):
        return lax.all_to_all(values, ("wide", "narrow"), 0, 0, tiled=True)

    def gather_early(self, shard):
        near = shard[None]
        for step in self.bits()[:0:-1]:
            near = jnp.concatenate([near, self.cross(near, step)])
        return near

    def gather_late(self, near):
        return jnp.concatenate([near, self.cross(near, 1)])

    def gather_depth(self, shard):
        return self.gather_late(self.gather_early(shard))

    def bits(self):
        return [1 << number for number in range(self.depth.bit_length() - 1)]

    def steps(self):
        found = [0]
        for step in self.bits()[::-1]:
            found = found + [number ^ step for number in found]
        return found

    def plane_first(self, near):
        cut = halves(near.shape[-1])
        left, right = near[..., :cut], near[..., cut:]
        return left, right, self.swap(left, "x"), self.swap(right, "y")

    def plane_second(self, left, right, left_x, right_y):
        left, right = jnp.stack([left, left_x]), jnp.stack([right, right_y])
        return [left, self.swap(left, "y"), right, self.swap(right, "x")]

    def plane_core(self, pieces):
        return pieces + [self.swap(piece, "c") for piece in pieces]

    def gather_plane(self, near):
        return self.plane_core(self.plane_second(*self.plane_first(near)))

    def assemble(self, pieces, core_first=False):
        depth = self.depth
        unused, unused_depth, rows, cut = pieces[0].shape
        width = cut + pieces[2].shape[3]

        def kernel(place, *refs):
            sources, target = refs[:-1], refs[-1]
            x, y, c = place[0], place[1], place[2]
            for number, source in enumerate(sources):
                far_core, far, second = number // 4, number % 2, number // 2 % 2
                to_c = 1 - c if far_core else c
                columns = slice(cut, width) if second else slice(0, cut)
                for side in range(2):
                    across_x, across_y = (far, side) if second else (side, far)
                    to_x = 1 - x if across_x else x
                    to_y = 1 - y if across_y else y
                    if core_first:
                        target[to_c, to_x, to_y, 0, :, columns] = source[side, 0]
                    else:
                        target[0, to_x, to_y, to_c, :, columns] = source[side, 0]

        place = [self.place["x"], self.place["y"], self.place["c"]]
        place = jnp.stack(place + [self.z ^ step for step in self.steps()]).astype(jnp.int32)
        if core_first:
            shape = (2, 2, 2, depth, rows, width)
            target_spec = pl.BlockSpec(
                (2, 2, 2, 1, rows, width), lambda k, place: (0, 0, 0, place[3 + k], 0, 0)
            )
        else:
            shape = (depth, 2, 2, 2, rows, width)
            target_spec = pl.BlockSpec(
                (1, 2, 2, 2, rows, width), lambda k, place: (place[3 + k], 0, 0, 0, 0, 0)
            )
        whole = pl.pallas_call(
            kernel,
            out_shape=jax.ShapeDtypeStruct(shape, pieces[0].dtype),
            grid_spec=pltpu.PrefetchScalarGridSpec(
                num_scalar_prefetch=1,
                grid=(depth,),
                in_specs=[
                    pl.BlockSpec((2, 1, rows, piece.shape[3]), lambda k, place: (0, k, 0, 0))
                    for piece in pieces
                ],
                out_specs=target_spec,
            ),
            compiler_params=pltpu.CompilerParams(vmem_limit_bytes=32 * 2**20),
            name="assemble",
        )(place, *pieces)
        return whole.reshape(-1, width)

    def share_first(self, values):
        cut = halves(values.shape[-1])
        left, right = values[:, :cut], values[:, cut:]
        return left, right, self.swap(left, "x"), self.swap(right, "y")

    def share_second(self, left, right, left_x, right_y):
        left, right = jnp.stack([left, left_x]), jnp.stack([right, right_y])
        return left, right, self.swap(left, "y"), self.swap(right, "x")

    def share_last(self, *pieces):
        return list(pieces) + [self.swap(piece, "c") for piece in pieces]

    def scatter_plane(self, full):
        cut = halves(full.shape[-1])
        x, y = self.place["x"], self.place["y"]

        def pick(values, spot, dim):
            return lax.dynamic_index_in_dim(values, spot, dim, keepdims=False)

        left, right = full[..., :cut], full[..., cut:]
        from_x = self.swap(pick(left, 1 - x, 0), "x")
        from_y = self.swap(pick(right, 1 - y, 1), "y")
        left = (pick(left, x, 0).astype(f32) + from_x.astype(f32)).astype(bf16)
        right = (pick(right, y, 1).astype(f32) + from_y.astype(f32)).astype(bf16)
        from_y = self.swap(pick(left, 1 - y, 0), "y")
        from_x = self.swap(pick(right, 1 - x, 0), "x")
        left = pick(left, y, 0).astype(f32) + from_y.astype(f32)
        right = pick(right, x, 0).astype(f32) + from_x.astype(f32)
        return jnp.concatenate([left, right], axis=-1).astype(bf16)

    def scatter_depth(self, near, *before_last):
        for step in self.bits():
            if step == self.bits()[-1]:
                near = after(near, *before_last)
            pairs = near.reshape((-1, 2) + near.shape[1:])
            bit = self.z // step % 2
            other = lax.dynamic_index_in_dim(pairs, 1 - bit, 1, keepdims=False)
            mine = lax.dynamic_index_in_dim(pairs, bit, 1, keepdims=False)
            other = self.cross(other.astype(bf16), step)
            near = mine.astype(f32) + other.astype(f32)
        return near[0]


def halves(width):
    return width // 256 * 128


def tie(*values):
    return lax.optimization_barrier(values)


def after(values, *others):
    return lax.optimization_barrier((values, *others))[0]


def lane_halves(values, first):
    lane = lax.broadcasted_iota(jnp.int32, values.shape, 1)
    return jnp.where((lane < HEAD_DIM) == first, values, jnp.zeros_like(values))


def attend(qkv_all, pick_rows, allowed, micro_count):
    token_count = qkv_all.shape[0]
    width = qkv_all.shape[1] // 3
    pick_total = pick_rows.shape[0]
    length, picked = token_count // micro_count, pick_total // micro_count
    pair = 2 * HEAD_DIM
    scale = HEAD_DIM ** (-0.5)

    def kernel(qkv_ref, pick_ref, allowed_ref, context_ref, query_ref, prob_ref):
        query_ref[...] = jnp.dot(
            pick_ref[...], qkv_ref[:, :width], preferred_element_type=f32
        ).astype(bf16)
        for micro in range(micro_count):
            rows = slice(micro * picked, (micro + 1) * picked)
            keep = allowed_ref[rows] > 0.5
            keep = jnp.concatenate([keep, keep], axis=0)
            for number in range(width // pair):
                columns = slice(number * pair, (number + 1) * pair)
                keys = qkv_ref[
                    micro * length : (micro + 1) * length,
                    width + number * pair : width + (number + 1) * pair,
                ]
                values = qkv_ref[
                    micro * length : (micro + 1) * length,
                    2 * width + number * pair : 2 * width + (number + 1) * pair,
                ]
                query = query_ref[rows, columns]
                both = jnp.concatenate(
                    [lane_halves(query, True), lane_halves(query, False)], axis=0
                )
                scores = contract_cols(both, keys) * scale
                scores = jnp.where(keep, scores, neg_fill)
                shifted = jnp.exp(scores - jnp.max(scores, axis=1, keepdims=True))
                probs = shifted / jnp.sum(shifted, axis=1, keepdims=True)
                prob_ref[micro, number] = probs
                mixed = jnp.dot(probs.astype(bf16), values, preferred_element_type=f32)
                context_ref[rows, columns] = (
                    lane_halves(mixed[:picked], True) + lane_halves(mixed[picked:], False)
                ).astype(bf16)

    return pl.pallas_call(
        kernel,
        out_shape=(
            jax.ShapeDtypeStruct((pick_total, width), bf16),
            jax.ShapeDtypeStruct((pick_total, width), bf16),
            jax.ShapeDtypeStruct((micro_count, width // pair, 2 * picked, length), f32),
        ),
        compiler_params=pltpu.CompilerParams(vmem_limit_bytes=32 * 2**20),
        name="attend",
    )(qkv_all, pick_rows, allowed)


def attend_backward(qkv_all, pick_rows, query_all, probs_all, grad_context, micro_count):
    token_count = qkv_all.shape[0]
    width = qkv_all.shape[1] // 3
    pick_total = pick_rows.shape[0]
    length, picked = token_count // micro_count, pick_total // micro_count
    pair = 2 * HEAD_DIM
    scale = HEAD_DIM ** (-0.5)

    def kernel(qkv_ref, pick_ref, query_ref, prob_ref, grad_ref, out_ref, query_grad_ref):
        for micro in range(micro_count):
            rows = slice(micro * picked, (micro + 1) * picked)
            tokens = slice(micro * length, (micro + 1) * length)
            for number in range(width // pair):
                columns = slice(number * pair, (number + 1) * pair)
                key_columns = slice(width + number * pair, width + (number + 1) * pair)
                value_columns = slice(2 * width + number * pair, 2 * width + (number + 1) * pair)
                query, grad = query_ref[rows, columns], grad_ref[rows, columns]
                queries = jnp.concatenate(
                    [lane_halves(query, True), lane_halves(query, False)], axis=0
                )
                grads = jnp.concatenate(
                    [lane_halves(grad, True), lane_halves(grad, False)], axis=0
                )
                probs = prob_ref[micro, number]
                grad_probs = contract_cols(grads, qkv_ref[tokens, value_columns])
                inner = jnp.sum(probs * grad_probs, axis=1, keepdims=True)
                grad_scores = (probs * (grad_probs - inner)).astype(bf16)
                mixed = (
                    jnp.dot(
                        grad_scores, qkv_ref[tokens, key_columns], preferred_element_type=f32
                    )
                    * scale
                )
                query_grad_ref[rows, columns] = (
                    lane_halves(mixed[:picked], True) + lane_halves(mixed[picked:], False)
                ).astype(bf16)
                out_ref[tokens, key_columns] = (
                    contract_rows(grad_scores, queries) * scale
                ).astype(bf16)
                out_ref[tokens, value_columns] = contract_rows(probs.astype(bf16), grads).astype(
                    bf16
                )
        out_ref[:, :width] = contract_rows(pick_ref[...], query_grad_ref[...]).astype(bf16)

    return pl.pallas_call(
        kernel,
        out_shape=jax.ShapeDtypeStruct(qkv_all.shape, bf16),
        scratch_shapes=[pltpu.VMEM((pick_total, width), bf16)],
        compiler_params=pltpu.CompilerParams(vmem_limit_bytes=32 * 2**20),
        name="attend_backward",
    )(qkv_all, pick_rows, query_all, probs_all, grad_context)


def plane_products(known, grads, place, depth, widths):
    hidden, model = widths
    rows = known[0].shape[-2]
    width = hidden + 2 * model
    down_rows, model_rows = hidden // (8 * depth), model // (8 * depth)

    def kernel(place_ref, *refs):
        pieces, grad_pieces = refs[:8], refs[8:16]
        down_ref, up_ref, out_ref, known_ref, grads_ref, own_ref = refs[16:]
        for parts, target in ((pieces, known_ref), (grad_pieces, grads_ref)):
            cut = parts[0].shape[-1]
            for far_core in range(2):
                left, right, left_y, right_x = parts[4 * far_core : 4 * far_core + 4]
                for x in range(2):
                    for y in range(2):
                        spot = pl.ds(((far_core * 2 + x) * 2 + y) * rows, rows)
                        target[spot, :cut] = (left_y if y else left)[x]
                        target[spot, cut:] = (right_x if x else right)[y]
        place = place_ref[0]

        def own_columns(count, block_rows):
            feature = lax.broadcasted_iota(jnp.int32, (count, depth * block_rows), 0)
            own = lax.broadcasted_iota(jnp.int32, (count, depth * block_rows), 1)
            block, offset = own // block_rows, own % block_rows
            return jnp.where(
                feature == (block * 8 + place) * block_rows + offset, 1.0, 0.0
            ).astype(bf16)

        if down_rows % 128 == 0:
            for z in range(depth):
                start = pl.multiple_of((z * 8 + place) * down_rows, down_rows)
                own_ref[:, z * down_rows : (z + 1) * down_rows] = known_ref[
                    :, pl.ds(start, down_rows)
                ]
        else:
            own_ref[...] = matmul(known_ref[:, :hidden], own_columns(hidden, down_rows)).astype(
                bf16
            )
        chosen = own_columns(model, model_rows)
        down_ref[...] = contract_rows(own_ref[...], grads_ref[:, hidden : hidden + model]).astype(
            bf16
        )
        own_normed = matmul(known_ref[:, hidden : hidden + model], chosen).astype(bf16)
        up_ref[...] = contract_rows(own_normed, grads_ref[:, :hidden]).astype(bf16)
        own_context = matmul(known_ref[:, hidden + model :], chosen).astype(bf16)
        out_ref[...] = contract_rows(own_context, grads_ref[:, hidden + model :]).astype(bf16)

    in_vmem = pl.BlockSpec(memory_space=pltpu.VMEM)
    down, up, out = pl.pallas_call(
        kernel,
        in_specs=[pl.BlockSpec(memory_space=pltpu.SMEM)] + [in_vmem] * 16,
        out_shape=(
            jax.ShapeDtypeStruct((depth * down_rows, model), bf16),
            jax.ShapeDtypeStruct((depth * model_rows, hidden), bf16),
            jax.ShapeDtypeStruct((depth * model_rows, model), bf16),
        ),
        scratch_shapes=[
            pltpu.VMEM((8 * rows, width), bf16),
            pltpu.VMEM((8 * rows, width), bf16),
            pltpu.VMEM((8 * rows, depth * down_rows), bf16),
        ],
        compiler_params=pltpu.CompilerParams(vmem_limit_bytes=48 * 2**20),
        name="plane_products",
    )(place.reshape(1).astype(jnp.int32), *known, *grads)
    return (
        down.reshape(depth, down_rows, model),
        up.reshape(depth, model_rows, hidden),
        out.reshape(depth, model_rows, model),
    )


def on_lane(place, value):
    lane = lax.broadcasted_iota(jnp.int32, (1, 128), 1)
    return jnp.where(lane == place, value, 0.0)


def whole_sum(values):
    return jnp.sum(jnp.sum(values, axis=0, keepdims=True), axis=1, keepdims=True)


def sum_squares(all_grads, weight_row, target_sum, devices):
    def kernel(table_ref, target_ref, weight_ref, *refs):
        grads, rows_ref = refs[:-1], refs[-1]
        row = on_lane(0, table_ref[...])
        for place, grad in enumerate(grads):
            row = row + on_lane(place + 1, whole_sum(grad[...] * grad[...]))
        rows_ref[:, :128] = jnp.broadcast_to(row, (devices, 128))
        rows_ref[:, 128:] = jnp.broadcast_to(
            weight_ref[...] + on_lane(64, target_ref[...]), (devices, 128)
        )

    table_square = jnp.sum(all_grads[0] * all_grads[0]).reshape(1, 1)
    return pl.pallas_call(
        kernel,
        out_shape=jax.ShapeDtypeStruct((devices, 256), f32),
        name="sum_squares",
    )(table_square, target_sum.reshape(1, 1), weight_row, *all_grads[1:])


grid_steps = 8


def group_specs(arrays):
    table_rows = -(-arrays[0].shape[0] // (8 * grid_steps)) * 8
    specs = [pl.BlockSpec((table_rows, arrays[0].shape[1]), lambda k: (k, 0))]
    for array in arrays[1:5]:
        rows, width = array.shape
        specs.append(pl.BlockSpec((rows, width // grid_steps), lambda k: (0, k)))
    specs.append(pl.BlockSpec(arrays[5].shape, lambda k: (0, 0)))
    return specs


def lamb_directions(totals, all_grads, firsts, seconds, masters):
    devices = totals.shape[0]
    table_count = all_grads[0].shape[0]
    specs = group_specs(all_grads)
    table_rows = specs[0].block_shape[0]
    first_scale = 1.0 / (1.0 - beta_first**step_count)
    second_scale = 1.0 / (1.0 - beta_second**step_count)

    def kernel(totals_ref, *refs):
        grads, olds, squares, weights = refs[:6], refs[6:12], refs[12:18], refs[18:24]
        new_olds, new_squares, directions, rows_ref = refs[24:30], refs[30:36], refs[36:42], refs[42]
        step = pl.program_id(0)
        grad_total = jnp.sum(totals_ref[:, :128], axis=0, keepdims=True)
        factor = jnp.minimum(
            1.0, clip_limit * lax.rsqrt(jnp.sum(grad_total, axis=1, keepdims=True))
        )

        @pl.when(step == 0)
        def _():
            rows_ref[...] = jnp.zeros_like(rows_ref)

        def update(group, rows, live=None):
            clipped = factor * grads[group][rows]
            new_old = beta_first * olds[group][rows] + (1.0 - beta_first) * clipped
            new_square = beta_second * squares[group][rows] + (1.0 - beta_second) * clipped * clipped
            direction = (new_old * first_scale) / (
                jnp.sqrt(new_square * second_scale) + adam_epsilon
            ) + decay_rates[group] * weights[group][rows]
            new_olds[group][rows] = new_old
            new_squares[group][rows] = new_square
            directions[group][rows] = direction
            square = direction * direction
            return square if live is None else jnp.where(live, square, 0.0)

        def table_part(part, total):
            rows = pl.ds(pl.multiple_of(part * 8, 8), 8)
            place = step * table_rows + part * 8 + lax.broadcasted_iota(
                jnp.int32, (8, 1), 0
            )
            return total + update(0, (rows, slice(None)), place < table_count)

        table_total = lax.fori_loop(
            0, table_rows // 8, table_part, jnp.zeros((8, all_grads[0].shape[1]), f32)
        )
        row = on_lane(0, whole_sum(table_total))
        for group in range(1, 5):
            row = row + on_lane(group, whole_sum(update(group, (slice(None), slice(None)))))
        rows_ref[...] += jnp.broadcast_to(row, rows_ref.shape)

        @pl.when(step == 0)
        def _():
            row = on_lane(5, whole_sum(update(5, (slice(None), slice(None)))))
            rows_ref[...] += jnp.broadcast_to(row, rows_ref.shape)

    shapes = [jax.ShapeDtypeStruct(array.shape, f32) for array in all_grads]
    results = pl.pallas_call(
        kernel,
        grid=(grid_steps,),
        in_specs=[pl.BlockSpec(totals.shape, lambda k: (0, 0))] + specs * 4,
        out_specs=specs * 3 + [pl.BlockSpec((devices, 128), lambda k: (0, 0))],
        out_shape=shapes * 3 + [jax.ShapeDtypeStruct((devices, 128), f32)],
        compiler_params=pltpu.CompilerParams(vmem_limit_bytes=56 * 2**20),
        name="lamb_directions",
    )(totals, *all_grads, *firsts, *seconds, *masters)
    return results[:6], results[6:12], results[12:18], results[18]


def lamb_weights(totals, update_rows, directions, masters):
    specs = group_specs(masters)

    def kernel(totals_ref, updates_ref, *refs):
        moves, weights, news, facts_ref = refs[:6], refs[6:12], refs[12:18], refs[18]
        step = pl.program_id(0)
        lane = lax.broadcasted_iota(jnp.int32, (1, 128), 1)
        grad_total = jnp.sum(totals_ref[:, :128], axis=0, keepdims=True)
        weight_total = jnp.sum(totals_ref[:, 128:], axis=0, keepdims=True)
        update_total = jnp.sum(updates_ref[...], axis=0, keepdims=True)
        weight_norms = jnp.where(lane < 6, jnp.sqrt(jnp.maximum(weight_total, 0.0)), 0.0)
        update_norms = jnp.where(lane < 6, jnp.sqrt(update_total), 1.0)
        rates = learn_rate * weight_norms / update_norms
        for group in range(5):
            rate = jnp.sum(jnp.where(lane == group, rates, 0.0), axis=1, keepdims=True)
            news[group][...] = weights[group][...] - rate * moves[group][...]

        @pl.when(step == 0)
        def _():
            rate = jnp.sum(jnp.where(lane == 5, rates, 0.0), axis=1, keepdims=True)
            news[5][...] = weights[5][...] - rate * moves[5][...]
            grad_norm = jnp.sqrt(jnp.sum(grad_total, axis=1, keepdims=True))
            factor = jnp.minimum(1.0, clip_limit / grad_norm)
            target = jnp.sum(jnp.where(lane == 64, weight_total, 0.0), axis=1, keepdims=True)
            facts_ref[0:1] = factor * jnp.sqrt(grad_total)
            facts_ref[1:2] = weight_norms
            facts_ref[2:3] = update_norms
            facts_ref[3:4] = jnp.broadcast_to(grad_norm, (1, 128))
            facts_ref[4:5] = jnp.broadcast_to(target, (1, 128))

    results = pl.pallas_call(
        kernel,
        grid=(grid_steps,),
        in_specs=[
            pl.BlockSpec(totals.shape, lambda k: (0, 0)),
            pl.BlockSpec(update_rows.shape, lambda k: (0, 0)),
        ]
        + specs * 2,
        out_specs=specs + [pl.BlockSpec((8, 128), lambda k: (0, 0))],
        out_shape=[jax.ShapeDtypeStruct(array.shape, f32) for array in masters]
        + [jax.ShapeDtypeStruct((8, 128), f32)],
        compiler_params=pltpu.CompilerParams(vmem_limit_bytes=56 * 2**20),
        name="lamb_weights",
    )(totals, update_rows, *directions, *masters)
    return results[:6], results[6]


def per_device(
    token_ids,
    doc_ids,
    loss_positions,
    tied_table_master,
    qkv_master,
    out_master,
    up_master,
    down_master,
    norm_master,
    table_first_moment,
    first_qkv,
    first_out,
    first_up,
    first_down,
    first_norms,
    table_second_moment,
    second_qkv,
    second_out,
    second_up,
    second_down,
    second_norms,
):
    links = Links()
    devices = links.wide * links.narrow
    micro_count, unused, length = token_ids.shape
    picked_count = loss_positions.shape[2]
    token_count = micro_count * length
    pick_total = micro_count * picked_count
    model_width = tied_table_master.shape[1]
    head_count = model_width // HEAD_DIM
    block_size = tied_table_master.shape[0]
    count_all = devices * pick_total
    shard_rows = qkv_master.shape[0]

    tokens = token_ids.reshape(token_count)
    picks = loss_positions.reshape(micro_count, picked_count)
    documents = doc_ids.reshape(micro_count, length)
    mean_load = token_count / devices
    slots = int(math.ceil((mean_load + 6.0 * math.sqrt(mean_load)) / 8.0)) * 8
    owner = tokens // block_size
    local_row = tokens % block_size
    token_place = jnp.arange(token_count)
    earlier = (owner[:, None] == owner[None, :]) & (token_place[None, :] < token_place[:, None])
    rank = jnp.sum(earlier.astype(jnp.int32), axis=1)
    most = jnp.max(rank) + 1
    slot_place = jnp.arange(devices * slots)
    line = -(-(slots + 1 + pick_total) // 128) * 128

    pick_hits = picks[:, :, None] == jnp.arange(length)[None, None, :]
    next_hits = picks[:, :, None] + 1 == jnp.arange(length)[None, None, :]
    own_targets = jnp.sum(
        jnp.where(next_hits, token_ids.reshape(micro_count, 1, length), 0), axis=2
    ).reshape(-1)
    pick_docs = jnp.sum(jnp.where(pick_hits, documents[:, None, :], 0), axis=2)

    def slot_of(round_index):
        inside = (rank >= round_index * slots) & (rank < (round_index + 1) * slots)
        return jnp.where(inside, owner * slots + rank - round_index * slots, -1)

    def message_of(slot):
        wanted = jnp.sum(
            jnp.where(slot[None, :] == slot_place[:, None], local_row[None, :] + 1, 0), axis=1
        ) - 1
        wanted = wanted.reshape(devices, slots)
        return jnp.concatenate(
            [
                wanted,
                jnp.broadcast_to(most, (devices, 1)),
                jnp.broadcast_to(own_targets[None, :], (devices, pick_total)),
                jnp.zeros((devices, line - slots - 1 - pick_total), jnp.int32),
            ],
            axis=1,
        )

    def ask(round_index):
        slot = slot_of(round_index)
        return slot, links.to_all(message_of(slot))[:, :slots].reshape(-1)

    def find(asked):
        row_hits = (asked[:, None] == jnp.arange(block_size)[None, :]).astype(bf16)
        return matmul(row_hits, table_low).astype(bf16)

    def place_rows(slot, landed):
        token_hits = (slot[:, None] == slot_place[None, :]).astype(bf16)
        return matmul(token_hits, landed).astype(bf16)

    def give(slot, grad_low):
        token_hits = (slot[:, None] == slot_place[None, :]).astype(bf16)
        return contract_rows(token_hits, grad_low).astype(bf16)

    def take(asked, landed):
        row_hits = (asked[None, :] == jnp.arange(block_size)[:, None]).astype(bf16)
        return matmul(row_hits, landed)

    gain_width = 128
    qkv_width = qkv_master.shape[1]
    gain_shard = jnp.pad(norm_master, ((0, 0), (0, gain_width - norm_master.shape[1])))
    first_shard = jnp.concatenate([qkv_master, gain_shard], axis=1).astype(bf16)
    first_early = links.gather_early(first_shard)
    first_near = links.gather_late(first_early)
    slot_first = slot_of(0)
    masters = (tied_table_master, qkv_master, out_master, up_master, down_master, norm_master)
    message = message_of(slot_first)
    answer = links.to_all(message)
    second_shard = jnp.concatenate([up_master, out_master], axis=1)
    second_near = links.gather_early(after(second_shard, first_early).astype(bf16))
    down_near = links.gather_early(after(down_master, first_early).astype(bf16))
    table_low = after(tied_table_master, message).astype(bf16)
    asked_first = answer[:, :slots].reshape(-1)
    found = after(find(asked_first), first_near, second_near, down_near)
    landed = links.to_all(found)
    rounds = (jnp.max(answer[:, slots]) + slots - 1) // slots
    targets = answer[:, slots + 1 : slots + 1 + pick_total]
    targets = targets.reshape(links.depth, 2, 2, 2, pick_total).transpose(3, 1, 2, 0, 4).reshape(-1)
    first_whole = links.assemble(links.gather_plane(first_near))
    second_near = links.gather_late(second_near)
    second_parts = links.plane_first(after(second_near, first_whole))
    weight_row = sum(
        on_lane(place, after(jnp.sum(weight * weight), found))
        for place, weight in enumerate(masters)
    )
    qkv_weight = first_whole[:, :qkv_width]
    gain_entries = first_whole[:, qkv_width : qkv_width + 6].astype(f32).T

    def more_rows(state):
        round_index, embedded = state
        slot, asked = ask(round_index)
        return (round_index + 1, embedded + place_rows(slot, links.to_all(find(asked))))

    unused_round, x_low = lax.while_loop(
        lambda state: state[0] < rounds,
        more_rows,
        (jnp.ones((), jnp.int32), place_rows(slot_first, landed)),
    )

    x_embed = x_low.astype(f32)
    normed_one = layer_norm(x_embed, gain_entries[0], gain_entries[1]).astype(bf16)
    second_pieces = links.plane_second(*second_parts)
    down_parts = links.plane_first(links.gather_late(after(down_near, normed_one)))
    qkv_all = matmul(normed_one, qkv_weight).astype(bf16)
    pick_rows = (
        pick_hits[:, :, None, :] & jnp.eye(micro_count, dtype=bool)[:, None, :, None]
    ).reshape(pick_total, token_count).astype(bf16)
    x_embed_picked = matmul(pick_rows, x_low)
    allowed = (jnp.arange(length)[None, None, :] <= picks[:, :, None]) & (
        documents[:, None, :] == pick_docs[:, :, None]
    )
    context, queries, probs = attend(
        qkv_all, pick_rows, allowed.reshape(pick_total, length).astype(f32), micro_count
    )
    second_whole = links.assemble(
        links.plane_core([after(piece, context) for piece in second_pieces])
    )
    hidden = up_master.shape[1]
    up_weight, out_weight = second_whole[:, :hidden], second_whole[:, hidden:]
    down_pieces = links.plane_second(*[after(part, context) for part in down_parts])
    down_weight = links.assemble(links.plane_core(down_pieces))
    x_attn = x_embed_picked + matmul(context, out_weight)
    normed_two = layer_norm(x_attn, gain_entries[2], gain_entries[3]).astype(bf16)
    up_value = matmul(normed_two, up_weight)
    activated = gelu_tanh(up_value).astype(bf16)
    x_out = x_attn + matmul(activated, down_weight)
    picked_low = layer_norm(x_out, gain_entries[4], gain_entries[5]).astype(bf16)

    head_rows = links.assemble(
        links.gather_plane(links.gather_depth(picked_low)), core_first=True
    )
    columns = links.device * block_size + jnp.arange(block_size)
    logits = contract_cols(head_rows, table_low)
    logits = jnp.where((columns < VOCAB)[None, :], logits, neg_fill)
    target_hits = targets[:, None] == columns[None, :]
    target_sum = jnp.sum(jnp.where(target_hits, logits, 0.0))
    local_top = jnp.max(logits, axis=1)
    local_sum = jnp.sum(jnp.exp(logits - local_top[:, None]), axis=1)

    def merge_totals(first, second):
        top = jnp.maximum(first[0], second[0])
        total = first[1] * jnp.exp(first[0] - top) + second[1] * jnp.exp(second[0] - top)
        return jnp.stack([top, total])

    known = jnp.concatenate([activated, normed_two, context], axis=1)
    known, head_rows = tie(known, head_rows)
    known_parts = links.share_first(known)
    local_sum, *known_parts = tie(local_sum, *known_parts)
    known_parts = links.share_second(*known_parts)
    merged = links.exchange(jnp.stack([local_top, local_sum]), merge_totals)
    log_total = merged[0] + jnp.log(merged[1])
    grad_logits = (
        (jnp.exp(logits - log_total[:, None]) - target_hits.astype(f32)) / count_all
    ).astype(bf16)
    half_rows = head_rows.shape[0] // 2
    core = links.place["c"]

    def picked_part(spot):
        part = lax.dynamic_slice_in_dim(grad_logits, spot * half_rows, half_rows, 0)
        return matmul(part, table_low)

    to_core = picked_part(1 - core).astype(bf16)
    to_core, grad_logits = tie(to_core, grad_logits)
    from_core = links.swap(to_core, "c")
    grad_near = links.scatter_plane(
        (picked_part(core) + from_core.astype(f32))
        .astype(bf16)
        .reshape(2, 2, links.depth, pick_total, model_width)
    )
    grad_near, grad_logits = tie(grad_near, grad_logits)
    table_head = contract_rows(grad_logits, head_rows)
    known = links.share_last(*[after(part, grad_near) for part in known_parts])
    grad_picked = links.scatter_depth(grad_near)

    grad_x_out, gain_last, shift_last = norm_backward(
        x_out, gain_entries[4], gain_entries[5], grad_picked
    )
    grad_mlp = grad_x_out.astype(bf16)
    unused, gelu_pull = jax.vjp(gelu_tanh, up_value)
    grad_up_low = gelu_pull(contract_cols(grad_mlp, down_weight))[0].astype(bf16)
    grad_x_attn, gain_two, shift_two = norm_backward(
        x_attn, gain_entries[2], gain_entries[3], contract_cols(grad_up_low, up_weight)
    )
    grad_x_attn = grad_x_out + grad_x_attn
    grad_attn_low = grad_x_attn.astype(bf16)
    grad_context = contract_cols(grad_attn_low, out_weight).astype(bf16)
    grad_parts = links.share_first(
        jnp.concatenate([grad_up_low, grad_mlp, grad_attn_low], axis=1)
    )
    grad_qkv_low = attend_backward(
        qkv_all, pick_rows, queries, probs, grad_context, micro_count
    )
    late = after(grad_qkv_low, *grad_parts)
    grad_parts = links.share_second(*grad_parts)
    grad_x_one, gain_one, shift_one = norm_backward(
        x_embed, gain_entries[0], gain_entries[1], contract_cols(late, qkv_weight)
    )
    grad_x_embed = grad_x_one + lax.dot_general(
        pick_rows.astype(f32),
        grad_x_attn,
        (((0,), (0,)), ((), ())),
        precision=lax.Precision.HIGHEST,
        preferred_element_type=f32,
    )
    grad_embed_low = grad_x_embed.astype(bf16)
    sent = give(slot_first, grad_embed_low)
    grad_qkv_low = after(grad_qkv_low, sent)
    returned = links.to_all(sent)
    down_near, up_near, out_near = plane_products(
        known,
        links.share_last(*[after(part, sent) for part in grad_parts]),
        (links.place["x"] * 2 + links.place["y"]) * 2 + core,
        links.depth,
        (activated.shape[1], model_width),
    )

    half_place = jnp.arange(model_width // 2)
    half_row = half_place % shard_rows
    half_z = half_place // shard_rows % links.depth
    half_plane = half_place // shard_rows // links.depth

    def qkv_part(spot):
        source = ((half_z * 4 + half_plane) * 2 + spot) * shard_rows + half_row
        columns = (jnp.arange(model_width)[:, None] == source[None, :]).astype(bf16)
        return contract_rows(matmul(normed_one, columns).astype(bf16), grad_qkv_low)

    to_core = qkv_part(1 - core).astype(bf16)
    from_core = links.swap(to_core, "c")
    last_near = links.scatter_plane(
        (qkv_part(core) + from_core.astype(f32))
        .astype(bf16)
        .reshape(2, 2, links.depth, shard_rows, qkv_width)
    )
    last_near = jnp.concatenate([last_near, out_near], axis=-1)
    down_grad = links.scatter_depth(down_near, returned)
    up_grad = links.scatter_depth(up_near, returned)
    last_grad = links.scatter_depth(after(last_near, returned))
    qkv_grad, out_grad = last_grad[:, :qkv_width], last_grad[:, qkv_width:]
    gain_grads = jnp.stack(
        [gain_one, shift_one, gain_two, shift_two, gain_last, shift_last]
    ).reshape(6, devices, shard_rows)
    gain_grads = jnp.pad(
        gain_grads.transpose(1, 0, 2).reshape(devices, 6 * shard_rows),
        ((0, 0), (0, -6 * shard_rows % 128)),
    )
    gain_grad = jnp.sum(links.to_all(after(gain_grads, returned)), axis=0)[: 6 * shard_rows]
    gain_grad = gain_grad.reshape(6, shard_rows).T

    def more_grads(state):
        round_index, earlier_grad = state
        slot, asked = ask(round_index)
        returned_rows = links.to_all(give(slot, grad_embed_low))
        return (round_index + 1, earlier_grad + take(asked, returned_rows))

    unused_round, table_grad = lax.while_loop(
        lambda state: state[0] < rounds,
        more_grads,
        (
            jnp.ones((), jnp.int32),
            table_head + take(asked_first, returned),
        ),
    )

    all_grads = (table_grad, qkv_grad, out_grad, up_grad, down_grad, gain_grad)
    firsts = (table_first_moment, first_qkv, first_out, first_up, first_down, first_norms)
    seconds = (table_second_moment, second_qkv, second_out, second_up, second_down, second_norms)
    totals = links.to_all(sum_squares(all_grads, weight_row, target_sum, devices))
    new_firsts, new_seconds, directions, update_rows = lamb_directions(
        totals, all_grads, firsts, seconds, masters
    )
    new_weights, facts = lamb_weights(totals, links.to_all(update_rows), directions, masters)
    return (
        (jnp.sum(log_total) - facts[4, 0]) / count_all,
        facts[3, 0],
        facts[:3, :6],
        *new_weights,
        *new_firsts,
        *new_seconds,
    )


def solution(mesh):
    rows = P(("wide", "narrow"), None)
    ids = P(None, ("wide", "narrow"), None)
    return jax.shard_map(
        per_device,
        mesh=mesh,
        in_specs=(ids,) * 3 + (rows,) * 18,
        out_specs=(P(),) * 3 + (rows,) * 18,
        check_vma=False,
    )
```

time: 917 us -> 710 us (0.77)
  local copies, waits for them, and re-layouts: 162 us -> 42.2 us
  Pallas kernels: 0 us -> 65.7 us
  other arithmetic: 122 us -> 73.7 us
  waiting for transfers between devices: 364 us -> 317 us
  matrix products: 128 us -> 98.1 us
  starting transfers between devices: 115 us -> 88.7 us
  loops' own time: 0.41 us -> 11.5 us
  between operations: 16.7 us -> 6.55 us
    pallas_call x0 -> x10, Pallas kernels: none -> 65.7 us  [the longest x1 23.1 us: lamb_directions(): pl.pallas_call(kernel, grid=(grid_steps,), in_specs=[pl.BlockSpec(totals....]
    dynamic_update_slice x36 -> x0, local copies, waits for them, and re-layouts: 55 us -> none  [the longest x24 48.5 us: gather(): both = lax.dynamic_update_slice(both, block, start)]
    ppermute x24 -> x16, waiting for transfers between devices: 62.7 us -> 100 us  [cross(): lax.ppermute(values, 'wide', [(i, i ^ 2 * step) for i in range(self.wide)])]
    ppermute x12 -> x3, waiting for transfers between devices: 46.9 us -> 9.54 us  [exchange(): lax.ppermute(values, 'wide', [(i, i ^ step) for i in range(self.wide)])]
    reduce_sum x21 -> x10, other arithmetic: 50.9 us -> 14 us  [the longest x6 7.7 us: per_device(): jnp.sum(weight * weight)]
    ppermute x8 -> x16, waiting for transfers between devices: 126 us -> 90.3 us  [swap(): return lax.ppermute(values, 'wide', [(i, i ^ 1) for i in range(self.wide)])]
    ppermute x12 -> x3, starting transfers between devices: 29.9 us -> 2.77 us  [exchange(): lax.ppermute(values, 'wide', [(i, i ^ step) for i in range(self.wide)])]
    ppermute x24 -> x16, starting transfers between devices: 41.6 us -> 17.4 us  [cross(): lax.ppermute(values, 'wide', [(i, i ^ 2 * step) for i in range(self.wide)])]
  transfers between devices with their start and end apart: 71 -> 85, of which waited for: 41 -> 44; matrix products, arithmetic and copies ran while one was open for 22% -> 22% of each run, Pallas kernels for 0% -> 3%
where the time goes in v2:
time: 710 us; the launch traced here: 703 us
  waiting for transfers between devices  317 us (45%)
  matrix products  98.1 us (14%)
  starting transfers between devices  88.7 us (12%)
  other arithmetic  73.7 us (10%)
  Pallas kernels  65.7 us (9%)
  local copies, waits for them, and re-layouts  42.2 us (6%)
  loops' own time  11.5 us (2%)
    ppermute x42, waiting for transfers between devices, swap(): lax.ppermute(values, 'narrow', [(i, i ^ step) for i in range(self.narrow)])  102 us
    ppermute x16, waiting for transfers between devices, cross(): lax.ppermute(values, 'wide', [(i, i ^ 2 * step) for i in range(self.wide)])  100 us
    ppermute x16, waiting for transfers between devices, swap(): return lax.ppermute(values, 'wide', [(i, i ^ 1) for i in range(self.wide)])  90.3 us
    dot_general x10, matrix products, matmul(): return jnp.dot(left_side, right_side, preferred_element_type=f32)  45.2 us
    dot_general x4, matrix products, contract_rows(): lax.dot_general(left_side, right_side, (((0,), (0,)), ((), ())), preferre...  29.3 us
    ppermute x42, starting transfers between devices, swap(): lax.ppermute(values, 'narrow', [(i, i ^ step) for i in range(self.narrow)])  25.6 us
    all_to_all x6, starting transfers between devices, to_all(): return lax.all_to_all(values, ('wide', 'narrow'), 0, 0, tiled=True)  24.5 us
    pallas_call x1, Pallas kernels, lamb_directions(): pl.pallas_call(kernel, grid=(grid_steps,), in_specs=[pl.BlockSpec(totals....  23.1 us
  transfers between devices with their start and end apart: 85, of which 44 were waited for; matrix products, arithmetic and copies ran while one was open for 22% of the time, Pallas kernels for 3%

profile of v2, /device:TPU:0, one launch (start us, length us, event | category | flops | bytes accessed | tf_op | source)
XLA Modules:
  0.0 703.2 jit_solution(9978291196968986519)
XLA Ops:
  28.2 8.3 %fusion.35 = bf16[1280,1024]{1,0:T(8,128)(2,1)} fusion(bf16[1572,1024]{1,0:T(8,128)(2,1)} %convert_element_type.287, s32[1280]{0:T(1024)S(1)} %eq.436), kind=kOutput, calls=%fused_computation.60 | convolution fusion | flops 4124226560 | bytes 5846016 | tf_op jit(solution)/shard_map/dot_general | solution.py:42
  37.5 10.3 %collective-permute-done.3 = bf16[1,128,1024]{2,1,0:T(8,128)(2,1)S(1)} collective-permute-done((bf16[1,128,1024]{2,1,0:T(8,128)(2,1)S(1)}, bf16[1,128,1024]{2,1,0:T(8,128)(2,1)S(1)}, u32[]{:S(2)}, u32[]{:S(2)}) %collective-permute-start.3) | collective-permute-done | bytes 262176 | tf_op jit(solution)/shard_map/ppermute | solution.py:75
  68.7 31.2 %collective-permute-done.6 = bf16[4,32,1664]{2,1,0:T(8,128)(2,1)S(1)} collective-permute-done((bf16[4,32,1664]{2,1,0:T(8,128)(2,1)S(1)}, bf16[4,32,1664]{2,1,0:T(8,128)(2,1)S(1)}, u32[]{:S(2)}, u32[]{:S(2)}) %collective-permute-start.6) | collective-permute-done | bytes 426016 | tf_op jit(solution)/shard_map/ppermute | solution.py:72
  103.2 23.4 %collective-permute-done.7.refs_3_ = bf16[2,4,32,1664]{3,2,1,0:T(8,128)(2,1)S(1)} collective-permute-done((bf16[2,4,32,1664]{3,2,1,0:T(8,128)(2,1)S(1)}, bf16[2,4,32,1664]{3,2,1,0:T(8,128)(2,1)S(1)}, u32[]{:S(2)}, u32[]{:S(2)}) %collective-permute-start.7) | collective-permute-done | bytes 852000 | tf_op jit(solution)/shard_map/ppermute | solution.py:70
  148.5 11.5 %while.30 = (s32[]{:T(128)}, bf16[512,1024]{1,0:T(8,128)(2,1)S(1)}, s32[]{:T(128)}, s32[512]{0:T(512)S(1)}, s32[512]{0:T(512)S(1)}, /*index=5*/s32[512]{0:T(512)...) while((s32[]{:T(128)}, bf16[512,1024]{1,0:T(8,128)(2,1)S(1)}, ...), condition=%wide.wide.region_7.8_spmd.clone.clone, body=%wide.wide.region_5.7_spmd.clone.clone.sunk | while | flops 5470090240 | bytes 15917673 | solution.py:698
  166.9 8.6 %collective-permute-done.21 = bf16[2,128,1024]{2,1,0:T(8,128)(2,1)S(1)} collective-permute-done((bf16[2,128,1024]{2,1,0:T(8,128)(2,1)S(1)}, bf16[2,128,1024]{2,1,0:T(8,128)(2,1)S(1)}, u32[]{:S(2)}, u32[]{:S(2)}) %collective-permute-start.21) | collective-permute-done | bytes 524320 | tf_op jit(solution)/shard_map/ppermute | solution.py:75
  197.2 8.0 %collective-permute-done.24 = bf16[4,128,512]{2,1,0:T(8,128)(2,1)S(1)} collective-permute-done((bf16[4,128,512]{2,1,0:T(8,128)(2,1)S(1)}, bf16[4,128,512]{2,1,0:T(8,128)(2,1)S(1)}, u32[]{:S(2)}, u32[]{:S(2)}) %collective-permute-start.24) | collective-permute-done | bytes 524320 | tf_op jit(solution)/shard_map/ppermute | solution.py:72
  206.1 12.2 %collective-permute-done.22 = bf16[4,128,512]{2,1,0:T(8,128)(2,1)S(1)} collective-permute-done((bf16[4,128,512]{2,1,0:T(8,128)(2,1)S(1)}, bf16[4,128,512]{2,1,0:T(8,128)(2,1)S(1)}, u32[]{:S(2)}, u32[]{:S(2)}) %collective-permute-start.22) | collective-permute-done | bytes 524320 | tf_op jit(solution)/shard_map/ppermute | solution.py:70
  224.3 17.7 %collective-permute-done.23.refs_1_ = bf16[2,4,128,512]{3,2,1,0:T(8,128)(2,1)S(1)} collective-permute-done((bf16[2,4,128,512]{3,2,1,0:T(8,128)(2,1)S(1)}, bf16[2,4,128,512]{3,2,1,0:T(8,128)(2,1)S(1)}, u32[]{:S(2)}, u32[]{:S(2)}) %collective-permute-start.23) | collective-permute-done | bytes 1048608 | tf_op jit(solution)/shard_map/ppermute | solution.py:72
  252.3 8.8 %collective-permute-done.30 = bf16[1,64,1024]{2,1,0:T(8,128)(2,1)S(1)} collective-permute-done((bf16[1,64,1024]{2,1,0:T(8,128)(2,1)S(1)}, bf16[1,64,1024]{2,1,0:T(8,128)(2,1)S(1)}, u32[]{:S(2)}, u32[]{:S(2)}) %collective-permute-start.30) | collective-permute-done | bytes 131104 | tf_op jit(solution)/shard_map/ppermute | solution.py:75
  261.2 8.0 %collective-permute-done.31 = bf16[2,64,1024]{2,1,0:T(8,128)(2,1)S(1)} collective-permute-done((bf16[2,64,1024]{2,1,0:T(8,128)(2,1)S(1)}, bf16[2,64,1024]{2,1,0:T(8,128)(2,1)S(1)}, u32[]{:S(2)}, u32[]{:S(2)}) %collective-permute-start.31) | collective-permute-done | bytes 262176 | tf_op jit(solution)/shard_map/ppermute | solution.py:75
  279.6 9.1 %collective-permute-done.33.refs_1_ = bf16[2,4,64,512]{3,2,1,0:T(8,128)(2,1)S(1)} collective-permute-done((bf16[2,4,64,512]{3,2,1,0:T(8,128)(2,1)S(1)}, bf16[2,4,64,512]{3,2,1,0:T(8,128)(2,1)S(1)}, u32[]{:S(2)}, u32[]{:S(2)}) %collective-permute-start.33) | collective-permute-done | bytes 524320 | tf_op jit(solution)/shard_map/ppermute | solution.py:72
  345.8 7.5 %add_convert_fusion.1 = bf16[1024,1024]{1,0:T(8,128)(2,1)S(1)} fusion(bf16[1024,1024]{1,0:T(8,128)(2,1)} %collective-permute-done.47, bf16[1572,1024]{1,0:T(8,128)(2,1)} %get-tuple-element.1115, bf16[2048,1572]{0,1:T(8,128)(2,1)} %copy-done.21, s32[]{:T(128)S(6)} %select_n.356), kind=kOutput, calls=%fused_computation.56 | convolution fusion | flops 3299868672 | bytes 10649604 | tf_op jit(solution)/shard_map/dot_general | solution.py:42
  428.5 15.7 %collective-permute-done.68.refs_11_ = bf16[2,64,3072]{2,1,0:T(8,128)(2,1)S(1)} collective-permute-done((bf16[2,64,3072]{2,1,0:T(8,128)(2,1)S(1)}, bf16[2,64,3072]{2,1,0:T(8,128)(2,1)S(1)}, u32[]{:S(2)}, u32[]{:S(2)}) %collective-permute-start.68) | collective-permute-done | bytes 786464 | tf_op jit(solution)/shard_map/ppermute | solution.py:70
  469.5 12.2 %fusion.141 = f32[1572,1024]{1,0:T(8,128)} fusion(bf16[2048,1572]{0,1:T(8,128)(2,1)} %copy-done.21, bf16[2048,1024]{1,0:T(8,128)(2,1)} %bitcast.325), kind=kOutput, calls=%fused_computation.332 | convolution fusion | flops 6593445888 | bytes 17072128 | tf_op jit(solution)/shard_map/dot_general | solution.py:46
  482.6 8.0 %plane_products.1 = (bf16[512,1024]{1,0:T(8,128)(2,1)}, bf16[128,4096]{1,0:T(8,128)(2,1)}, bf16[128,1024]{1,0:T(8,128)(2,1)S(1)}) custom-call(s32[1]{0:T(128)} %bitcast.91.place_ref, bf16[2,64,3072]{2,1,0:T(8,128)(2,1)} %pad_maximum_fusion.10.refs_0_, bf16[2,64,3072]{2,1,0:T(8,128)(2,1)S(1)} %pad_maximum_fusion.11.refs_1_, ...), custom_call_target="tpu_custom_call" | custom-call | tf_op jit(solution)/shard_map/plane_products/pallas_call | solution.py:390
  508.1 17.7 %collective-permute-done.75 = bf16[2,32,4096]{2,1,0:T(8,128)(2,1)} collective-permute-done((bf16[2,32,4096]{2,1,0:T(8,128)(2,1)}, bf16[2,32,4096]{2,1,0:T(8,128)(2,1)}, u32[]{:S(2)}, u32[]{:S(2)}) %collective-permute-start.75) | collective-permute-done | bytes 524320 | tf_op jit(solution)/shard_map/ppermute | solution.py:75
  533.3 12.7 %collective-permute-done.59 = bf16[2,4,32,1536]{3,2,1,0:T(8,128)(2,1)S(1)} collective-permute-done((bf16[2,4,32,1536]{3,2,1,0:T(8,128)(2,1)S(1)}, bf16[2,4,32,1536]{3,2,1,0:T(8,128)(2,1)S(1)}, u32[]{:S(2)}, u32[]{:S(2)}) %collective-permute-start.59) | collective-permute-done | bytes 786464 | tf_op jit(solution)/shard_map/ppermute | solution.py:72
  546.3 17.1 %collective-permute-done.57 = bf16[2,4,32,1536]{3,2,1,0:T(8,128)(2,1)S(1)} collective-permute-done((bf16[2,4,32,1536]{3,2,1,0:T(8,128)(2,1)S(1)}, bf16[2,4,32,1536]{3,2,1,0:T(8,128)(2,1)S(1)}, u32[]{:S(2)}, u32[]{:S(2)}) %collective-permute-start.57) | collective-permute-done | bytes 786464 | tf_op jit(solution)/shard_map/ppermute | solution.py:70
  574.2 9.0 %fusion.33 = f32[1572,1024]{1,0:T(8,128)} fusion(f32[1572,1024]{1,0:T(8,128)} %fusion.141, bf16[1280,1024]{1,0:T(8,128)(2,1)} %bitcast.79, s32[1280]{0:T(1024)S(1)} %copy-done.58), kind=kOutput, calls=%fused_computation.57 | convolution fusion | flops 4124525568 | bytes 15504384 | tf_op jit(solution)/shard_map/dot_general | solution.py:42
  600.9 17.7 %collective-permute-done.73 = bf16[2,32,4096]{2,1,0:T(8,128)(2,1)} collective-permute-done((bf16[2,32,4096]{2,1,0:T(8,128)(2,1)}, bf16[2,32,4096]{2,1,0:T(8,128)(2,1)}, u32[]{:S(2)}, u32[]{:S(2)}) %collective-permute-start.73) | collective-permute-done | bytes 524320 | tf_op jit(solution)/shard_map/ppermute | solution.py:75
  625.1 8.6 %collective-permute-done.74 = bf16[1,32,4096]{2,1,0:T(8,128)(2,1)S(1)} collective-permute-done((bf16[1,32,4096]{2,1,0:T(8,128)(2,1)S(1)}, bf16[1,32,4096]{2,1,0:T(8,128)(2,1)S(1)}, u32[]{:S(2)}, u32[]{:S(2)}) %collective-permute-start.74) | collective-permute-done | bytes 262176 | tf_op jit(solution)/shard_map/ppermute | solution.py:75
  652.3 23.1 %lamb_directions.1 = (f32[1572,1024]{1,0:T(8,128)}, f32[32,3072]{1,0:T(8,128)}, f32[32,1024]{1,0:T(8,128)}, f32[32,4096]{1,0:T(8,128)}, f32[128,1024]{1,0:T(8,12...) custom-call(f32[32,256]{1,0:T(8,128)} %bitcast.367, ...), custom_call_target="tpu_custom_call" | custom-call | tf_op jit(solution)/shard_map/lamb_directions/pallas_call | solution.py:509
  685.7 10.9 %lamb_weights.1 = (f32[1572,1024]{1,0:T(8,128)}, f32[32,3072]{1,0:T(8,128)}, f32[32,1024]{1,0:T(8,128)}, f32[32,4096]{1,0:T(8,128)}, f32[128,1024]{1,0:T(8,128)}, /*index=5*/f32[32,6]{1,0:T(8,128)}, f32[8,128]{1,0:T(8,128)}) custom-call(f32[32,256]{1,0:T(8,128)} %bitcast.368, f32[32,128]{1,0:T(8,128)} %bitcast.386, f32[1572,1024]{1,0:T(8,128)} %get-tuple-element.414.refs_0_, ...), custom_call_target="tpu_custom_call" | custom-call | tf_op jit(solution)/shard_map/lamb_weights/pallas_call | solution.py:551
  (553 shorter events, 379.2 us)
Async XLA Ops:
  27.2 26.8 %collective-permute-start.2 = (bf16[1,32,5120]{2,1,0:T(8,128)(2,1)S(1)}, bf16[1,32,5120]{2,1,0:T(8,128)(2,1)S(1)}, u32[]{:S(2)}, u32[]{:S(2)}) collective-permute-start(bf16[1,32,5120]{2,1,0:T(8,128)(2,1)S(1)} %bitcast.335), channel_id=1, source_target_pairs={{0,16},{4,20},{8,24},{12,28},{16,0},{20,4},{24,8},{28,12},{1,17},{... | collective-permute-start | bytes 983048 | tf_op jit(solution)/shard_map/ppermute | solution.py:75
  59.0 86.1 %all-to-all-start.5 = ((bf16[32,40,1024]{2,1,0:T(8,128)(2,1)}), bf16[32,40,1024]{2,1,0:T(8,128)(2,1)}, u32[]{:S(2)}, u32[]{:S(2)}) async-start(bf16[32,40,1024]{2,1,0:T(8,128)(2,1)} %bitcast.338), calls=%async_computation.5 | async-start | bytes 5242880 | tf_op jit(solution)/shard_map/all_to_all | solution.py:89
  65.4 34.6 %collective-permute-start.6 = (bf16[4,32,1664]{2,1,0:T(8,128)(2,1)S(1)}, bf16[4,32,1664]{2,1,0:T(8,128)(2,1)S(1)}, u32[]{:S(2)}, u32[]{:S(2)}) collective-permute-start(bf16[4,32,1664]{2,1,0:T(8,128)(2,1)S(1)} %get-tuple-element.732), channel_id=1, source_target_pairs={{0,2},{1,3},{2,0},{3,1},{4,6},{5,7},{6,4},{7,5},{8,10},{9,11},{10,... | collective-permute-start | bytes 1277960 | tf_op jit(solution)/shard_map/ppermute | solution.py:72
  67.2 34.8 %collective-permute-start.4 = (bf16[4,32,1536]{2,1,0:T(8,128)(2,1)S(1)}, bf16[4,32,1536]{2,1,0:T(8,128)(2,1)S(1)}, u32[]{:S(2)}, u32[]{:S(2)}) collective-permute-start(bf16[4,32,1536]{2,1,0:T(8,128)(2,1)S(1)} %get-tuple-element.734), channel_id=1, source_target_pairs={{0,4},{4,0},{8,12},{12,8},{16,20},{20,16},{24,28},{28,24},{1,5},{5... | collective-permute-start | bytes 1179656 | tf_op jit(solution)/shard_map/ppermute | solution.py:70
  100.1 26.4 %collective-permute-start.7 = (bf16[2,4,32,1664]{3,2,1,0:T(8,128)(2,1)S(1)}, bf16[2,4,32,1664]{3,2,1,0:T(8,128)(2,1)S(1)}, u32[]{:S(2)}, u32[]{:S(2)}) collective-permute-start(bf16[2,4,32,1664]{3,2,1,0:T(8,128)(2,1)S(1)} %pad_maximum_fusion.6.refs_2_), channel_id=1, source_target_pairs={{0,4},{4,0},{8,12},{12,8},{16,20},{20,16},{24,28},{28,24},{1,5},{5... | collective-permute-start | bytes 2555912 | tf_op jit(solution)/shard_map/ppermute | solution.py:70
  102.1 26.9 %collective-permute-start.5 = (bf16[2,4,32,1536]{3,2,1,0:T(8,128)(2,1)S(1)}, bf16[2,4,32,1536]{3,2,1,0:T(8,128)(2,1)}, u32[]{:S(2)}, u32[]{:S(2)}) collective-permute-start(bf16[2,4,32,1536]{3,2,1,0:T(8,128)(2,1)S(1)} %pad_maximum_fusion.8.refs_0_), channel_id=1, source_target_pairs={{0,2},{1,3},{2,0},{3,1},{4,6},{5,7},{6,4},{7,5},{8,10},{9,11},{10,... | collective-permute-start | bytes 2359304 | tf_op jit(solution)/shard_map/ppermute | solution.py:72
  103.0 28.1 %collective-permute-start.12 = (bf16[2,32,5120]{2,1,0:T(8,128)(2,1)}, bf16[2,32,5120]{2,1,0:T(8,128)(2,1)}, u32[]{:S(2)}, u32[]{:S(2)}) collective-permute-start(bf16[2,32,5120]{2,1,0:T(8,128)(2,1)} %pad_maximum_fusion.15), channel_id=1, source_target_pairs={{0,8},{4,12},{8,0},{12,4},{16,24},{20,28},{24,16},{28,20},{1,9},{5... | collective-permute-start | bytes 1966088 | tf_op jit(solution)/shard_map/ppermute | solution.py:75
  103.1 30.4 %collective-permute-start.10 = (bf16[2,4,32,1664]{3,2,1,0:T(8,128)(2,1)S(1)}, bf16[2,4,32,1664]{3,2,1,0:T(8,128)(2,1)S(1)}, u32[]{:S(2)}, u32[]{:S(2)}) collective-permute-start(bf16[2,4,32,1664]{3,2,1,0:T(8,128)(2,1)S(1)} %pad_maximum_fusion.6.refs_2_), channel_id=1, source_target_pairs={{0,1},{1,0},{2,3},{3,2},{4,5},{5,4},{6,7},{7,6},{8,9},{9,8},{10,11... | collective-permute-start | bytes 2555912 | tf_op jit(solution)/shard_map/ppermute | solution.py:72
  163.1 33.7 %collective-permute-start.14 = (bf16[2,4,32,2560]{3,2,1,0:T(8,128)(2,1)S(1)}, bf16[2,4,32,2560]{3,2,1,0:T(8,128)(2,1)S(1)}, u32[]{:S(2)}, u32[]{:S(2)}) collective-permute-start(bf16[2,4,32,2560]{3,2,1,0:T(8,128)(2,1)S(1)} %pad_maximum_fusion.1.refs_0_), channel_id=1, source_target_pairs={{0,2},{1,3},{2,0},{3,1},{4,6},{5,7},{6,4},{7,5},{8,10},{9,11},{10,... | collective-permute-start | bytes 3932168 | tf_op jit(solution)/shard_map/ppermute | solution.py:72
  166.4 30.3 %collective-permute-start.16 = (bf16[2,4,32,2560]{3,2,1,0:T(8,128)(2,1)S(1)}, bf16[2,4,32,2560]{3,2,1,0:T(8,128)(2,1)S(1)}, u32[]{:S(2)}, u32[]{:S(2)}) collective-permute-start(bf16[2,4,32,2560]{3,2,1,0:T(8,128)(2,1)S(1)} %pad_maximum_fusion.2.refs_2_), channel_id=1, source_target_pairs={{0,4},{4,0},{8,12},{12,8},{16,20},{20,16},{24,28},{28,24},{1,5},{5... | collective-permute-start | bytes 3932168 | tf_op jit(solution)/shard_map/ppermute | solution.py:70
  175.6 29.6 %collective-permute-start.24 = (bf16[4,128,512]{2,1,0:T(8,128)(2,1)S(1)}, bf16[4,128,512]{2,1,0:T(8,128)(2,1)S(1)}, u32[]{:S(2)}, u32[]{:S(2)}) collective-permute-start(bf16[4,128,512]{2,1,0:T(8,128)(2,1)S(1)} %get-tuple-element.374), channel_id=1, source_target_pairs={{0,2},{1,3},{2,0},{3,1},{4,6},{5,7},{6,4},{7,5},{8,10},{9,11},{10,... | collective-permute-start | bytes 1572872 | tf_op jit(solution)/shard_map/ppermute | solution.py:72
  190.9 29.2 %collective-permute-start.17 = (bf16[2,4,32,2560]{3,2,1,0:T(8,128)(2,1)S(1)}, bf16[2,4,32,2560]{3,2,1,0:T(8,128)(2,1)S(1)}, u32[]{:S(2)}, u32[]{:S(2)}) collective-permute-start(bf16[2,4,32,2560]{3,2,1,0:T(8,128)(2,1)S(1)} %pad_maximum_fusion.1.refs_0_), channel_id=1, source_target_pairs={{0,1},{1,0},{2,3},{3,2},{4,5},{5,4},{6,7},{7,6},{8,9},{9,8},{10,11... | collective-permute-start | bytes 3932168 | tf_op jit(solution)/shard_map/ppermute | solution.py:72
  386.5 27.0 %collective-permute-start.62 = (bf16[2,64,3072]{2,1,0:T(8,128)(2,1)S(1)}, bf16[2,64,3072]{2,1,0:T(8,128)(2,1)}, u32[]{:S(2)}, u32[]{:S(2)}) collective-permute-start(bf16[2,64,3072]{2,1,0:T(8,128)(2,1)S(1)} %pad_maximum_fusion.11.refs_1_), channel_id=1, source_target_pairs={{0,4},{4,0},{8,12},{12,8},{16,20},{20,16},{24,28},{28,24},{1,5},{5... | collective-permute-start | bytes 2359304 | tf_op jit(solution)/shard_map/ppermute | solution.py:70
  413.5 54.7 %collective-permute-start.63 = (bf16[2,64,3072]{2,1,0:T(8,128)(2,1)}, bf16[2,64,3072]{2,1,0:T(8,128)(2,1)}, u32[]{:S(2)}, u32[]{:S(2)}) collective-permute-start(bf16[2,64,3072]{2,1,0:T(8,128)(2,1)} %pad_maximum_fusion.10.refs_0_), channel_id=1, source_target_pairs={{0,1},{1,0},{2,3},{3,2},{4,5},{5,4},{6,7},{7,6},{8,9},{9,8},{10,11... | collective-permute-start | bytes 2359304 | tf_op jit(solution)/shard_map/ppermute | solution.py:72
  413.6 55.3 %collective-permute-start.64 = (bf16[2,64,3072]{2,1,0:T(8,128)(2,1)S(1)}, bf16[2,64,3072]{2,1,0:T(8,128)(2,1)}, u32[]{:S(2)}, u32[]{:S(2)}) collective-permute-start(bf16[2,64,3072]{2,1,0:T(8,128)(2,1)S(1)} %pad_maximum_fusion.11.refs_1_), channel_id=1, source_target_pairs={{0,1},{1,0},{2,3},{3,2},{4,5},{5,4},{6,7},{7,6},{8,9},{9,8},{10,11... | collective-permute-start | bytes 2359304 | tf_op jit(solution)/shard_map/ppermute | solution.py:72
  414.1 54.9 %collective-permute-start.65 = (bf16[2,64,3072]{2,1,0:T(8,128)(2,1)}, bf16[2,64,3072]{2,1,0:T(8,128)(2,1)}, u32[]{:S(2)}, u32[]{:S(2)}) collective-permute-start(bf16[2,64,3072]{2,1,0:T(8,128)(2,1)} %collective-permute-done.61.refs_2_), channel_id=1, source_target_pairs={{0,1},{1,0},{2,3},{3,2},{4,5},{5,4},{6,7},{7,6},{8,9},{9,8},{10,11... | collective-permute-start | bytes 2359304 | tf_op jit(solution)/shard_map/ppermute | solution.py:72
  420.1 49.2 %collective-permute-start.66 = (bf16[2,64,3072]{2,1,0:T(8,128)(2,1)}, bf16[2,64,3072]{2,1,0:T(8,128)(2,1)}, u32[]{:S(2)}, u32[]{:S(2)}) collective-permute-start(bf16[2,64,3072]{2,1,0:T(8,128)(2,1)} %collective-permute-done.62.refs_3_), channel_id=1, source_target_pairs={{0,1},{1,0},{2,3},{3,2},{4,5},{5,4},{6,7},{7,6},{8,9},{9,8},{10,11... | collective-permute-start | bytes 2359304 | tf_op jit(solution)/shard_map/ppermute | solution.py:72
  463.9 32.5 %collective-permute-start.56 = (bf16[512,3072]{1,0:T(8,128)(2,1)}, bf16[512,3072]{1,0:T(8,128)(2,1)}, u32[]{:S(2)}, u32[]{:S(2)}) collective-permute-start(bf16[512,3072]{1,0:T(8,128)(2,1)} %convolution_convert_fusion.1), channel_id=1, source_target_pairs={{0,1},{1,0},{2,3},{3,2},{4,5},{5,4},{6,7},{7,6},{8,9},{9,8},{10,11... | collective-permute-start | bytes 9437192 | tf_op jit(solution)/shard_map/ppermute | solution.py:72
  492.5 38.6 %collective-permute-start.77 = (bf16[2,128,1024]{2,1,0:T(8,128)(2,1)}, bf16[2,128,1024]{2,1,0:T(8,128)(2,1)}, u32[]{:S(2)}, u32[]{:S(2)}) collective-permute-start(bf16[2,128,1024]{2,1,0:T(8,128)(2,1)} %dynamic-slice_bitcast_fusion.2), channel_id=1, source_target_pairs={{0,8},{4,12},{8,0},{12,4},{16,24},{20,28},{24,16},{28,20},{1,9},{5... | collective-permute-start | bytes 1572872 | tf_op jit(solution)/shard_map/ppermute | solution.py:75
  494.5 31.3 %collective-permute-start.75 = (bf16[2,32,4096]{2,1,0:T(8,128)(2,1)}, bf16[2,32,4096]{2,1,0:T(8,128)(2,1)}, u32[]{:S(2)}, u32[]{:S(2)}) collective-permute-start(bf16[2,32,4096]{2,1,0:T(8,128)(2,1)} %dynamic-slice_bitcast_fusion.3), channel_id=1, source_target_pairs={{0,8},{4,12},{8,0},{12,4},{16,24},{20,28},{24,16},{28,20},{1,9},{5... | collective-permute-start | bytes 1572872 | tf_op jit(solution)/shard_map/ppermute | solution.py:75
  502.0 72.2 %all-to-all-start.6 = ((bf16[32,40,1024]{2,1,0:T(8,128)(2,1)}), bf16[32,40,1024]{2,1,0:T(8,128)(2,1)}, u32[]{:S(2)}, u32[]{:S(2)}) async-start(bf16[32,40,1024]{2,1,0:T(8,128)(2,1)} %bitcast.339), calls=%async_computation.6 | async-start | bytes 5242880 | tf_op jit(solution)/shard_map/all_to_all | solution.py:89
  506.2 39.8 %collective-permute-start.59 = (bf16[2,4,32,1536]{3,2,1,0:T(8,128)(2,1)S(1)}, bf16[2,4,32,1536]{3,2,1,0:T(8,128)(2,1)S(1)}, u32[]{:S(2)}, u32[]{:S(2)}) collective-permute-start(bf16[2,4,32,1536]{3,2,1,0:T(8,128)(2,1)S(1)} %dynamic-slice_bitcast_fusion), channel_id=1, source_target_pairs={{0,2},{1,3},{2,0},{3,1},{4,6},{5,7},{6,4},{7,5},{8,10},{9,11},{10,... | collective-permute-start | bytes 2359304 | tf_op jit(solution)/shard_map/ppermute | solution.py:72
  528.0 35.5 %collective-permute-start.57 = (bf16[2,4,32,1536]{3,2,1,0:T(8,128)(2,1)S(1)}, bf16[2,4,32,1536]{3,2,1,0:T(8,128)(2,1)S(1)}, u32[]{:S(2)}, u32[]{:S(2)}) collective-permute-start(bf16[2,4,32,1536]{3,2,1,0:T(8,128)(2,1)S(1)} %dynamic-slice_bitcast_fusion.1), channel_id=1, source_target_pairs={{0,4},{4,0},{8,12},{12,8},{16,20},{20,16},{24,28},{28,24},{1,5},{5... | collective-permute-start | bytes 2359304 | tf_op jit(solution)/shard_map/ppermute | solution.py:70
  596.2 28.0 %collective-permute-start.78 = (bf16[1,128,1024]{2,1,0:T(8,128)(2,1)}, bf16[1,128,1024]{2,1,0:T(8,128)(2,1)S(1)}, u32[]{:S(2)}, u32[]{:S(2)}) collective-permute-start(bf16[1,128,1024]{2,1,0:T(8,128)(2,1)} %dynamic-slice_convert_fusion), channel_id=1, source_target_pairs={{0,16},{4,20},{8,24},{12,28},{16,0},{20,4},{24,8},{28,12},{1,17},{... | collective-permute-start | bytes 786440 | tf_op jit(solution)/shard_map/ppermute | solution.py:75
  (151 other events, 2327.3 us)

commit v3 on v2

--- a/solution.py
+++ b/solution.py
@@ -88,10 +88,10 @@
     def to_all(self, values):
         return lax.all_to_all(values, ("wide", "narrow"), 0, 0, tiled=True)
 
-    def gather_early(self, shard):
+    def gather_early(self, shard, *before):
         near = shard[None]
         for step in self.bits()[:0:-1]:
-            near = jnp.concatenate([near, self.cross(near, step)])
+            near = jnp.concatenate([near, after(self.cross(near, step), *before)])
         return near
 
     def gather_late(self, near):
@@ -124,13 +124,14 @@
     def gather_plane(self, near):
         return self.plane_core(self.plane_second(*self.plane_first(near)))
 
-    def assemble(self, pieces, core_first=False):
+    def assemble(self, pieces, core_first=False, folded=None):
         depth = self.depth
         unused, unused_depth, rows, cut = pieces[0].shape
-        width = cut + pieces[2].shape[3]
+        count, fold = folded or (0, 0)
+        width = cut + pieces[2].shape[3] - count * fold
 
         def kernel(place, *refs):
-            sources, target = refs[:-1], refs[-1]
+            sources, target = refs[: len(pieces)], refs[len(pieces)]
             x, y, c = place[0], place[1], place[2]
             for number, source in enumerate(sources):
                 far_core, far, second = number // 4, number % 2, number // 2 % 2
@@ -142,6 +143,13 @@
                     to_y = 1 - y if across_y else y
                     if core_first:
                         target[to_c, to_x, to_y, 0, :, columns] = source[side, 0]
+                    elif second:
+                        target[0, to_x, to_y, to_c, :, columns] = source[side, 0, :, : width - cut]
+                        for number_in in range(count):
+                            start = width - cut + number_in * fold
+                            refs[-1][
+                                0, to_x, to_y, to_c, number_in * rows : (number_in + 1) * rows
+                            ] = source[side, 0, :, start : start + fold]
                     else:
                         target[0, to_x, to_y, to_c, :, columns] = source[side, 0]
 
@@ -157,9 +165,20 @@
             target_spec = pl.BlockSpec(
                 (1, 2, 2, 2, rows, width), lambda k, place: (place[3 + k], 0, 0, 0, 0, 0)
             )
-        whole = pl.pallas_call(
+        shapes, target_specs = [jax.ShapeDtypeStruct(shape, pieces[0].dtype)], [target_spec]
+        if count:
+            shapes.append(
+                jax.ShapeDtypeStruct((depth, 2, 2, 2, count * rows, fold), pieces[0].dtype)
+            )
+            target_specs.append(
+                pl.BlockSpec(
+                    (1, 2, 2, 2, count * rows, fold),
+                    lambda k, place: (place[3 + k], 0, 0, 0, 0, 0),
+                )
+            )
+        wholes = pl.pallas_call(
             kernel,
-            out_shape=jax.ShapeDtypeStruct(shape, pieces[0].dtype),
+            out_shape=shapes,
             grid_spec=pltpu.PrefetchScalarGridSpec(
                 num_scalar_prefetch=1,
                 grid=(depth,),
@@ -167,12 +186,29 @@
                     pl.BlockSpec((2, 1, rows, piece.shape[3]), lambda k, place: (0, k, 0, 0))
                     for piece in pieces
                 ],
-                out_specs=target_spec,
+                out_specs=target_specs,
             ),
-            compiler_params=pltpu.CompilerParams(vmem_limit_bytes=32 * 2**20),
+            compiler_params=pltpu.CompilerParams(vmem_limit_bytes=40 * 2**20),
             name="assemble",
         )(place, *pieces)
-        return whole.reshape(-1, width)
+        wholes = [whole.reshape(-1, whole.shape[-1]) for whole in wholes]
+        return wholes if count else wholes[0]
+
+    def exchange_plane(self, values):
+        for axis in "xyc":
+            dim = " xyc".index(axis) - 1
+            mine = lax.dynamic_index_in_dim(values, self.place[axis], dim, keepdims=False)
+            other = lax.dynamic_index_in_dim(values, 1 - self.place[axis], dim, keepdims=False)
+            values = jnp.stack([mine, self.swap(other, axis)], axis=dim)
+        return values.transpose(2, 0, 1, 3, 4).reshape(-1, values.shape[-1])
+
+    def share_direct(self, values):
+        pairs = []
+        for wide in range(self.wide):
+            for narrow in range(self.narrow):
+                pairs.append((wide * self.narrow + narrow, (wide ^ 1) * self.narrow + (narrow ^ 2)))
+        across = lax.ppermute(values, ("wide", "narrow"), pairs)
+        return [values, self.swap(values, "y"), self.swap(values, "x"), across]
 
     def share_first(self, values):
         cut = halves(values.shape[-1])
@@ -186,7 +222,7 @@
     def share_last(self, *pieces):
         return list(pieces) + [self.swap(piece, "c") for piece in pieces]
 
-    def scatter_plane(self, full):
+    def scatter_plane(self, full, *before_second):
         cut = halves(full.shape[-1])
         x, y = self.place["x"], self.place["y"]
 
@@ -198,6 +234,7 @@
         from_y = self.swap(pick(right, 1 - y, 1), "y")
         left = (pick(left, x, 0).astype(f32) + from_x.astype(f32)).astype(bf16)
         right = (pick(right, y, 1).astype(f32) + from_y.astype(f32)).astype(bf16)
+        left, right = after(left, *before_second), after(right, *before_second)
         from_y = self.swap(pick(left, 1 - y, 0), "y")
         from_x = self.swap(pick(right, 1 - x, 0), "x")
         left = pick(left, y, 0).astype(f32) + from_y.astype(f32)
@@ -339,57 +376,39 @@
     )(qkv_all, pick_rows, query_all, probs_all, grad_context)
 
 
-def plane_products(known, grads, place, depth, widths):
+def plane_products(known, grads, attn_grads, depth, widths):
     hidden, model = widths
-    rows = known[0].shape[-2]
+    rows = grads[0].shape[-2]
     width = hidden + 2 * model
     down_rows, model_rows = hidden // (8 * depth), model // (8 * depth)
-
-    def kernel(place_ref, *refs):
-        pieces, grad_pieces = refs[:8], refs[8:16]
-        down_ref, up_ref, out_ref, known_ref, grads_ref, own_ref = refs[16:]
-        for parts, target in ((pieces, known_ref), (grad_pieces, grads_ref)):
-            cut = parts[0].shape[-1]
-            for far_core in range(2):
-                left, right, left_y, right_x = parts[4 * far_core : 4 * far_core + 4]
-                for x in range(2):
-                    for y in range(2):
-                        spot = pl.ds(((far_core * 2 + x) * 2 + y) * rows, rows)
-                        target[spot, :cut] = (left_y if y else left)[x]
-                        target[spot, cut:] = (right_x if x else right)[y]
-        place = place_ref[0]
-
-        def own_columns(count, block_rows):
-            feature = lax.broadcasted_iota(jnp.int32, (count, depth * block_rows), 0)
-            own = lax.broadcasted_iota(jnp.int32, (count, depth * block_rows), 1)
-            block, offset = own // block_rows, own % block_rows
-            return jnp.where(
-                feature == (block * 8 + place) * block_rows + offset, 1.0, 0.0
-            ).astype(bf16)
-
-        if down_rows % 128 == 0:
-            for z in range(depth):
-                start = pl.multiple_of((z * 8 + place) * down_rows, down_rows)
-                own_ref[:, z * down_rows : (z + 1) * down_rows] = known_ref[
-                    :, pl.ds(start, down_rows)
-                ]
-        else:
-            own_ref[...] = matmul(known_ref[:, :hidden], own_columns(hidden, down_rows)).astype(
-                bf16
-            )
-        chosen = own_columns(model, model_rows)
-        down_ref[...] = contract_rows(own_ref[...], grads_ref[:, hidden : hidden + model]).astype(
-            bf16
-        )
-        own_normed = matmul(known_ref[:, hidden : hidden + model], chosen).astype(bf16)
-        up_ref[...] = contract_rows(own_normed, grads_ref[:, :hidden]).astype(bf16)
-        own_context = matmul(known_ref[:, hidden + model :], chosen).astype(bf16)
-        out_ref[...] = contract_rows(own_context, grads_ref[:, hidden + model :]).astype(bf16)
+    down_width, model_width = hidden // 8, model // 8
+
+    def kernel(known_ref, *refs):
+        down_ref, up_ref, out_ref, grads_ref = refs[10:]
+        cut = grads[0].shape[-1]
+        for far_core in range(2):
+            left, right, left_y, right_x = refs[4 * far_core : 4 * far_core + 4]
+            attn = refs[8 + far_core]
+            for x in range(2):
+                for y in range(2):
+                    spot = pl.ds(((far_core * 2 + x) * 2 + y) * rows, rows)
+                    grads_ref[spot, :cut] = (left_y if y else left)[x]
+                    grads_ref[spot, cut : hidden + model] = (right_x if x else right)[y]
+                    grads_ref[spot, hidden + model :] = attn[2 * x + y]
+        down_ref[...] = contract_rows(
+            known_ref[:, :down_width], grads_ref[:, hidden : hidden + model]
+        ).astype(bf16)
+        up_ref[...] = contract_rows(
+            known_ref[:, down_width : down_width + model_width], grads_ref[:, :hidden]
+        ).astype(bf16)
+        out_ref[...] = contract_rows(
+            known_ref[:, down_width + model_width :], grads_ref[:, hidden + model :]
+        ).astype(bf16)
 
     in_vmem = pl.BlockSpec(memory_space=pltpu.VMEM)
     down, up, out = pl.pallas_call(
         kernel,
-        in_specs=[pl.BlockSpec(memory_space=pltpu.SMEM)] + [in_vmem] * 16,
+        in_specs=[in_vmem] * 11,
         out_shape=(
             jax.ShapeDtypeStruct((depth * down_rows, model), bf16),
             jax.ShapeDtypeStruct((depth * model_rows, hidden), bf16),
@@ -397,12 +416,10 @@
         ),
         scratch_shapes=[
             pltpu.VMEM((8 * rows, width), bf16),
-            pltpu.VMEM((8 * rows, width), bf16),
-            pltpu.VMEM((8 * rows, depth * down_rows), bf16),
         ],
         compiler_params=pltpu.CompilerParams(vmem_limit_bytes=48 * 2**20),
         name="plane_products",
-    )(place.reshape(1).astype(jnp.int32), *known, *grads)
+    )(known, *grads, *attn_grads)
     return (
         down.reshape(depth, down_rows, model),
         up.reshape(depth, model_rows, hidden),
@@ -439,6 +456,40 @@
 
 
 grid_steps = 8
+
+
+def weight_squares(masters):
+    table_rows = -(-masters[0].shape[0] // (8 * grid_steps)) * 8
+    table_count = masters[0].shape[0]
+
+    def kernel(table_ref, *refs):
+        others, row_ref = refs[:-1], refs[-1]
+        step = pl.program_id(0)
+
+        @pl.when(step == 0)
+        def _():
+            row = jnp.zeros((1, 128), f32)
+            for place, other in enumerate(others):
+                row = row + on_lane(place + 1, whole_sum(other[...] * other[...]))
+            row_ref[...] = row
+
+        place = step * table_rows + lax.broadcasted_iota(jnp.int32, (table_rows, 1), 0)
+        square = jnp.where(place < table_count, table_ref[...] * table_ref[...], 0.0)
+        row_ref[...] += on_lane(0, whole_sum(square))
+
+    return pl.pallas_call(
+        kernel,
+        grid=(grid_steps,),
+        in_specs=[pl.BlockSpec((table_rows, masters[0].shape[1]), lambda k: (k, 0))]
+        + [
+            pl.BlockSpec(array.shape, lambda k: (0, 0), pipeline_mode=pl.Buffered(1))
+            for array in masters[1:]
+        ],
+        out_specs=pl.BlockSpec((1, 128), lambda k: (0, 0)),
+        out_shape=jax.ShapeDtypeStruct((1, 128), f32),
+        compiler_params=pltpu.CompilerParams(vmem_limit_bytes=32 * 2**20),
+        name="weight_squares",
+    )(*masters)
 
 
 def group_specs(arrays):
@@ -663,30 +714,37 @@
     gain_width = 128
     qkv_width = qkv_master.shape[1]
     gain_shard = jnp.pad(norm_master, ((0, 0), (0, gain_width - norm_master.shape[1])))
+    slot_first = slot_of(0)
+    masters = (tied_table_master, qkv_master, out_master, up_master, down_master, norm_master)
     first_shard = jnp.concatenate([qkv_master, gain_shard], axis=1).astype(bf16)
     first_early = links.gather_early(first_shard)
     first_near = links.gather_late(first_early)
-    slot_first = slot_of(0)
-    masters = (tied_table_master, qkv_master, out_master, up_master, down_master, norm_master)
     message = message_of(slot_first)
     answer = links.to_all(message)
-    second_shard = jnp.concatenate([up_master, out_master], axis=1)
-    second_near = links.gather_early(after(second_shard, first_early).astype(bf16))
-    down_near = links.gather_early(after(down_master, first_early).astype(bf16))
     table_low = after(tied_table_master, message).astype(bf16)
     asked_first = answer[:, :slots].reshape(-1)
-    found = after(find(asked_first), first_near, second_near, down_near)
-    landed = links.to_all(found)
     rounds = (jnp.max(answer[:, slots]) + slots - 1) // slots
     targets = answer[:, slots + 1 : slots + 1 + pick_total]
     targets = targets.reshape(links.depth, 2, 2, 2, pick_total).transpose(3, 1, 2, 0, 4).reshape(-1)
-    first_whole = links.assemble(links.gather_plane(first_near))
-    second_near = links.gather_late(second_near)
-    second_parts = links.plane_first(after(second_near, first_whole))
-    weight_row = sum(
-        on_lane(place, after(jnp.sum(weight * weight), found))
-        for place, weight in enumerate(masters)
-    )
+    fold_count = down_master.shape[0] // shard_rows
+    second_shard = jnp.concatenate(
+        [up_master, out_master]
+        + [
+            down_master[number * shard_rows : (number + 1) * shard_rows]
+            for number in range(fold_count)
+        ],
+        axis=1,
+    )
+    second_near = links.gather_early(after(second_shard, first_early).astype(bf16))
+    first_parts = links.plane_first(first_near)
+    found = after(find(asked_first), first_near)
+    landed = links.to_all(found)
+    first_pieces = links.plane_second(*first_parts)
+    weight_row = weight_squares(tie(*masters, found)[:6])
+    first_pieces[0] = after(first_pieces[0], weight_row)
+    first_whole = links.assemble(links.plane_core(first_pieces))
+    second_near = links.gather_late(after(second_near, *first_parts))
+    second_parts = links.plane_first(after(second_near, *first_pieces))
     qkv_weight = first_whole[:, :qkv_width]
     gain_entries = first_whole[:, qkv_width : qkv_width + 6].astype(f32).T
 
@@ -703,8 +761,7 @@
 
     x_embed = x_low.astype(f32)
     normed_one = layer_norm(x_embed, gain_entries[0], gain_entries[1]).astype(bf16)
-    second_pieces = links.plane_second(*second_parts)
-    down_parts = links.plane_first(links.gather_late(after(down_near, normed_one)))
+    normed_one = after(normed_one, *second_parts)
     qkv_all = matmul(normed_one, qkv_weight).astype(bf16)
     pick_rows = (
         pick_hits[:, :, None, :] & jnp.eye(micro_count, dtype=bool)[:, None, :, None]
@@ -716,13 +773,13 @@
     context, queries, probs = attend(
         qkv_all, pick_rows, allowed.reshape(pick_total, length).astype(f32), micro_count
     )
-    second_whole = links.assemble(
-        links.plane_core([after(piece, context) for piece in second_pieces])
+    second_pieces = links.plane_second(*second_parts)
+    second_whole, down_weight = links.assemble(
+        links.plane_core([after(piece, context) for piece in second_pieces]),
+        folded=(fold_count, model_width),
     )
     hidden = up_master.shape[1]
     up_weight, out_weight = second_whole[:, :hidden], second_whole[:, hidden:]
-    down_pieces = links.plane_second(*[after(part, context) for part in down_parts])
-    down_weight = links.assemble(links.plane_core(down_pieces))
     x_attn = x_embed_picked + matmul(context, out_weight)
     normed_two = layer_norm(x_attn, gain_entries[2], gain_entries[3]).astype(bf16)
     up_value = matmul(normed_two, up_weight)
@@ -730,8 +787,9 @@
     x_out = x_attn + matmul(activated, down_weight)
     picked_low = layer_norm(x_out, gain_entries[4], gain_entries[5]).astype(bf16)
 
+    head_pieces = links.plane_second(*links.plane_first(links.gather_depth(picked_low)))
     head_rows = links.assemble(
-        links.gather_plane(links.gather_depth(picked_low)), core_first=True
+        links.plane_core(head_pieces), core_first=True
     )
     columns = links.device * block_size + jnp.arange(block_size)
     logits = contract_cols(head_rows, table_low)
@@ -746,16 +804,34 @@
         total = first[1] * jnp.exp(first[0] - top) + second[1] * jnp.exp(second[0] - top)
         return jnp.stack([top, total])
 
-    known = jnp.concatenate([activated, normed_two, context], axis=1)
-    known, head_rows = tie(known, head_rows)
-    known_parts = links.share_first(known)
-    local_sum, *known_parts = tie(local_sum, *known_parts)
-    known_parts = links.share_second(*known_parts)
     merged = links.exchange(jnp.stack([local_top, local_sum]), merge_totals)
+    def by_owner(values, block_rows):
+        if block_rows % 128 == 0:
+            blocks = values.reshape(pick_total, links.depth, 8, block_rows)
+            blocks = blocks.transpose(2, 0, 1, 3).reshape(8 * pick_total, -1)
+            return blocks.reshape(8, pick_total, -1)
+        count = values.shape[1]
+        place = jnp.arange(count)
+        source = place % (count // 8) // block_rows * 8 + place // (count // 8)
+        source = source * block_rows + place % block_rows
+        order = (jnp.arange(count)[:, None] == source[None, :]).astype(bf16)
+        ordered = matmul(values, order).astype(bf16)
+        return ordered.reshape(pick_total, 8, count // 8).transpose(1, 0, 2)
+
+    known = jnp.concatenate(
+        [
+            by_owner(activated, down_master.shape[0]),
+            by_owner(normed_two, shard_rows),
+            by_owner(context, shard_rows),
+        ],
+        axis=2,
+    )
+    known = known.reshape(2, 2, 2, pick_total, -1)
     log_total = merged[0] + jnp.log(merged[1])
     grad_logits = (
         (jnp.exp(logits - log_total[:, None]) - target_hits.astype(f32)) / count_all
     ).astype(bf16)
+
     half_rows = head_rows.shape[0] // 2
     core = links.place["c"]
 
@@ -769,11 +845,10 @@
     grad_near = links.scatter_plane(
         (picked_part(core) + from_core.astype(f32))
         .astype(bf16)
-        .reshape(2, 2, links.depth, pick_total, model_width)
-    )
-    grad_near, grad_logits = tie(grad_near, grad_logits)
-    table_head = contract_rows(grad_logits, head_rows)
-    known = links.share_last(*[after(part, grad_near) for part in known_parts])
+        .reshape(2, 2, links.depth, pick_total, model_width),
+        known,
+    )
+    known = links.exchange_plane(after(known, grad_near))
     grad_picked = links.scatter_depth(grad_near)
 
     grad_x_out, gain_last, shift_last = norm_backward(
@@ -782,20 +857,20 @@
     grad_mlp = grad_x_out.astype(bf16)
     unused, gelu_pull = jax.vjp(gelu_tanh, up_value)
     grad_up_low = gelu_pull(contract_cols(grad_mlp, down_weight))[0].astype(bf16)
+    grad_parts = links.share_first(jnp.concatenate([grad_up_low, grad_mlp], axis=1))
     grad_x_attn, gain_two, shift_two = norm_backward(
         x_attn, gain_entries[2], gain_entries[3], contract_cols(grad_up_low, up_weight)
     )
     grad_x_attn = grad_x_out + grad_x_attn
+    grad_x_attn = after(grad_x_attn, *grad_parts)
     grad_attn_low = grad_x_attn.astype(bf16)
     grad_context = contract_cols(grad_attn_low, out_weight).astype(bf16)
-    grad_parts = links.share_first(
-        jnp.concatenate([grad_up_low, grad_mlp, grad_attn_low], axis=1)
-    )
+    attn_parts = links.share_direct(grad_attn_low)
+    grad_parts = links.share_second(*grad_parts)
     grad_qkv_low = attend_backward(
         qkv_all, pick_rows, queries, probs, grad_context, micro_count
     )
-    late = after(grad_qkv_low, *grad_parts)
-    grad_parts = links.share_second(*grad_parts)
+    late = grad_qkv_low
     grad_x_one, gain_one, shift_one = norm_backward(
         x_embed, gain_entries[0], gain_entries[1], contract_cols(late, qkv_weight)
     )
@@ -808,16 +883,9 @@
     )
     grad_embed_low = grad_x_embed.astype(bf16)
     sent = give(slot_first, grad_embed_low)
-    grad_qkv_low = after(grad_qkv_low, sent)
+    grad_qkv_low = after(grad_qkv_low, sent, known, *grad_parts, *attn_parts)
     returned = links.to_all(sent)
-    down_near, up_near, out_near = plane_products(
-        known,
-        links.share_last(*[after(part, sent) for part in grad_parts]),
-        (links.place["x"] * 2 + links.place["y"]) * 2 + core,
-        links.depth,
-        (activated.shape[1], model_width),
-    )
-
+    table_head = contract_rows(after(grad_logits, returned), head_rows)
     half_place = jnp.arange(model_width // 2)
     half_row = half_place % shard_rows
     half_z = half_place // shard_rows % links.depth
@@ -830,16 +898,24 @@
 
     to_core = qkv_part(1 - core).astype(bf16)
     from_core = links.swap(to_core, "c")
+    last_mine = (qkv_part(core) + from_core.astype(f32)).astype(bf16)
     last_near = links.scatter_plane(
-        (qkv_part(core) + from_core.astype(f32))
-        .astype(bf16)
-        .reshape(2, 2, links.depth, shard_rows, qkv_width)
-    )
+        last_mine.reshape(2, 2, links.depth, shard_rows, qkv_width), returned
+    )
+    down_near, up_near, out_near = plane_products(
+        known,
+        links.share_last(*[after(part, last_mine) for part in grad_parts]),
+        links.share_last(after(jnp.stack(attn_parts), last_mine)),
+        links.depth,
+        (activated.shape[1], model_width),
+    )
+
     last_near = jnp.concatenate([last_near, out_near], axis=-1)
     down_grad = links.scatter_depth(down_near, returned)
     up_grad = links.scatter_depth(up_near, returned)
-    last_grad = links.scatter_depth(after(last_near, returned))
+    last_grad = links.scatter_depth(last_near)
     qkv_grad, out_grad = last_grad[:, :qkv_width], last_grad[:, qkv_width:]
+    gain_one = after(gain_one, returned)
     gain_grads = jnp.stack(
         [gain_one, shift_one, gain_two, shift_two, gain_last, shift_last]
     ).reshape(6, devices, shard_rows)

time: 710 us -> 674 us (0.949)
  waiting for transfers between devices: 317 us -> 270 us
  matrix products: 98.1 us -> 117 us
  starting transfers between devices: 88.7 us -> 72.5 us
  loops' own time: 11.5 us -> 0.35 us
  local copies, waits for them, and re-layouts: 42.2 us -> 51.8 us
  Pallas kernels: 65.7 us -> 74.3 us
    ppermute x42 -> x34, waiting for transfers between devices: 102 us -> 56.9 us  [swap(): lax.ppermute(values, 'narrow', [(i, i ^ step) for i in range(self.narrow)])]
    dot_general x10 -> x12, matrix products: 45.2 us -> 57 us  [matmul(): return jnp.dot(left_side, right_side, preferred_element_type=f32)]
    another operation x1, loops' own time: 11.5 us -> 0.16 us  [per_device(): lax.while_loop(lambda state: state[0] < rounds, more_rows, (jnp.ones((),...]
    dot_general x5, matrix products: 21.3 us -> 30.7 us  [contract_cols(): lax.dot_general(left_side, right_side, (((1,), (1,)), ((), ())), preferre...]
    all_to_all x6, waiting for transfers between devices: 10.5 us -> 19.5 us  [to_all(): return lax.all_to_all(values, ('wide', 'narrow'), 0, 0, tiled=True)]
    pallas_call x5, Pallas kernels: 17.5 us -> 26.2 us  [the longest x3 20.3 us: assemble(): pl.pallas_call(kernel, out_shape=shapes, grid_spec=pltpu.PrefetchScalarGr...]
    reduce_sum x6 -> x0, other arithmetic: 7.7 us -> none  [per_device(): jnp.sum(weight * weight)]
    ppermute x16 -> x14, waiting for transfers between devices: 90.3 us -> 83.3 us  [swap(): return lax.ppermute(values, 'wide', [(i, i ^ 1) for i in range(self.wide)])]
  transfers between devices with their start and end apart: 85 -> 74, of which waited for: 44 -> 41; matrix products, arithmetic and copies ran while one was open for 22% -> 20% of each run, Pallas kernels for 3% -> 3%
where the time goes in v3:
time: 674 us; the launch traced here: 664 us
  waiting for transfers between devices  270 us (40%)
  matrix products  117 us (17%)
  Pallas kernels  74.3 us (11%)
  starting transfers between devices  72.5 us (11%)
  other arithmetic  70.7 us (10%)
  local copies, waits for them, and re-layouts  51.8 us (8%)
  between operations  6.74 us (1%)
    ppermute x14, waiting for transfers between devices, cross(): lax.ppermute(values, 'wide', [(i, i ^ 2 * step) for i in range(self.wide)])  96.5 us
    ppermute x14, waiting for transfers between devices, swap(): return lax.ppermute(values, 'wide', [(i, i ^ 1) for i in range(self.wide)])  83.3 us
    dot_general x12, matrix products, matmul(): return jnp.dot(left_side, right_side, preferred_element_type=f32)  57 us
    ppermute x34, waiting for transfers between devices, swap(): lax.ppermute(values, 'narrow', [(i, i ^ step) for i in range(self.narrow)])  56.9 us
    dot_general x5, matrix products, contract_cols(): lax.dot_general(left_side, right_side, (((1,), (1,)), ((), ())), preferre...  30.7 us
    dot_general x4, matrix products, contract_rows(): lax.dot_general(left_side, right_side, (((0,), (0,)), ((), ())), preferre...  28.3 us
    pallas_call x1, Pallas kernels, lamb_directions(): pl.pallas_call(kernel, grid=(grid_steps,), in_specs=[pl.BlockSpec(totals....  23.1 us
    all_to_all x6, starting transfers between devices, to_all(): return lax.all_to_all(values, ('wide', 'narrow'), 0, 0, tiled=True)  22.6 us
  transfers between devices with their start and end apart: 74, of which 41 were waited for; matrix products, arithmetic and copies ran while one was open for 20% of the time, Pallas kernels for 3%

profile of v3, /device:TPU:0, one launch (start us, length us, event | category | flops | bytes accessed | tf_op | source)
XLA Modules:
  0.0 663.9 jit_solution(4605870770772485943)
XLA Ops:
  34.4 25.8 %collective-permute-done.10 = bf16[1,32,9216]{2,1,0:T(8,128)(2,1)S(1)} collective-permute-done((bf16[1,32,9216]{2,1,0:T(8,128)(2,1)S(1)}, bf16[1,32,9216]{2,1,0:T(8,128)(2,1)S(1)}, u32[]{:S(2)}, u32[]{:S(2)}) %collective-permute-start.10) | collective-permute-done | bytes 589856 | tf_op jit(solution)/shard_map/ppermute | solution.py:75
  62.8 8.3 %fusion.36 = bf16[1280,1024]{1,0:T(8,128)(2,1)} fusion(bf16[1572,1024]{1,0:T(8,128)(2,1)} %convert_element_type.294, s32[1280]{0:T(1024)S(1)} %eq.383), kind=kOutput, calls=%fused_computation.62 | convolution fusion | flops 4124226560 | bytes 5846016 | tf_op jit(solution)/shard_map/dot_general | solution.py:42
  86.9 16.8 %collective-permute-done.11 = bf16[2,32,9216]{2,1,0:T(8,128)(2,1)} collective-permute-done((bf16[2,32,9216]{2,1,0:T(8,128)(2,1)}, bf16[2,32,9216]{2,1,0:T(8,128)(2,1)}, u32[]{:S(2)}, u32[]{:S(2)}) %collective-permute-start.11) | collective-permute-done | bytes 1179680 | tf_op jit(solution)/shard_map/ppermute | solution.py:75
  119.8 25.7 %collective-permute-done.13 = bf16[4,32,4608]{2,1,0:T(8,128)(2,1)} collective-permute-done((bf16[4,32,4608]{2,1,0:T(8,128)(2,1)}, bf16[4,32,4608]{2,1,0:T(8,128)(2,1)}, u32[]{:S(2)}, u32[]{:S(2)}) %collective-permute-start.13) | collective-permute-done | bytes 1179680 | tf_op jit(solution)/shard_map/ppermute | solution.py:72
  160.3 6.8 %fusion.29.qkv_ref = bf16[512,3072]{1,0:T(8,128)(2,1)S(1)} fusion(bf16[512,1024]{1,0:T(8,128)(2,1)S(1)} %fusion.49, bf16[1024,3200]{1,0:T(8,128)(2,1)} %bitcast.337), kind=kOutput, calls=%fused_computation.52 | convolution fusion | flops 3222798336 | bytes 10485760 | tf_op jit(solution)/shard_map/dot_general | solution.py:42
  173.2 26.3 %collective-permute-done.15.refs_3_ = bf16[2,4,32,4608]{3,2,1,0:T(8,128)(2,1)} collective-permute-done((bf16[2,4,32,4608]{3,2,1,0:T(8,128)(2,1)}, bf16[2,4,32,4608]{3,2,1,0:T(8,128)(2,1)}, u32[]{:S(2)}, u32[]{:S(2)}) %collective-permute-start.15) | collective-permute-done | bytes 2359328 | tf_op jit(solution)/shard_map/ppermute | solution.py:70
  207.6 12.5 %assemble.4 = (bf16[4,2,2,2,32,5120]{5,4,3,2,1,0:T(8,128)(2,1)}, bf16[4,2,2,2,128,1024]{5,4,3,2,1,0:T(8,128)(2,1)}) custom-call(s32[7]{0:T(128)S(1)} %stack.205.place, bf16[2,4,32,4608]{3,2,1,0:T(8,128)(2,1)} %pad_maximum_fusion.1.refs_0_, bf16[2,4,32,4608]{3,2,1,0:T(8,128)(2,1)} %collective-permute-done.14.refs_1_, ...), custom_call_target="tpu_custom_call" | custom-call | tf_op jit(solution)/shard_map/assemble/pallas_call | solution.py:179
  230.4 9.2 %collective-permute-done.20 = bf16[1,64,1024]{2,1,0:T(8,128)(2,1)S(1)} collective-permute-done((bf16[1,64,1024]{2,1,0:T(8,128)(2,1)S(1)}, bf16[1,64,1024]{2,1,0:T(8,128)(2,1)S(1)}, u32[]{:S(2)}, u32[]{:S(2)}) %collective-permute-start.20) | collective-permute-done | bytes 131104 | tf_op jit(solution)/shard_map/ppermute | solution.py:75
  239.8 7.8 %collective-permute-done.21 = bf16[2,64,1024]{2,1,0:T(8,128)(2,1)S(1)} collective-permute-done((bf16[2,64,1024]{2,1,0:T(8,128)(2,1)S(1)}, bf16[2,64,1024]{2,1,0:T(8,128)(2,1)S(1)}, u32[]{:S(2)}, u32[]{:S(2)}) %collective-permute-start.21) | collective-permute-done | bytes 262176 | tf_op jit(solution)/shard_map/ppermute | solution.py:75
  258.9 8.9 %collective-permute-done.25.refs_3_ = bf16[2,4,64,512]{3,2,1,0:T(8,128)(2,1)} collective-permute-done((bf16[2,4,64,512]{3,2,1,0:T(8,128)(2,1)}, bf16[2,4,64,512]{3,2,1,0:T(8,128)(2,1)}, u32[]{:S(2)}, u32[]{:S(2)}) %collective-permute-start.25) | collective-permute-done | bytes 524320 | tf_op jit(solution)/shard_map/ppermute | solution.py:70
  276.7 10.4 %select_reduce_fusion.2 = (f32[2048]{0:T(1024)S(1)}, f32[2048,1572]{0,1:T(8,128)S(1)}) fusion(pred[1572]{0:T(1024)(128)(4,1)S(1)} %broadcast_compare_fusion, bf16[2048,1024]{1,0:T(8,128)(2,1)S(1)} %bitcast.341, bf16[1572,1024]{1,0:T(8,128)(2,1)} %convert_element_type.294), kind=kOutput, calls=%fused_computation.37 | convolution fusion | flops 6599882752 | bytes 20301348 | tf_op jit(solution)/shard_map/dot_general | solution.py:52
  312.2 7.1 %fusion.17 = bf16[2048,1572]{0,1:T(8,128)(2,1)S(1)} fusion(f32[2048,1572]{0,1:T(8,128)} %copy-done.23, s32[2048]{0:T(1024)S(1)} %eq.396, f32[2048]{0:T(1024)S(1)} %get-tuple-element.694, s32[1572]{0:T(1024)S(1)} %iota_add_fusion, pred[1572]{0:T(1024)(128)(4,1)S(1)} %broadcast_compare_fusion), kind=kLoop, calls=%fused_computation.34 | loop fusion | flops 22536192 | bytes 19340980 | tf_op jit(solution)/shard_map/convert_element_type | solution.py:833
  319.4 9.7 %fusion.57 = bf16[1024,1024]{1,0:T(8,128)(2,1)} fusion(bf16[1572,1024]{1,0:T(8,128)(2,1)} %convert_element_type.294, bf16[2048,1572]{0,1:T(8,128)(2,1)S(1)} %fusion.17, s32[]{:T(128)S(6)} %select_n.349), kind=kOutput, calls=%fused_computation.95 | convolution fusion | flops 3297771520 | bytes 8544260 | tf_op jit(solution)/shard_map/dot_general | solution.py:42
  333.6 7.5 %add_convert_fusion.1 = bf16[1024,1024]{1,0:T(8,128)(2,1)S(1)} fusion(bf16[1024,1024]{1,0:T(8,128)(2,1)} %collective-permute-done.35, bf16[1572,1024]{1,0:T(8,128)(2,1)} %convert_element_type.294, bf16[2048,1572]{0,1:T(8,128)(2,1)} %copy-done.29, s32[]{:T(128)S(6)} %select_n.350), kind=kOutput, calls=%fused_computation.58 | convolution fusion | flops 3299868672 | bytes 10649604 | tf_op jit(solution)/shard_map/dot_general | solution.py:42
  403.5 7.2 %multiply_reduce_fusion.1 = (f32[1024]{0:T(1024)}, f32[64]{0:T(128)S(1)}, f32[1024]{0:T(1024)}, f32[64,1024]{1,0:T(8,128)S(1)}) fusion(f32[64,1024]{1,0:T(8,128)S(1)} %copy-done.32, f32[64]{0:T(128)S(1)} %copy-done.97, f32[64]{0:T(128)S(1)} %copy-done.92, f32[1024]{0:T(1024)S(1)} %bitcast.428, bf16[64,4096]{1,0:T(8,128)(2,1)S(1)} %fusion.89, ...), kind=kOutput, calls=%fused_computation.208 | convolution fusion | flops 537393088 | bytes 9450240 | tf_op jit(solution)/shard_map/dot_general | solution.py:52
  413.0 6.8 %collective-permute-done.42 = bf16[64,2560]{1,0:T(8,128)(2,1)S(1)} collective-permute-done((bf16[64,2560]{1,0:T(8,128)(2,1)S(1)}, bf16[64,2560]{1,0:T(8,128)(2,1)S(1)}, u32[]{:S(2)}, u32[]{:S(2)}) %collective-permute-start.42) | collective-permute-done | bytes 327712 | tf_op jit(solution)/shard_map/ppermute | solution.py:70
  490.5 18.2 %collective-permute-done.53 = bf16[2,4,32,1536]{3,2,1,0:T(8,128)(2,1)S(1)} collective-permute-done((bf16[2,4,32,1536]{3,2,1,0:T(8,128)(2,1)S(1)}, bf16[2,4,32,1536]{3,2,1,0:T(8,128)(2,1)S(1)}, u32[]{:S(2)}, u32[]{:S(2)}) %collective-permute-start.53) | collective-permute-done | bytes 786464 | tf_op jit(solution)/shard_map/ppermute | solution.py:70
  516.8 12.6 %collective-permute-done.64 = bf16[2,32,4096]{2,1,0:T(8,128)(2,1)S(1)} collective-permute-done((bf16[2,32,4096]{2,1,0:T(8,128)(2,1)S(1)}, bf16[2,32,4096]{2,1,0:T(8,128)(2,1)S(1)}, u32[]{:S(2)}, u32[]{:S(2)}) %collective-permute-start.64) | collective-permute-done | bytes 524320 | tf_op jit(solution)/shard_map/ppermute | solution.py:75
  529.5 8.3 %fusion.20 = f32[1572,1024]{1,0:T(8,128)} fusion(bf16[1280,1024]{1,0:T(8,128)(2,1)} %bitcast.76, s32[1280]{0:T(1024)S(1)} %copy-done.78), kind=kOutput, calls=%fused_computation.41 | convolution fusion | flops 4122915840 | bytes 9065472 | tf_op jit(solution)/shard_map/dot_general | solution.py:42
  548.0 13.3 %convolution_add_fusion = f32[1572,1024]{1,0:T(8,128)} fusion(f32[1572,1024]{1,0:T(8,128)} %fusion.20, bf16[2048,1572]{0,1:T(8,128)(2,1)} %copy-done.29, bf16[2048,1024]{1,0:T(8,128)(2,1)} %bitcast.342), kind=kOutput, calls=%fused_computation.59 | convolution fusion | flops 6595055616 | bytes 23511040 | tf_op jit(solution)/shard_map/dot_general | solution.py:46
  572.7 6.7 %all-to-all-done.7 = f32[32,1,256]{2,1,0:T(1,128)S(1)} async-done(((f32[32,1,256]{2,1,0:T(1,128)}), f32[32,1,256]{2,1,0:T(1,128)S(1)}, u32[]{:S(2)}, u32[]{:S(2)}) %all-to-all-start.7) | async-done | bytes 32800 | tf_op jit(solution)/shard_map/all_to_all | solution.py:89
  585.2 11.0 %collective-permute-done.63 = bf16[1,32,4096]{2,1,0:T(8,128)(2,1)S(1)} collective-permute-done((bf16[1,32,4096]{2,1,0:T(8,128)(2,1)S(1)}, bf16[1,32,4096]{2,1,0:T(8,128)(2,1)S(1)}, u32[]{:S(2)}, u32[]{:S(2)}) %collective-permute-start.63) | collective-permute-done | bytes 262176 | tf_op jit(solution)/shard_map/ppermute | solution.py:75
  613.0 23.1 %lamb_directions.1 = (f32[1572,1024]{1,0:T(8,128)}, f32[32,3072]{1,0:T(8,128)}, f32[32,1024]{1,0:T(8,128)}, f32[32,4096]{1,0:T(8,128)}, f32[128,1024]{1,0:T(8,12...) custom-call(f32[32,256]{1,0:T(8,128)} %bitcast.387, ...), custom_call_target="tpu_custom_call" | custom-call | tf_op jit(solution)/shard_map/lamb_directions/pallas_call | solution.py:560
  646.4 11.0 %lamb_weights.1 = (f32[1572,1024]{1,0:T(8,128)}, f32[32,3072]{1,0:T(8,128)}, f32[32,1024]{1,0:T(8,128)}, f32[32,4096]{1,0:T(8,128)}, f32[128,1024]{1,0:T(8,128)}, /*index=5*/f32[32,6]{1,0:T(8,128)}, f32[8,128]{1,0:T(8,128)}) custom-call(f32[32,256]{1,0:T(8,128)} %bitcast.388, f32[32,128]{1,0:T(8,128)} %bitcast.406, f32[1572,1024]{1,0:T(8,128)} %get-tuple-element.398.refs_0_, ...), custom_call_target="tpu_custom_call" | custom-call | tf_op jit(solution)/shard_map/lamb_weights/pallas_call | solution.py:602
  (563 shorter events, 355.8 us)
Async XLA Ops:
  31.6 28.6 %collective-permute-start.10 = (bf16[1,32,9216]{2,1,0:T(8,128)(2,1)S(1)}, bf16[1,32,9216]{2,1,0:T(8,128)(2,1)S(1)}, u32[]{:S(2)}, u32[]{:S(2)}) collective-permute-start(bf16[1,32,9216]{2,1,0:T(8,128)(2,1)S(1)} %bitcast.357), channel_id=1, source_target_pairs={{0,16},{4,20},{8,24},{12,28},{16,0},{20,4},{24,8},{28,12},{1,17},{... | collective-permute-start | bytes 1769480 | tf_op jit(solution)/shard_map/ppermute | solution.py:75
  32.4 28.9 %collective-permute-start.2 = (bf16[4,32,1536]{2,1,0:T(8,128)(2,1)S(1)}, bf16[4,32,1536]{2,1,0:T(8,128)(2,1)S(1)}, u32[]{:S(2)}, u32[]{:S(2)}) collective-permute-start(bf16[4,32,1536]{2,1,0:T(8,128)(2,1)S(1)} %get-tuple-element.714), channel_id=1, source_target_pairs={{0,4},{4,0},{8,12},{12,8},{16,20},{20,16},{24,28},{28,24},{1,5},{5... | collective-permute-start | bytes 1179656 | tf_op jit(solution)/shard_map/ppermute | solution.py:70
  33.1 29.0 %collective-permute-start.4 = (bf16[4,32,1664]{2,1,0:T(8,128)(2,1)S(1)}, bf16[4,32,1664]{2,1,0:T(8,128)(2,1)S(1)}, u32[]{:S(2)}, u32[]{:S(2)}) collective-permute-start(bf16[4,32,1664]{2,1,0:T(8,128)(2,1)S(1)} %get-tuple-element.712), channel_id=1, source_target_pairs={{0,2},{1,3},{2,0},{3,1},{4,6},{5,7},{6,4},{7,5},{8,10},{9,11},{10,... | collective-permute-start | bytes 1277960 | tf_op jit(solution)/shard_map/ppermute | solution.py:72
  62.1 41.6 %collective-permute-start.11 = (bf16[2,32,9216]{2,1,0:T(8,128)(2,1)}, bf16[2,32,9216]{2,1,0:T(8,128)(2,1)}, u32[]{:S(2)}, u32[]{:S(2)}) collective-permute-start(bf16[2,32,9216]{2,1,0:T(8,128)(2,1)} %pad_maximum_fusion.3), channel_id=1, source_target_pairs={{0,8},{4,12},{8,0},{12,4},{16,24},{20,28},{24,16},{28,20},{1,9},{5... | collective-permute-start | bytes 3538952 | tf_op jit(solution)/shard_map/ppermute | solution.py:75
  62.2 24.7 %collective-permute-start.5 = (bf16[2,4,32,1664]{3,2,1,0:T(8,128)(2,1)S(1)}, bf16[2,4,32,1664]{3,2,1,0:T(8,128)(2,1)}, u32[]{:S(2)}, u32[]{:S(2)}) collective-permute-start(bf16[2,4,32,1664]{3,2,1,0:T(8,128)(2,1)S(1)} %pad_maximum_fusion.5.refs_2_), channel_id=1, source_target_pairs={{0,4},{4,0},{8,12},{12,8},{16,20},{20,16},{24,28},{28,24},{1,5},{5... | collective-permute-start | bytes 2555912 | tf_op jit(solution)/shard_map/ppermute | solution.py:70
  71.1 81.0 %all-to-all-start.5 = ((bf16[32,40,1024]{2,1,0:T(8,128)(2,1)}), bf16[32,40,1024]{2,1,0:T(8,128)(2,1)}, u32[]{:S(2)}, u32[]{:S(2)}) async-start(bf16[32,40,1024]{2,1,0:T(8,128)(2,1)} %bitcast.351), calls=%async_computation.5 | async-start | bytes 5242880 | tf_op jit(solution)/shard_map/all_to_all | solution.py:89
  80.3 31.5 %collective-permute-start.6 = (bf16[2,4,32,1536]{3,2,1,0:T(8,128)(2,1)S(1)}, bf16[2,4,32,1536]{3,2,1,0:T(8,128)(2,1)}, u32[]{:S(2)}, u32[]{:S(2)}) collective-permute-start(bf16[2,4,32,1536]{3,2,1,0:T(8,128)(2,1)S(1)} %pad_maximum_fusion.7.refs_0_), channel_id=1, source_target_pairs={{0,1},{1,0},{2,3},{3,2},{4,5},{5,4},{6,7},{7,6},{8,9},{9,8},{10,11... | collective-permute-start | bytes 2359304 | tf_op jit(solution)/shard_map/ppermute | solution.py:72
  80.5 32.8 %collective-permute-start.8 = (bf16[2,4,32,1664]{3,2,1,0:T(8,128)(2,1)S(1)}, bf16[2,4,32,1664]{3,2,1,0:T(8,128)(2,1)S(1)}, u32[]{:S(2)}, u32[]{:S(2)}) collective-permute-start(bf16[2,4,32,1664]{3,2,1,0:T(8,128)(2,1)S(1)} %pad_maximum_fusion.5.refs_2_), channel_id=1, source_target_pairs={{0,1},{1,0},{2,3},{3,2},{4,5},{5,4},{6,7},{7,6},{8,9},{9,8},{10,11... | collective-permute-start | bytes 2555912 | tf_op jit(solution)/shard_map/ppermute | solution.py:72
  82.3 31.0 %collective-permute-start.7 = (bf16[2,4,32,1536]{3,2,1,0:T(8,128)(2,1)}, bf16[2,4,32,1536]{3,2,1,0:T(8,128)(2,1)}, u32[]{:S(2)}, u32[]{:S(2)}) collective-permute-start(bf16[2,4,32,1536]{3,2,1,0:T(8,128)(2,1)} %collective-permute-done.3.refs_1_), channel_id=1, source_target_pairs={{0,1},{1,0},{2,3},{3,2},{4,5},{5,4},{6,7},{7,6},{8,9},{9,8},{10,11... | collective-permute-start | bytes 2359304 | tf_op jit(solution)/shard_map/ppermute | solution.py:72
  86.8 26.5 %collective-permute-start.9 = (bf16[2,4,32,1664]{3,2,1,0:T(8,128)(2,1)}, bf16[2,4,32,1664]{3,2,1,0:T(8,128)(2,1)S(1)}, u32[]{:S(2)}, u32[]{:S(2)}) collective-permute-start(bf16[2,4,32,1664]{3,2,1,0:T(8,128)(2,1)} %collective-permute-done.5.refs_3_), channel_id=1, source_target_pairs={{0,1},{1,0},{2,3},{3,2},{4,5},{5,4},{6,7},{7,6},{8,9},{9,8},{10,11... | collective-permute-start | bytes 2555912 | tf_op jit(solution)/shard_map/ppermute | solution.py:72
  107.9 37.6 %collective-permute-start.13 = (bf16[4,32,4608]{2,1,0:T(8,128)(2,1)}, bf16[4,32,4608]{2,1,0:T(8,128)(2,1)}, u32[]{:S(2)}, u32[]{:S(2)}) collective-permute-start(bf16[4,32,4608]{2,1,0:T(8,128)(2,1)} %get-tuple-element.707), channel_id=1, source_target_pairs={{0,2},{1,3},{2,0},{3,1},{4,6},{5,7},{6,4},{7,5},{8,10},{9,11},{10,... | collective-permute-start | bytes 3538952 | tf_op jit(solution)/shard_map/ppermute | solution.py:72
  111.8 36.9 %collective-permute-start.12 = (bf16[4,32,4608]{2,1,0:T(8,128)(2,1)}, bf16[4,32,4608]{2,1,0:T(8,128)(2,1)}, u32[]{:S(2)}, u32[]{:S(2)}) collective-permute-start(bf16[4,32,4608]{2,1,0:T(8,128)(2,1)} %get-tuple-element.708), channel_id=1, source_target_pairs={{0,4},{4,0},{8,12},{12,8},{16,20},{20,16},{24,28},{28,24},{1,5},{5... | collective-permute-start | bytes 3538952 | tf_op jit(solution)/shard_map/ppermute | solution.py:70
  148.8 50.7 %collective-permute-start.15 = (bf16[2,4,32,4608]{3,2,1,0:T(8,128)(2,1)}, bf16[2,4,32,4608]{3,2,1,0:T(8,128)(2,1)}, u32[]{:S(2)}, u32[]{:S(2)}) collective-permute-start(bf16[2,4,32,4608]{3,2,1,0:T(8,128)(2,1)} %pad_maximum_fusion.2.refs_2_), channel_id=1, source_target_pairs={{0,4},{4,0},{8,12},{12,8},{16,20},{20,16},{24,28},{28,24},{1,5},{5... | collective-permute-start | bytes 7077896 | tf_op jit(solution)/shard_map/ppermute | solution.py:70
  151.7 50.7 %collective-permute-start.14 = (bf16[2,4,32,4608]{3,2,1,0:T(8,128)(2,1)}, bf16[2,4,32,4608]{3,2,1,0:T(8,128)(2,1)}, u32[]{:S(2)}, u32[]{:S(2)}) collective-permute-start(bf16[2,4,32,4608]{3,2,1,0:T(8,128)(2,1)} %pad_maximum_fusion.1.refs_0_), channel_id=1, source_target_pairs={{0,2},{1,3},{2,0},{3,1},{4,6},{5,7},{6,4},{7,5},{8,10},{9,11},{10,... | collective-permute-start | bytes 7077896 | tf_op jit(solution)/shard_map/ppermute | solution.py:72
  172.6 30.1 %collective-permute-start.18 = (bf16[2,4,32,4608]{3,2,1,0:T(8,128)(2,1)}, bf16[2,4,32,4608]{3,2,1,0:T(8,128)(2,1)S(1)}, u32[]{:S(2)}, u32[]{:S(2)}) collective-permute-start(bf16[2,4,32,4608]{3,2,1,0:T(8,128)(2,1)} %pad_maximum_fusion.2.refs_2_), channel_id=1, source_target_pairs={{0,1},{1,0},{2,3},{3,2},{4,5},{5,4},{6,7},{7,6},{8,9},{9,8},{10,11... | collective-permute-start | bytes 7077896 | tf_op jit(solution)/shard_map/ppermute | solution.py:72
  172.7 30.0 %collective-permute-start.16 = (bf16[2,4,32,4608]{3,2,1,0:T(8,128)(2,1)}, bf16[2,4,32,4608]{3,2,1,0:T(8,128)(2,1)S(1)}, u32[]{:S(2)}, u32[]{:S(2)}) collective-permute-start(bf16[2,4,32,4608]{3,2,1,0:T(8,128)(2,1)} %pad_maximum_fusion.1.refs_0_), channel_id=1, source_target_pairs={{0,1},{1,0},{2,3},{3,2},{4,5},{5,4},{6,7},{7,6},{8,9},{9,8},{10,11... | collective-permute-start | bytes 7077896 | tf_op jit(solution)/shard_map/ppermute | solution.py:72
  422.5 21.7 %collective-permute-start.49 = (bf16[64,1024]{1,0:T(8,128)(2,1)S(1)}, bf16[64,1024]{1,0:T(8,128)(2,1)S(1)}, u32[]{:S(2)}, u32[]{:S(2)}) collective-permute-start(bf16[64,1024]{1,0:T(8,128)(2,1)S(1)} %convert_element_type.334), channel_id=1, source_target_pairs={{0,2},{1,3},{2,0},{3,1},{4,6},{5,7},{6,4},{7,5},{8,10},{9,11},{10,... | collective-permute-start | bytes 393224 | tf_op jit(solution)/shard_map/ppermute | solution.py:72
  457.7 71.9 %all-to-all-start.6 = ((bf16[32,40,1024]{2,1,0:T(8,128)(2,1)}), bf16[32,40,1024]{2,1,0:T(8,128)(2,1)}, u32[]{:S(2)}, u32[]{:S(2)}) async-start(bf16[32,40,1024]{2,1,0:T(8,128)(2,1)} %bitcast.352), calls=%async_computation.6 | async-start | bytes 5242880 | tf_op jit(solution)/shard_map/all_to_all | solution.py:89
  478.8 29.8 %collective-permute-start.53 = (bf16[2,4,32,1536]{3,2,1,0:T(8,128)(2,1)S(1)}, bf16[2,4,32,1536]{3,2,1,0:T(8,128)(2,1)S(1)}, u32[]{:S(2)}, u32[]{:S(2)}) collective-permute-start(bf16[2,4,32,1536]{3,2,1,0:T(8,128)(2,1)S(1)} %dynamic-slice_bitcast_fusion.1), channel_id=1, source_target_pairs={{0,4},{4,0},{8,12},{12,8},{16,20},{20,16},{24,28},{28,24},{1,5},{5... | collective-permute-start | bytes 2359304 | tf_op jit(solution)/shard_map/ppermute | solution.py:70
  480.7 29.1 %collective-permute-start.55 = (bf16[2,4,32,1536]{3,2,1,0:T(8,128)(2,1)S(1)}, bf16[2,4,32,1536]{3,2,1,0:T(8,128)(2,1)S(1)}, u32[]{:S(2)}, u32[]{:S(2)}) collective-permute-start(bf16[2,4,32,1536]{3,2,1,0:T(8,128)(2,1)S(1)} %dynamic-slice_bitcast_fusion), channel_id=1, source_target_pairs={{0,2},{1,3},{2,0},{3,1},{4,6},{5,7},{6,4},{7,5},{8,10},{9,11},{10,... | collective-permute-start | bytes 2359304 | tf_op jit(solution)/shard_map/ppermute | solution.py:72
  487.2 29.3 %collective-permute-start.66 = (bf16[2,128,1024]{2,1,0:T(8,128)(2,1)S(1)}, bf16[2,128,1024]{2,1,0:T(8,128)(2,1)S(1)}, u32[]{:S(2)}, u32[]{:S(2)}) collective-permute-start(bf16[2,128,1024]{2,1,0:T(8,128)(2,1)S(1)} %dynamic-slice_bitcast_fusion.2), channel_id=1, source_target_pairs={{0,8},{4,12},{8,0},{12,4},{16,24},{20,28},{24,16},{28,20},{1,9},{5... | collective-permute-start | bytes 1572872 | tf_op jit(solution)/shard_map/ppermute | solution.py:75
  489.9 39.5 %collective-permute-start.64 = (bf16[2,32,4096]{2,1,0:T(8,128)(2,1)S(1)}, bf16[2,32,4096]{2,1,0:T(8,128)(2,1)S(1)}, u32[]{:S(2)}, u32[]{:S(2)}) collective-permute-start(bf16[2,32,4096]{2,1,0:T(8,128)(2,1)S(1)} %dynamic-slice_bitcast_fusion.3), channel_id=1, source_target_pairs={{0,8},{4,12},{8,0},{12,4},{16,24},{20,28},{24,16},{28,20},{1,9},{5... | collective-permute-start | bytes 1572872 | tf_op jit(solution)/shard_map/ppermute | solution.py:75
  539.6 43.8 %collective-permute-start.67 = (bf16[1,128,1024]{2,1,0:T(8,128)(2,1)}, bf16[1,128,1024]{2,1,0:T(8,128)(2,1)}, u32[]{:S(2)}, u32[]{:S(2)}) collective-permute-start(bf16[1,128,1024]{2,1,0:T(8,128)(2,1)} %dynamic-slice_convert_fusion), channel_id=1, source_target_pairs={{0,16},{4,20},{8,24},{12,28},{16,0},{20,4},{24,8},{28,12},{1,17},{... | collective-permute-start | bytes 786440 | tf_op jit(solution)/shard_map/ppermute | solution.py:75
  542.8 38.8 %collective-permute-start.65 = (bf16[1,32,4096]{2,1,0:T(8,128)(2,1)}, bf16[1,32,4096]{2,1,0:T(8,128)(2,1)}, u32[]{:S(2)}, u32[]{:S(2)}) collective-permute-start(bf16[1,32,4096]{2,1,0:T(8,128)(2,1)} %dynamic-slice_convert_fusion.1), channel_id=1, source_target_pairs={{0,16},{4,20},{8,24},{12,28},{16,0},{20,4},{24,8},{28,12},{1,17},{... | collective-permute-start | bytes 786440 | tf_op jit(solution)/shard_map/ppermute | solution.py:75
  (156 other events, 1963.3 us)

commit v4 on v3

--- a/solution.py
+++ b/solution.py
@@ -188,7 +188,7 @@
                 ],
                 out_specs=target_specs,
             ),
-            compiler_params=pltpu.CompilerParams(vmem_limit_bytes=40 * 2**20),
+            compiler_params=pltpu.CompilerParams(vmem_limit_bytes=24 * 2**20),
             name="assemble",
         )(place, *pieces)
         wholes = [whole.reshape(-1, whole.shape[-1]) for whole in wholes]
@@ -235,11 +235,11 @@
         left = (pick(left, x, 0).astype(f32) + from_x.astype(f32)).astype(bf16)
         right = (pick(right, y, 1).astype(f32) + from_y.astype(f32)).astype(bf16)
         left, right = after(left, *before_second), after(right, *before_second)
-        from_y = self.swap(pick(left, 1 - y, 0), "y")
-        from_x = self.swap(pick(right, 1 - x, 0), "x")
+        sends = pick(left, 1 - y, 0), pick(right, 1 - x, 0)
+        from_y, from_x = self.swap(sends[0], "y"), self.swap(sends[1], "x")
         left = pick(left, y, 0).astype(f32) + from_y.astype(f32)
         right = pick(right, x, 0).astype(f32) + from_x.astype(f32)
-        return jnp.concatenate([left, right], axis=-1).astype(bf16)
+        return jnp.concatenate([left, right], axis=-1).astype(bf16), sends
 
     def scatter_depth(self, near, *before_last):
         for step in self.bits():
@@ -249,9 +249,9 @@
             bit = self.z // step % 2
             other = lax.dynamic_index_in_dim(pairs, 1 - bit, 1, keepdims=False)
             mine = lax.dynamic_index_in_dim(pairs, bit, 1, keepdims=False)
-            other = self.cross(other.astype(bf16), step)
-            near = mine.astype(f32) + other.astype(f32)
-        return near[0]
+            send = other.astype(bf16)
+            near = mine.astype(f32) + self.cross(send, step).astype(f32)
+        return near[0], send
 
 
 def halves(width):
@@ -455,7 +455,115 @@
     )(table_square, target_sum.reshape(1, 1), weight_row, *all_grads[1:])
 
 
-grid_steps = 8
+grid_steps = 4
+
+
+row_block = 256
+
+
+def head_logits(head_rows, table_low, targets, base, block_size):
+    row_count, width = head_rows.shape
+    columns = table_low.shape[0]
+    block = min(row_block, row_count)
+
+    def kernel(base_ref, rows_ref, table_ref, targets_ref, logits_ref, top_ref, sum_ref, hit_ref):
+        step = pl.program_id(0)
+        place = lax.broadcasted_iota(jnp.int32, (1, columns), 1)
+        column = jnp.where(place < block_size, place + base_ref[0], VOCAB)
+        fill = jnp.where(column < VOCAB, 0.0, neg_fill)
+        logits = contract_cols(rows_ref[...], table_ref[...]) + fill
+        logits_ref[...] = logits
+        top = jnp.max(logits, axis=1, keepdims=True)
+        total = jnp.sum(jnp.exp(logits - top), axis=1, keepdims=True)
+        top_ref[...] = jnp.broadcast_to(top, (block, 128)).T[:1]
+        sum_ref[...] = jnp.broadcast_to(total, (block, 128)).T[:1]
+
+        @pl.when(step == 0)
+        def _():
+            hit_ref[...] = jnp.zeros_like(hit_ref)
+
+        hits = targets_ref[...] == column
+        hit_ref[...] += jnp.broadcast_to(whole_sum(jnp.where(hits, logits, 0.0)), (1, 128))
+
+    return pl.pallas_call(
+        kernel,
+        out_shape=(
+            jax.ShapeDtypeStruct((row_count, columns), f32),
+            jax.ShapeDtypeStruct((1, row_count), f32),
+            jax.ShapeDtypeStruct((1, row_count), f32),
+            jax.ShapeDtypeStruct((1, 128), f32),
+        ),
+        grid=(row_count // block,),
+        in_specs=[
+            pl.BlockSpec(memory_space=pltpu.SMEM),
+            pl.BlockSpec((block, width), lambda k: (k, 0)),
+            pl.BlockSpec((columns, width), lambda k: (0, 0)),
+            pl.BlockSpec((block, 1), lambda k: (k, 0)),
+        ],
+        out_specs=(
+            pl.BlockSpec((block, columns), lambda k: (k, 0)),
+            pl.BlockSpec((1, block), lambda k: (0, k)),
+            pl.BlockSpec((1, block), lambda k: (0, k)),
+            pl.BlockSpec((1, 128), lambda k: (0, 0)),
+        ),
+        compiler_params=pltpu.CompilerParams(vmem_limit_bytes=56 * 2**20),
+        name="head_logits",
+    )(base.reshape(1), head_rows, table_low, targets)
+
+
+def head_grads(logits, log_total, table_low, targets, base, half, count_all, block_size, add=None):
+    row_count, columns = logits.shape
+    width = table_low.shape[1]
+    block = min(row_block, row_count // 2)
+    steps = row_count // 2 // block
+    scale = 1.0 / count_all
+
+    def kernel(place_ref, logits_ref, total_ref, table_ref, targets_ref, *refs):
+        grads_ref, out_ref = refs[-2:]
+        place = lax.broadcasted_iota(jnp.int32, (1, columns), 1)
+        column = jnp.where(place < block_size, place + place_ref[1], VOCAB)
+        total = jnp.broadcast_to(total_ref[...], (128, block)).T[:, :1]
+        hits = targets_ref[...] == column
+        probs = jnp.exp(logits_ref[...] - total)
+        grads = ((probs - jnp.where(hits, 1.0, 0.0)) * scale).astype(bf16)
+        grads_ref[...] = grads
+        product = matmul(grads, table_ref[...])
+        if add is not None:
+            product = product + refs[0][...].astype(f32)
+        out_ref[...] = product.astype(bf16)
+
+    half_spec = pl.BlockSpec((block, width), lambda k, place: (k, 0))
+    return pl.pallas_call(
+        kernel,
+        out_shape=(
+            jax.ShapeDtypeStruct((row_count // 2, columns), bf16),
+            jax.ShapeDtypeStruct((row_count // 2, width), bf16),
+        ),
+        grid_spec=pltpu.PrefetchScalarGridSpec(
+            num_scalar_prefetch=1,
+            grid=(steps,),
+            in_specs=[
+                pl.BlockSpec((block, columns), lambda k, place: (place[0] * steps + k, 0)),
+                pl.BlockSpec((1, block), lambda k, place: (0, place[0] * steps + k)),
+                pl.BlockSpec((columns, width), lambda k, place: (0, 0)),
+                pl.BlockSpec((block, 1), lambda k, place: (place[0] * steps + k, 0)),
+            ]
+            + ([] if add is None else [half_spec]),
+            out_specs=(
+                pl.BlockSpec((block, columns), lambda k, place: (k, 0)),
+                half_spec,
+            ),
+        ),
+        compiler_params=pltpu.CompilerParams(vmem_limit_bytes=56 * 2**20),
+        name="head_grads",
+    )(
+        jnp.stack([half, base]).astype(jnp.int32),
+        logits,
+        log_total,
+        table_low,
+        targets,
+        *(() if add is None else (add,)),
+    )
 
 
 def weight_squares(masters):
@@ -696,7 +804,7 @@
         return slot, links.to_all(message_of(slot))[:, :slots].reshape(-1)
 
     def find(asked):
-        row_hits = (asked[:, None] == jnp.arange(block_size)[None, :]).astype(bf16)
+        row_hits = (asked[:, None] == jnp.arange(padded_rows)[None, :]).astype(bf16)
         return matmul(row_hits, table_low).astype(bf16)
 
     def place_rows(slot, landed):
@@ -721,7 +829,10 @@
     first_near = links.gather_late(first_early)
     message = message_of(slot_first)
     answer = links.to_all(message)
-    table_low = after(tied_table_master, message).astype(bf16)
+    padded_rows = -(-block_size // 128) * 128
+    table_low = jnp.pad(
+        after(tied_table_master, message), ((0, padded_rows - block_size), (0, 0))
+    ).astype(bf16)
     asked_first = answer[:, :slots].reshape(-1)
     rounds = (jnp.max(answer[:, slots]) + slots - 1) // slots
     targets = answer[:, slots + 1 : slots + 1 + pick_total]
@@ -741,7 +852,7 @@
     landed = links.to_all(found)
     first_pieces = links.plane_second(*first_parts)
     weight_row = weight_squares(tie(*masters, found)[:6])
-    first_pieces[0] = after(first_pieces[0], weight_row)
+    first_pieces[0] = after(first_pieces[0], weight_row, table_low)
     first_whole = links.assemble(links.plane_core(first_pieces))
     second_near = links.gather_late(after(second_near, *first_parts))
     second_parts = links.plane_first(after(second_near, *first_pieces))
@@ -791,20 +902,19 @@
     head_rows = links.assemble(
         links.plane_core(head_pieces), core_first=True
     )
-    columns = links.device * block_size + jnp.arange(block_size)
-    logits = contract_cols(head_rows, table_low)
-    logits = jnp.where((columns < VOCAB)[None, :], logits, neg_fill)
-    target_hits = targets[:, None] == columns[None, :]
-    target_sum = jnp.sum(jnp.where(target_hits, logits, 0.0))
-    local_top = jnp.max(logits, axis=1)
-    local_sum = jnp.sum(jnp.exp(logits - local_top[:, None]), axis=1)
+    base = links.device * block_size
+    target_column = targets[:, None]
+    logits, local_top, local_sum, target_sum = head_logits(
+        head_rows, table_low, target_column, base, block_size
+    )
+    target_sum = target_sum[:, :1]
 
     def merge_totals(first, second):
         top = jnp.maximum(first[0], second[0])
         total = first[1] * jnp.exp(first[0] - top) + second[1] * jnp.exp(second[0] - top)
         return jnp.stack([top, total])
 
-    merged = links.exchange(jnp.stack([local_top, local_sum]), merge_totals)
+    merged = links.exchange(jnp.concatenate([local_top, local_sum]), merge_totals)
     def by_owner(values, block_rows):
         if block_rows % 128 == 0:
             blocks = values.reshape(pick_total, links.depth, 8, block_rows)
@@ -828,28 +938,25 @@
     )
     known = known.reshape(2, 2, 2, pick_total, -1)
     log_total = merged[0] + jnp.log(merged[1])
-    grad_logits = (
-        (jnp.exp(logits - log_total[:, None]) - target_hits.astype(f32)) / count_all
-    ).astype(bf16)
-
-    half_rows = head_rows.shape[0] // 2
     core = links.place["c"]
-
-    def picked_part(spot):
-        part = lax.dynamic_slice_in_dim(grad_logits, spot * half_rows, half_rows, 0)
-        return matmul(part, table_low)
-
-    to_core = picked_part(1 - core).astype(bf16)
-    to_core, grad_logits = tie(to_core, grad_logits)
+    log_row = log_total[None]
+    far_grads, to_core = head_grads(
+        logits, log_row, table_low, target_column, base, 1 - core, count_all, block_size
+    )
     from_core = links.swap(to_core, "c")
-    grad_near = links.scatter_plane(
-        (picked_part(core) + from_core.astype(f32))
-        .astype(bf16)
-        .reshape(2, 2, links.depth, pick_total, model_width),
+    own_grads, near_sum = head_grads(
+        logits, log_row, table_low, target_column, base, core, count_all, block_size, from_core
+    )
+    own_rows = [
+        lax.dynamic_slice_in_dim(head_rows, spot * far_grads.shape[0], far_grads.shape[0], 0)
+        for spot in (1 - core, core)
+    ]
+    grad_near, unused = links.scatter_plane(
+        near_sum.reshape(2, 2, links.depth, pick_total, model_width),
         known,
     )
     known = links.exchange_plane(after(known, grad_near))
-    grad_picked = links.scatter_depth(grad_near)
+    grad_picked, unused = links.scatter_depth(grad_near)
 
     grad_x_out, gain_last, shift_last = norm_backward(
         x_out, gain_entries[4], gain_entries[5], grad_picked
@@ -862,10 +969,10 @@
         x_attn, gain_entries[2], gain_entries[3], contract_cols(grad_up_low, up_weight)
     )
     grad_x_attn = grad_x_out + grad_x_attn
-    grad_x_attn = after(grad_x_attn, *grad_parts)
     grad_attn_low = grad_x_attn.astype(bf16)
     grad_context = contract_cols(grad_attn_low, out_weight).astype(bf16)
     attn_parts = links.share_direct(grad_attn_low)
+    grad_context = after(grad_context, *grad_parts)
     grad_parts = links.share_second(*grad_parts)
     grad_qkv_low = attend_backward(
         qkv_all, pick_rows, queries, probs, grad_context, micro_count
@@ -883,9 +990,7 @@
     )
     grad_embed_low = grad_x_embed.astype(bf16)
     sent = give(slot_first, grad_embed_low)
-    grad_qkv_low = after(grad_qkv_low, sent, known, *grad_parts, *attn_parts)
-    returned = links.to_all(sent)
-    table_head = contract_rows(after(grad_logits, returned), head_rows)
+    returned = links.to_all(after(sent, known, *grad_parts, *attn_parts))
     half_place = jnp.arange(model_width // 2)
     half_row = half_place % shard_rows
     half_z = half_place // shard_rows % links.depth
@@ -899,7 +1004,7 @@
     to_core = qkv_part(1 - core).astype(bf16)
     from_core = links.swap(to_core, "c")
     last_mine = (qkv_part(core) + from_core.astype(f32)).astype(bf16)
-    last_near = links.scatter_plane(
+    last_near, last_sends = links.scatter_plane(
         last_mine.reshape(2, 2, links.depth, shard_rows, qkv_width), returned
     )
     down_near, up_near, out_near = plane_products(
@@ -911,11 +1016,16 @@
     )
 
     last_near = jnp.concatenate([last_near, out_near], axis=-1)
-    down_grad = links.scatter_depth(down_near, returned)
-    up_grad = links.scatter_depth(up_near, returned)
-    last_grad = links.scatter_depth(last_near)
+    down_grad, down_send = links.scatter_depth(down_near, returned)
+    up_grad, up_send = links.scatter_depth(up_near, returned)
+    last_grad, unused = links.scatter_depth(last_near)
     qkv_grad, out_grad = last_grad[:, :qkv_width], last_grad[:, qkv_width:]
-    gain_one = after(gain_one, returned)
+    far_grads = after(far_grads, returned, down_send, up_send, *last_sends)
+    own_grads = after(own_grads, far_grads)
+    table_head = contract_rows(far_grads[:, :block_size], own_rows[0]) + contract_rows(
+        own_grads[:, :block_size], own_rows[1]
+    )
+    gain_one = after(gain_one, returned, down_send, up_send, *last_sends)
     gain_grads = jnp.stack(
         [gain_one, shift_one, gain_two, shift_two, gain_last, shift_last]
     ).reshape(6, devices, shard_rows)
@@ -937,7 +1047,7 @@
         more_grads,
         (
             jnp.ones((), jnp.int32),
-            table_head + take(asked_first, returned),
+            table_head + take(asked_first, after(returned, down_send, up_send, *last_sends)),
         ),
     )
 

time: 674 us -> 671 us (level)
  Pallas kernels: 74.3 us -> 114 us
  matrix products: 117 us -> 86.3 us
  waiting for transfers between devices: 270 us -> 249 us
  local copies, waits for them, and re-layouts: 51.8 us -> 64.8 us
  starting transfers between devices: 72.5 us -> 80.6 us
    pallas_call x0 -> x3, Pallas kernels: none -> 47.5 us  [the longest x2 30.8 us: head_grads(): pl.pallas_call(kernel, out_shape=(jax.ShapeDtypeStruct((row_count // 2, c...]
    dot_general x12 -> x10, matrix products: 57 us -> 36.7 us  [matmul(): return jnp.dot(left_side, right_side, preferred_element_type=f32)]
    ppermute x14, waiting for transfers between devices: 83.3 us -> 64.9 us  [swap(): return lax.ppermute(values, 'wide', [(i, i ^ 1) for i in range(self.wide)])]
    convert_element_type x2 -> x0, other arithmetic: 12.2 us -> none  [the longest x1 7.14 us: per_device(): grad_logits = ((jnp.exp(logits - log_total[:, None]) - target_hits.astype...]
    another operation x6 -> x8, other arithmetic: 1.06 us -> 9.3 us
    dot_general x5 -> x4, matrix products: 30.7 us -> 22.5 us  [contract_cols(): lax.dot_general(left_side, right_side, (((1,), (1,)), ((), ())), preferre...]
    dot_general x4 -> x5, matrix products: 28.3 us -> 25.9 us  [contract_rows(): lax.dot_general(left_side, right_side, (((0,), (0,)), ((), ())), preferre...]
  transfers between devices with their start and end apart: 74 -> 74, of which waited for: 41 -> 41; matrix products, arithmetic and copies ran while one was open for 20% -> 23% of each run, Pallas kernels for 3% -> 3%
where the time goes in v4:
time: 671 us; the launch traced here: 666 us
  waiting for transfers between devices  249 us (37%)
  Pallas kernels  114 us (17%)
  matrix products  86.3 us (13%)
  starting transfers between devices  80.6 us (12%)
  other arithmetic  65 us (10%)
  local copies, waits for them, and re-layouts  64.8 us (10%)
    ppermute x14, waiting for transfers between devices, cross(): lax.ppermute(values, 'wide', [(i, i ^ 2 * step) for i in range(self.wide)])  95.5 us
    ppermute x14, waiting for transfers between devices, swap(): return lax.ppermute(values, 'wide', [(i, i ^ 1) for i in range(self.wide)])  64.9 us
    ppermute x34, waiting for transfers between devices, swap(): lax.ppermute(values, 'narrow', [(i, i ^ step) for i in range(self.narrow)])  54.8 us
    dot_general x10, matrix products, matmul(): return jnp.dot(left_side, right_side, preferred_element_type=f32)  36.7 us
    pallas_call x2, Pallas kernels, head_grads(): pl.pallas_call(kernel, out_shape=(jax.ShapeDtypeStruct((row_count // 2, c...  30.8 us
    dot_general x5, matrix products, contract_rows(): lax.dot_general(left_side, right_side, (((0,), (0,)), ((), ())), preferre...  25.9 us
    unnamed x230, local copies, waits for them, and re-layouts  25.3 us
    all_to_all x6, starting transfers between devices, to_all(): return lax.all_to_all(values, ('wide', 'narrow'), 0, 0, tiled=True)  24.2 us
  transfers between devices with their start and end apart: 74, of which 41 were waited for; matrix products, arithmetic and copies ran while one was open for 23% of the time, Pallas kernels for 3%

profile of v4, /device:TPU:0, one launch (start us, length us, event | category | flops | bytes accessed | tf_op | source)
XLA Modules:
  0.0 666.3 jit_solution(3002340813437307238)
XLA Ops:
  34.4 25.8 %collective-permute-done.10 = bf16[1,32,9216]{2,1,0:T(8,128)(2,1)S(1)} collective-permute-done((bf16[1,32,9216]{2,1,0:T(8,128)(2,1)S(1)}, bf16[1,32,9216]{2,1,0:T(8,128)(2,1)S(1)}, u32[]{:S(2)}, u32[]{:S(2)}) %collective-permute-start.10) | collective-permute-done | bytes 589856 | tf_op jit(solution)/shard_map/ppermute | solution.py:75
  62.9 6.4 fusion.32
  87.0 17.5 %collective-permute-done.11 = bf16[2,32,9216]{2,1,0:T(8,128)(2,1)} collective-permute-done((bf16[2,32,9216]{2,1,0:T(8,128)(2,1)}, bf16[2,32,9216]{2,1,0:T(8,128)(2,1)}, u32[]{:S(2)}, u32[]{:S(2)}) %collective-permute-start.11) | collective-permute-done | bytes 1179680 | tf_op jit(solution)/shard_map/ppermute | solution.py:75
  122.2 22.1 %collective-permute-done.12 = bf16[4,32,4608]{2,1,0:T(8,128)(2,1)} collective-permute-done((bf16[4,32,4608]{2,1,0:T(8,128)(2,1)}, bf16[4,32,4608]{2,1,0:T(8,128)(2,1)}, u32[]{:S(2)}, u32[]{:S(2)}) %collective-permute-start.12) | collective-permute-done | bytes 1179680 | tf_op jit(solution)/shard_map/ppermute | solution.py:70
  162.5 6.4 fusion.25.qkv_ref
  175.0 24.8 %collective-permute-done.14.refs_1_ = bf16[2,4,32,4608]{3,2,1,0:T(8,128)(2,1)} collective-permute-done((bf16[2,4,32,4608]{3,2,1,0:T(8,128)(2,1)}, bf16[2,4,32,4608]{3,2,1,0:T(8,128)(2,1)}, u32[]{:S(2)}, u32[]{:S(2)}) %collective-permute-start.14) | collective-permute-done | bytes 2359328 | tf_op jit(solution)/shard_map/ppermute | solution.py:72
  212.3 8.7 %assemble.4 = (bf16[4,2,2,2,32,5120]{5,4,3,2,1,0:T(8,128)(2,1)}, bf16[4,2,2,2,128,1024]{5,4,3,2,1,0:T(8,128)(2,1)S(1)}) custom-call(s32[7]{0:T(128)S(1)} %stack.208.place, bf16[2,4,32,4608]{3,2,1,0:T(8,128)(2,1)} %pad_maximum_fusion.1.refs_0_, bf16[2,4,32,4608]{3,2,1,0:T(8,128)(2,1)} %collective-permute-done.14.refs_1_, ...), custom_call_target="tpu_custom_call" | custom-call | tf_op jit(solution)/shard_map/assemble/pallas_call | solution.py:179
  232.2 8.5 %collective-permute-done.20 = bf16[1,64,1024]{2,1,0:T(8,128)(2,1)S(1)} collective-permute-done((bf16[1,64,1024]{2,1,0:T(8,128)(2,1)S(1)}, bf16[1,64,1024]{2,1,0:T(8,128)(2,1)S(1)}, u32[]{:S(2)}, u32[]{:S(2)}) %collective-permute-start.20) | collective-permute-done | bytes 131104 | tf_op jit(solution)/shard_map/ppermute | solution.py:75
  240.8 8.2 %collective-permute-done.21 = bf16[2,64,1024]{2,1,0:T(8,128)(2,1)S(1)} collective-permute-done((bf16[2,64,1024]{2,1,0:T(8,128)(2,1)S(1)}, bf16[2,64,1024]{2,1,0:T(8,128)(2,1)S(1)}, u32[]{:S(2)}, u32[]{:S(2)}) %collective-permute-start.21) | collective-permute-done | bytes 262176 | tf_op jit(solution)/shard_map/ppermute | solution.py:75
  249.8 6.9 %collective-permute-done.22 = bf16[4,64,512]{2,1,0:T(8,128)(2,1)S(1)} collective-permute-done((bf16[4,64,512]{2,1,0:T(8,128)(2,1)S(1)}, bf16[4,64,512]{2,1,0:T(8,128)(2,1)S(1)}, u32[]{:S(2)}, u32[]{:S(2)}) %collective-permute-start.22) | collective-permute-done | bytes 262176 | tf_op jit(solution)/shard_map/ppermute | solution.py:70
  259.8 10.1 %collective-permute-done.23.refs_1_ = bf16[2,4,64,512]{3,2,1,0:T(8,128)(2,1)} collective-permute-done((bf16[2,4,64,512]{3,2,1,0:T(8,128)(2,1)}, bf16[2,4,64,512]{3,2,1,0:T(8,128)(2,1)}, u32[]{:S(2)}, u32[]{:S(2)}) %collective-permute-start.23) | collective-permute-done | bytes 524320 | tf_op jit(solution)/shard_map/ppermute | solution.py:72
  279.1 16.7 %head_logits.1 = (f32[2048,1664]{1,0:T(8,128)}, f32[1,2048]{1,0:T(1,128)}, f32[1,2048]{1,0:T(1,128)}, f32[1,128]{1,0:T(1,128)}) custom-call(s32[1]{0:T(128)} %bitcast.base_ref, bf16[2048,1024]{1,0:T(8,128)(2,1)} %bitcast.329, bf16[1664,1024]{1,0:T(8,128)(2,1)S(1)} %copy-done.21, s32[2048,1]{1,0:T(8,128)} %broadcast_in_dim_reshape.3.targets_ref), custom_call_target="tpu_custom_call" | custom-call | tf_op jit(solution)/shard_map/head_logits/pallas_call | solution.py:488
  318.0 21.4 %head_grads.2 = (bf16[1024,1664]{1,0:T(8,128)(2,1)}, bf16[1024,1024]{1,0:T(8,128)(2,1)}) custom-call(s32[2]{0:T(128)} %pad_add_fusion.place_ref, f32[2048,1664]{1,0:T(8,128)} %get-tuple-element.383.logits_ref, f32[1,2048]{1,0:T(1,128)} %get-tuple-element.727.total_ref, bf16[1664,1024]{1,0:T(8,128)(2,1)} %get-tuple-element.1058, ...), custom_call_target="tpu_custom_call" | custom-call | tf_op jit(solution)/shard_map/head_grads/pallas_call | solution.py:536
  343.9 9.4 %head_grads.3 = (bf16[1024,1664]{1,0:T(8,128)(2,1)}, bf16[1024,1024]{1,0:T(8,128)(2,1)}) custom-call(s32[2]{0:T(128)} %pad_add_fusion.1.place_ref, f32[2048,1664]{1,0:T(8,128)} %get-tuple-element.383.logits_ref, f32[1,2048]{1,0:T(1,128)} %get-tuple-element.727.total_ref, bf16[1664,1024]{1,0:T(8,128)(2,1)S(1)} %copy-done.22, ...), custom_call_target="tpu_custom_call" | custom-call | tf_op jit(solution)/shard_map/head_grads/pallas_call | solution.py:536
  406.0 6.3 fusion.81
  412.4 6.2 multiply_reduce_fusion.1
  439.4 7.0 %convolution_convert_fusion.1 = bf16[512,3072]{1,0:T(8,128)(2,1)} fusion(bf16[512,3072]{1,0:T(8,128)(2,1)} %copy-done.8, bf16[512,1024]{1,0:T(8,128)(2,1)} %copy-done.55, s32[512]{0:T(512)S(1)} %multiply_add_fusion.4), kind=kOutput, calls=%fused_computation.46 | convolution fusion | flops 2149842944 | bytes 7342080 | tf_op jit(solution)/shard_map/dot_general | solution.py:46
  448.2 7.6 %fusion.45 = (f32[1024]{0:T(1024)}, f32[512]{0:T(512)S(1)}, f32[1024]{0:T(1024)S(1)}, f32[512,1024]{1,0:T(8,128)S(1)}) fusion(bf16[512,1024]{1,0:T(8,128)(2,1)S(1)} %copy-done.24, f32[512]{0:T(512)S(1)} %fusion.155, f32[512]{0:T(512)S(1)} %broadcast_multiply_fusion, f32[1024]{0:T(1024)S(1)} %bitcast.400, bf16[512,3072]{1,0:T(8,128)(2,1)} %copy-done.8, ...), kind=kOutput, calls=%fused_computation.75 | convolution fusion | flops 3225941504 | bytes 12601344 | tf_op jit(solution)/shard_map/dot_general | solution.py:52
  478.8 6.5 add_convert_fusion
  504.0 15.2 %collective-permute-done.60 = bf16[2,4,32,1536]{3,2,1,0:T(8,128)(2,1)S(1)} collective-permute-done((bf16[2,4,32,1536]{3,2,1,0:T(8,128)(2,1)S(1)}, bf16[2,4,32,1536]{3,2,1,0:T(8,128)(2,1)S(1)}, u32[]{:S(2)}, u32[]{:S(2)}) %collective-permute-start.60) | collective-permute-done | bytes 786464 | tf_op jit(solution)/shard_map/ppermute | solution.py:70
  526.8 12.9 %collective-permute-done.59 = bf16[2,32,4096]{2,1,0:T(8,128)(2,1)S(1)} collective-permute-done((bf16[2,32,4096]{2,1,0:T(8,128)(2,1)S(1)}, bf16[2,32,4096]{2,1,0:T(8,128)(2,1)S(1)}, u32[]{:S(2)}, u32[]{:S(2)}) %collective-permute-start.59) | collective-permute-done | bytes 524320 | tf_op jit(solution)/shard_map/ppermute | solution.py:75
  590.9 10.4 %collective-permute-done.65 = bf16[1,32,4096]{2,1,0:T(8,128)(2,1)S(1)} collective-permute-done((bf16[1,32,4096]{2,1,0:T(8,128)(2,1)S(1)}, bf16[1,32,4096]{2,1,0:T(8,128)(2,1)S(1)}, u32[]{:S(2)}, u32[]{:S(2)}) %collective-permute-start.65) | collective-permute-done | bytes 262176 | tf_op jit(solution)/shard_map/ppermute | solution.py:75
  619.3 21.2 %lamb_directions.1 = (f32[1572,1024]{1,0:T(8,128)}, f32[32,3072]{1,0:T(8,128)}, f32[32,1024]{1,0:T(8,128)}, f32[32,4096]{1,0:T(8,128)}, f32[128,1024]{1,0:T(8,12...) custom-call(f32[32,256]{1,0:T(8,128)} %bitcast.379, ...), custom_call_target="tpu_custom_call" | custom-call | tf_op jit(solution)/shard_map/lamb_directions/pallas_call | solution.py:668
  650.7 8.9 %lamb_weights.1 = (f32[1572,1024]{1,0:T(8,128)}, f32[32,3072]{1,0:T(8,128)}, f32[32,1024]{1,0:T(8,128)}, f32[32,4096]{1,0:T(8,128)}, f32[128,1024]{1,0:T(8,128)}, /*index=5*/f32[32,6]{1,0:T(8,128)}, f32[8,128]{1,0:T(8,128)}) custom-call(f32[32,256]{1,0:T(8,128)} %bitcast.380, f32[32,128]{1,0:T(8,128)} %bitcast.394, f32[1572,1024]{1,0:T(8,128)} %get-tuple-element.414.refs_0_, ...), custom_call_target="tpu_custom_call" | custom-call | tf_op jit(solution)/shard_map/lamb_weights/pallas_call | solution.py:710
  (560 shorter events, 364.8 us)
Async XLA Ops:
  31.6 28.6 %collective-permute-start.10 = (bf16[1,32,9216]{2,1,0:T(8,128)(2,1)S(1)}, bf16[1,32,9216]{2,1,0:T(8,128)(2,1)S(1)}, u32[]{:S(2)}, u32[]{:S(2)}) collective-permute-start(bf16[1,32,9216]{2,1,0:T(8,128)(2,1)S(1)} %bitcast.349), channel_id=1, source_target_pairs={{0,16},{4,20},{8,24},{12,28},{16,0},{20,4},{24,8},{28,12},{1,17},{... | collective-permute-start | bytes 1769480 | tf_op jit(solution)/shard_map/ppermute | solution.py:75
  32.4 29.0 %collective-permute-start.2 = (bf16[4,32,1536]{2,1,0:T(8,128)(2,1)S(1)}, bf16[4,32,1536]{2,1,0:T(8,128)(2,1)S(1)}, u32[]{:S(2)}, u32[]{:S(2)}) collective-permute-start(bf16[4,32,1536]{2,1,0:T(8,128)(2,1)S(1)} %get-tuple-element.707), channel_id=1, source_target_pairs={{0,4},{4,0},{8,12},{12,8},{16,20},{20,16},{24,28},{28,24},{1,5},{5... | collective-permute-start | bytes 1179656 | tf_op jit(solution)/shard_map/ppermute | solution.py:70
  33.1 29.1 %collective-permute-start.4 = (bf16[4,32,1664]{2,1,0:T(8,128)(2,1)S(1)}, bf16[4,32,1664]{2,1,0:T(8,128)(2,1)S(1)}, u32[]{:S(2)}, u32[]{:S(2)}) collective-permute-start(bf16[4,32,1664]{2,1,0:T(8,128)(2,1)S(1)} %get-tuple-element.705), channel_id=1, source_target_pairs={{0,2},{1,3},{2,0},{3,1},{4,6},{5,7},{6,4},{7,5},{8,10},{9,11},{10,... | collective-permute-start | bytes 1277960 | tf_op jit(solution)/shard_map/ppermute | solution.py:72
  62.2 42.4 %collective-permute-start.11 = (bf16[2,32,9216]{2,1,0:T(8,128)(2,1)}, bf16[2,32,9216]{2,1,0:T(8,128)(2,1)}, u32[]{:S(2)}, u32[]{:S(2)}) collective-permute-start(bf16[2,32,9216]{2,1,0:T(8,128)(2,1)} %pad_maximum_fusion.3), channel_id=1, source_target_pairs={{0,8},{4,12},{8,0},{12,4},{16,24},{20,28},{24,16},{28,20},{1,9},{5... | collective-permute-start | bytes 3538952 | tf_op jit(solution)/shard_map/ppermute | solution.py:75
  69.2 84.1 %all-to-all-start.5 = ((bf16[32,40,1024]{2,1,0:T(8,128)(2,1)}), bf16[32,40,1024]{2,1,0:T(8,128)(2,1)}, u32[]{:S(2)}, u32[]{:S(2)}) async-start(bf16[32,40,1024]{2,1,0:T(8,128)(2,1)} %bitcast.343), calls=%async_computation.5 | async-start | bytes 5242880 | tf_op jit(solution)/shard_map/all_to_all | solution.py:89
  82.3 30.3 %collective-permute-start.6 = (bf16[2,4,32,1536]{3,2,1,0:T(8,128)(2,1)S(1)}, bf16[2,4,32,1536]{3,2,1,0:T(8,128)(2,1)}, u32[]{:S(2)}, u32[]{:S(2)}) collective-permute-start(bf16[2,4,32,1536]{3,2,1,0:T(8,128)(2,1)S(1)} %pad_maximum_fusion.7.refs_0_), channel_id=1, source_target_pairs={{0,1},{1,0},{2,3},{3,2},{4,5},{5,4},{6,7},{7,6},{8,9},{9,8},{10,11... | collective-permute-start | bytes 2359304 | tf_op jit(solution)/shard_map/ppermute | solution.py:72
  82.5 33.2 %collective-permute-start.8 = (bf16[2,4,32,1664]{3,2,1,0:T(8,128)(2,1)S(1)}, bf16[2,4,32,1664]{3,2,1,0:T(8,128)(2,1)S(1)}, u32[]{:S(2)}, u32[]{:S(2)}) collective-permute-start(bf16[2,4,32,1664]{3,2,1,0:T(8,128)(2,1)S(1)} %pad_maximum_fusion.5.refs_2_), channel_id=1, source_target_pairs={{0,1},{1,0},{2,3},{3,2},{4,5},{5,4},{6,7},{7,6},{8,9},{9,8},{10,11... | collective-permute-start | bytes 2555912 | tf_op jit(solution)/shard_map/ppermute | solution.py:72
  83.8 32.0 %collective-permute-start.7 = (bf16[2,4,32,1536]{3,2,1,0:T(8,128)(2,1)}, bf16[2,4,32,1536]{3,2,1,0:T(8,128)(2,1)}, u32[]{:S(2)}, u32[]{:S(2)}) collective-permute-start(bf16[2,4,32,1536]{3,2,1,0:T(8,128)(2,1)} %collective-permute-done.3.refs_1_), channel_id=1, source_target_pairs={{0,1},{1,0},{2,3},{3,2},{4,5},{5,4},{6,7},{7,6},{8,9},{9,8},{10,11... | collective-permute-start | bytes 2359304 | tf_op jit(solution)/shard_map/ppermute | solution.py:72
  87.0 28.8 %collective-permute-start.9 = (bf16[2,4,32,1664]{3,2,1,0:T(8,128)(2,1)}, bf16[2,4,32,1664]{3,2,1,0:T(8,128)(2,1)S(1)}, u32[]{:S(2)}, u32[]{:S(2)}) collective-permute-start(bf16[2,4,32,1664]{3,2,1,0:T(8,128)(2,1)} %collective-permute-done.5.refs_3_), channel_id=1, source_target_pairs={{0,1},{1,0},{2,3},{3,2},{4,5},{5,4},{6,7},{7,6},{8,9},{9,8},{10,11... | collective-permute-start | bytes 2555912 | tf_op jit(solution)/shard_map/ppermute | solution.py:72
  108.8 35.5 %collective-permute-start.12 = (bf16[4,32,4608]{2,1,0:T(8,128)(2,1)}, bf16[4,32,4608]{2,1,0:T(8,128)(2,1)}, u32[]{:S(2)}, u32[]{:S(2)}) collective-permute-start(bf16[4,32,4608]{2,1,0:T(8,128)(2,1)} %get-tuple-element.701), channel_id=1, source_target_pairs={{0,4},{4,0},{8,12},{12,8},{16,20},{20,16},{24,28},{28,24},{1,5},{5... | collective-permute-start | bytes 3538952 | tf_op jit(solution)/shard_map/ppermute | solution.py:70
  112.6 37.8 %collective-permute-start.13 = (bf16[4,32,4608]{2,1,0:T(8,128)(2,1)}, bf16[4,32,4608]{2,1,0:T(8,128)(2,1)}, u32[]{:S(2)}, u32[]{:S(2)}) collective-permute-start(bf16[4,32,4608]{2,1,0:T(8,128)(2,1)} %get-tuple-element.700), channel_id=1, source_target_pairs={{0,2},{1,3},{2,0},{3,1},{4,6},{5,7},{6,4},{7,5},{8,10},{9,11},{10,... | collective-permute-start | bytes 3538952 | tf_op jit(solution)/shard_map/ppermute | solution.py:72
  147.5 52.3 %collective-permute-start.14 = (bf16[2,4,32,4608]{3,2,1,0:T(8,128)(2,1)}, bf16[2,4,32,4608]{3,2,1,0:T(8,128)(2,1)}, u32[]{:S(2)}, u32[]{:S(2)}) collective-permute-start(bf16[2,4,32,4608]{3,2,1,0:T(8,128)(2,1)} %pad_maximum_fusion.1.refs_0_), channel_id=1, source_target_pairs={{0,2},{1,3},{2,0},{3,1},{4,6},{5,7},{6,4},{7,5},{8,10},{9,11},{10,... | collective-permute-start | bytes 7077896 | tf_op jit(solution)/shard_map/ppermute | solution.py:72
  153.3 50.9 %collective-permute-start.15 = (bf16[2,4,32,4608]{3,2,1,0:T(8,128)(2,1)}, bf16[2,4,32,4608]{3,2,1,0:T(8,128)(2,1)}, u32[]{:S(2)}, u32[]{:S(2)}) collective-permute-start(bf16[2,4,32,4608]{3,2,1,0:T(8,128)(2,1)} %pad_maximum_fusion.2.refs_2_), channel_id=1, source_target_pairs={{0,4},{4,0},{8,12},{12,8},{16,20},{20,16},{24,28},{28,24},{1,5},{5... | collective-permute-start | bytes 7077896 | tf_op jit(solution)/shard_map/ppermute | solution.py:70
  174.4 30.6 %collective-permute-start.16 = (bf16[2,4,32,4608]{3,2,1,0:T(8,128)(2,1)}, bf16[2,4,32,4608]{3,2,1,0:T(8,128)(2,1)S(1)}, u32[]{:S(2)}, u32[]{:S(2)}) collective-permute-start(bf16[2,4,32,4608]{3,2,1,0:T(8,128)(2,1)} %pad_maximum_fusion.1.refs_0_), channel_id=1, source_target_pairs={{0,1},{1,0},{2,3},{3,2},{4,5},{5,4},{6,7},{7,6},{8,9},{9,8},{10,11... | collective-permute-start | bytes 7077896 | tf_op jit(solution)/shard_map/ppermute | solution.py:72
  174.5 30.6 %collective-permute-start.18 = (bf16[2,4,32,4608]{3,2,1,0:T(8,128)(2,1)}, bf16[2,4,32,4608]{3,2,1,0:T(8,128)(2,1)S(1)}, u32[]{:S(2)}, u32[]{:S(2)}) collective-permute-start(bf16[2,4,32,4608]{3,2,1,0:T(8,128)(2,1)} %pad_maximum_fusion.2.refs_2_), channel_id=1, source_target_pairs={{0,1},{1,0},{2,3},{3,2},{4,5},{5,4},{6,7},{7,6},{8,9},{9,8},{10,11... | collective-permute-start | bytes 7077896 | tf_op jit(solution)/shard_map/ppermute | solution.py:72
  421.9 36.2 %collective-permute-start.49 = (bf16[64,1024]{1,0:T(8,128)(2,1)}, bf16[64,1024]{1,0:T(8,128)(2,1)}, u32[]{:S(2)}, u32[]{:S(2)}) collective-permute-start(bf16[64,1024]{1,0:T(8,128)(2,1)} %fusion.159), channel_id=1, source_target_pairs={{0,2},{1,3},{2,0},{3,1},{4,6},{5,7},{6,4},{7,5},{8,10},{9,11},{10,... | collective-permute-start | bytes 393224 | tf_op jit(solution)/shard_map/ppermute | solution.py:72
  422.4 39.2 %collective-permute-start.50 = (bf16[64,1024]{1,0:T(8,128)(2,1)}, bf16[64,1024]{1,0:T(8,128)(2,1)}, u32[]{:S(2)}, u32[]{:S(2)}) collective-permute-start(bf16[64,1024]{1,0:T(8,128)(2,1)} %fusion.159), channel_id=1, source_target_pairs={{0,4},{4,0},{8,12},{12,8},{16,20},{20,16},{24,28},{28,24},{1,5},{5... | collective-permute-start | bytes 393224 | tf_op jit(solution)/shard_map/ppermute | solution.py:70
  431.1 35.4 %collective-permute-start.47 = (bf16[2,64,2560]{2,1,0:T(8,128)(2,1)}, bf16[2,64,2560]{2,1,0:T(8,128)(2,1)}, u32[]{:S(2)}, u32[]{:S(2)}) collective-permute-start(bf16[2,64,2560]{2,1,0:T(8,128)(2,1)} %pad_maximum_fusion.9.refs_0_), channel_id=1, source_target_pairs={{0,2},{1,3},{2,0},{3,1},{4,6},{5,7},{6,4},{7,5},{8,10},{9,11},{10,... | collective-permute-start | bytes 1966088 | tf_op jit(solution)/shard_map/ppermute | solution.py:72
  446.4 32.4 %collective-permute-start.52 = (bf16[512,3072]{1,0:T(8,128)(2,1)}, bf16[512,3072]{1,0:T(8,128)(2,1)}, u32[]{:S(2)}, u32[]{:S(2)}) collective-permute-start(bf16[512,3072]{1,0:T(8,128)(2,1)} %convolution_convert_fusion.1), channel_id=1, source_target_pairs={{0,1},{1,0},{2,3},{3,2},{4,5},{5,4},{6,7},{7,6},{8,9},{9,8},{10,11... | collective-permute-start | bytes 9437192 | tf_op jit(solution)/shard_map/ppermute | solution.py:72
  467.4 72.5 %all-to-all-start.6 = ((bf16[32,40,1024]{2,1,0:T(8,128)(2,1)}), bf16[32,40,1024]{2,1,0:T(8,128)(2,1)}, u32[]{:S(2)}, u32[]{:S(2)}) async-start(bf16[32,40,1024]{2,1,0:T(8,128)(2,1)} %bitcast.344), calls=%async_computation.6 | async-start | bytes 5242880 | tf_op jit(solution)/shard_map/all_to_all | solution.py:89
  491.2 27.9 %collective-permute-start.60 = (bf16[2,4,32,1536]{3,2,1,0:T(8,128)(2,1)S(1)}, bf16[2,4,32,1536]{3,2,1,0:T(8,128)(2,1)S(1)}, u32[]{:S(2)}, u32[]{:S(2)}) collective-permute-start(bf16[2,4,32,1536]{3,2,1,0:T(8,128)(2,1)S(1)} %dynamic-slice_bitcast_fusion.1), channel_id=1, source_target_pairs={{0,4},{4,0},{8,12},{12,8},{16,20},{20,16},{24,28},{28,24},{1,5},{5... | collective-permute-start | bytes 2359304 | tf_op jit(solution)/shard_map/ppermute | solution.py:70
  503.3 36.4 %collective-permute-start.59 = (bf16[2,32,4096]{2,1,0:T(8,128)(2,1)S(1)}, bf16[2,32,4096]{2,1,0:T(8,128)(2,1)S(1)}, u32[]{:S(2)}, u32[]{:S(2)}) collective-permute-start(bf16[2,32,4096]{2,1,0:T(8,128)(2,1)S(1)} %dynamic-slice_bitcast_fusion.3), channel_id=1, source_target_pairs={{0,8},{4,12},{8,0},{12,4},{16,24},{20,28},{24,16},{28,20},{1,9},{5... | collective-permute-start | bytes 1572872 | tf_op jit(solution)/shard_map/ppermute | solution.py:75
  546.5 40.8 %collective-permute-start.66 = (bf16[1,32,4096]{2,1,0:T(8,128)(2,1)}, bf16[1,32,4096]{2,1,0:T(8,128)(2,1)}, u32[]{:S(2)}, u32[]{:S(2)}) collective-permute-start(bf16[1,32,4096]{2,1,0:T(8,128)(2,1)} %dynamic-slice_convert_fusion.1), channel_id=1, source_target_pairs={{0,16},{4,20},{8,24},{12,28},{16,0},{20,4},{24,8},{28,12},{1,17},{... | collective-permute-start | bytes 786440 | tf_op jit(solution)/shard_map/ppermute | solution.py:75
  548.6 40.5 %collective-permute-start.67 = (bf16[1,128,1024]{2,1,0:T(8,128)(2,1)}, bf16[1,128,1024]{2,1,0:T(8,128)(2,1)}, u32[]{:S(2)}, u32[]{:S(2)}) collective-permute-start(bf16[1,128,1024]{2,1,0:T(8,128)(2,1)} %dynamic-slice_convert_fusion.2), channel_id=1, source_target_pairs={{0,16},{4,20},{8,24},{12,28},{16,0},{20,4},{24,8},{28,12},{1,17},{... | collective-permute-start | bytes 786440 | tf_op jit(solution)/shard_map/ppermute | solution.py:75
  (156 other events, 2077.7 us)

commit v5 on v4

--- a/solution.py
+++ b/solution.py
@@ -458,6 +458,27 @@
 grid_steps = 4
 
 
+def unfold(whole, count, width, shard_rows):
+    devices = whole.shape[0] // shard_rows
+    group = max(1, min(devices, 256 // shard_rows))
+
+    def kernel(source_ref, target_ref):
+        for number in range(count):
+            block = source_ref[:, number * width : (number + 1) * width]
+            target_ref[:, number] = block.reshape(group, shard_rows, width)
+
+    rows = pl.pallas_call(
+        kernel,
+        grid=(devices // group,),
+        in_specs=[pl.BlockSpec((group * shard_rows, count * width), lambda i: (i, 0))],
+        out_specs=pl.BlockSpec((group, count, shard_rows, width), lambda i: (i, 0, 0, 0)),
+        out_shape=jax.ShapeDtypeStruct((devices, count, shard_rows, width), whole.dtype),
+        compiler_params=pltpu.CompilerParams(vmem_limit_bytes=32 * 2**20),
+        name="unfold",
+    )(whole)
+    return rows.reshape(-1, width)
+
+
 row_block = 256
 
 
@@ -839,14 +860,16 @@
     targets = targets.reshape(links.depth, 2, 2, 2, pick_total).transpose(3, 1, 2, 0, 4).reshape(-1)
     fold_count = down_master.shape[0] // shard_rows
     second_shard = jnp.concatenate(
-        [up_master, out_master]
-        + [
+        [
             down_master[number * shard_rows : (number + 1) * shard_rows]
             for number in range(fold_count)
-        ],
+        ]
+        + [up_master, out_master],
         axis=1,
     )
-    second_near = links.gather_early(after(second_shard, first_early).astype(bf16))
+    second_whole = lax.all_gather(
+        second_shard.astype(bf16), ("wide", "narrow"), axis=0, tiled=True
+    )
     first_parts = links.plane_first(first_near)
     found = after(find(asked_first), first_near)
     landed = links.to_all(found)
@@ -854,8 +877,6 @@
     weight_row = weight_squares(tie(*masters, found)[:6])
     first_pieces[0] = after(first_pieces[0], weight_row, table_low)
     first_whole = links.assemble(links.plane_core(first_pieces))
-    second_near = links.gather_late(after(second_near, *first_parts))
-    second_parts = links.plane_first(after(second_near, *first_pieces))
     qkv_weight = first_whole[:, :qkv_width]
     gain_entries = first_whole[:, qkv_width : qkv_width + 6].astype(f32).T
 
@@ -872,7 +893,6 @@
 
     x_embed = x_low.astype(f32)
     normed_one = layer_norm(x_embed, gain_entries[0], gain_entries[1]).astype(bf16)
-    normed_one = after(normed_one, *second_parts)
     qkv_all = matmul(normed_one, qkv_weight).astype(bf16)
     pick_rows = (
         pick_hits[:, :, None, :] & jnp.eye(micro_count, dtype=bool)[:, None, :, None]
@@ -884,13 +904,11 @@
     context, queries, probs = attend(
         qkv_all, pick_rows, allowed.reshape(pick_total, length).astype(f32), micro_count
     )
-    second_pieces = links.plane_second(*second_parts)
-    second_whole, down_weight = links.assemble(
-        links.plane_core([after(piece, context) for piece in second_pieces]),
-        folded=(fold_count, model_width),
-    )
+    down_weight = unfold(second_whole, fold_count, model_width, shard_rows)
     hidden = up_master.shape[1]
-    up_weight, out_weight = second_whole[:, :hidden], second_whole[:, hidden:]
+    folded = fold_count * model_width
+    up_weight = second_whole[:, folded : folded + hidden]
+    out_weight = second_whole[:, folded + hidden :]
     x_attn = x_embed_picked + matmul(context, out_weight)
     normed_two = layer_norm(x_attn, gain_entries[2], gain_entries[3]).astype(bf16)
     up_value = matmul(normed_two, up_weight)

time: 671 us -> 648 us (0.966)
  waiting for transfers between devices: 249 us -> 233 us
  Pallas kernels: 114 us -> 99.2 us
  between operations: 6.61 us -> 20.3 us
  other arithmetic: 65 us -> 54.4 us
    ppermute x14 -> x12, waiting for transfers between devices: 95.5 us -> 58.1 us  [cross(): lax.ppermute(values, 'wide', [(i, i ^ 2 * step) for i in range(self.wide)])]
    all_gather x0 -> x1, waiting for transfers between devices: none -> 11.6 us  [per_device(): lax.all_gather(second_shard.astype(bf16), ('wide', 'narrow'), axis=0, til...]
    pallas_call x2, Pallas kernels: 30.8 us -> 19.9 us  [head_grads(): pl.pallas_call(kernel, out_shape=(jax.ShapeDtypeStruct((row_count // 2, c...]
    all_to_all x6, waiting for transfers between devices: 17.5 us -> 26.3 us  [to_all(): return lax.all_to_all(values, ('wide', 'narrow'), 0, 0, tiled=True)]
    pallas_call x3 -> x2, Pallas kernels: 16.2 us -> 7.91 us  [assemble(): pl.pallas_call(kernel, out_shape=shapes, grid_spec=pltpu.PrefetchScalarGr...]
    ppermute x34 -> x28, starting transfers between devices: 22.2 us -> 16.1 us  [swap(): lax.ppermute(values, 'narrow', [(i, i ^ step) for i in range(self.narrow)])]
    ppermute x14 -> x12, waiting for transfers between devices: 64.9 us -> 66.5 us  [swap(): return lax.ppermute(values, 'wide', [(i, i ^ 1) for i in range(self.wide)])]
    ppermute x14 -> x12, starting transfers between devices: 14.6 us -> 15.7 us  [swap(): return lax.ppermute(values, 'wide', [(i, i ^ 1) for i in range(self.wide)])]
  transfers between devices with their start and end apart: 74 -> 65, of which waited for: 41 -> 38; matrix products, arithmetic and copies ran while one was open for 23% -> 22% of each run, Pallas kernels for 3% -> 3%
where the time goes in v5:
time: 648 us; the launch traced here: 640 us
  waiting for transfers between devices  233 us (36%)
  Pallas kernels  99.2 us (15%)
  matrix products  91.8 us (14%)
  starting transfers between devices  76.1 us (12%)
  local copies, waits for them, and re-layouts  64.9 us (10%)
  other arithmetic  54.4 us (8%)
  between operations  20.3 us (3%)
    ppermute x12, waiting for transfers between devices, swap(): return lax.ppermute(values, 'wide', [(i, i ^ 1) for i in range(self.wide)])  66.5 us
    ppermute x12, waiting for transfers between devices, cross(): lax.ppermute(values, 'wide', [(i, i ^ 2 * step) for i in range(self.wide)])  58.1 us
    ppermute x28, waiting for transfers between devices, swap(): lax.ppermute(values, 'narrow', [(i, i ^ step) for i in range(self.narrow)])  54.3 us
    dot_general x10, matrix products, matmul(): return jnp.dot(left_side, right_side, preferred_element_type=f32)  41.2 us
    dot_general x5, matrix products, contract_rows(): lax.dot_general(left_side, right_side, (((0,), (0,)), ((), ())), preferre...  26.3 us
    all_to_all x6, waiting for transfers between devices, to_all(): return lax.all_to_all(values, ('wide', 'narrow'), 0, 0, tiled=True)  26.3 us
    unnamed x285, local copies, waits for them, and re-layouts  26.2 us
    dot_general x4, matrix products, contract_cols(): lax.dot_general(left_side, right_side, (((1,), (1,)), ((), ())), preferre...  23.1 us
  transfers between devices with their start and end apart: 65, of which 38 were waited for; matrix products, arithmetic and copies ran while one was open for 22% of the time, Pallas kernels for 3%

profile of v5, /device:TPU:0, one launch (start us, length us, event | category | flops | bytes accessed | tf_op | source)
XLA Modules:
  0.0 639.8 jit_solution(3055467553014008401)
XLA Ops:
  31.1 8.3 %fusion.32 = bf16[1280,1024]{1,0:T(8,128)(2,1)} fusion(s32[1280]{0:T(1024)S(1)} %eq.368, bf16[1572,1024]{1,0:T(8,128)(2,1)} %convert.59), kind=kOutput, calls=%fused_computation.53 | convolution fusion | flops 4365516800 | bytes 5846016 | tf_op jit(solution)/shard_map/dot_general | solution.py:42
  39.4 8.5 %collective-permute-done.1 = bf16[2,32,3200]{2,1,0:T(8,128)(2,1)S(1)} collective-permute-done((bf16[2,32,3200]{2,1,0:T(8,128)(2,1)S(1)}, bf16[2,32,3200]{2,1,0:T(8,128)(2,1)S(1)}, u32[]{:S(2)}, u32[]{:S(2)}) %collective-permute-start.1) | collective-permute-done | bytes 409632 | tf_op jit(solution)/shard_map/ppermute | solution.py:75
  56.2 30.8 %collective-permute-done.4 = bf16[4,32,1664]{2,1,0:T(8,128)(2,1)S(1)} collective-permute-done((bf16[4,32,1664]{2,1,0:T(8,128)(2,1)S(1)}, bf16[4,32,1664]{2,1,0:T(8,128)(2,1)S(1)}, u32[]{:S(2)}, u32[]{:S(2)}) %collective-permute-start.4) | collective-permute-done | bytes 426016 | tf_op jit(solution)/shard_map/ppermute | solution.py:72
  89.7 10.7 %collective-permute-done.2 = bf16[4,32,1536]{2,1,0:T(8,128)(2,1)S(1)} collective-permute-done((bf16[4,32,1536]{2,1,0:T(8,128)(2,1)S(1)}, bf16[4,32,1536]{2,1,0:T(8,128)(2,1)S(1)}, u32[]{:S(2)}, u32[]{:S(2)}) %collective-permute-start.2) | collective-permute-done | bytes 393248 | tf_op jit(solution)/shard_map/ppermute | solution.py:70
  102.0 20.9 %collective-permute-done.5.refs_3_ = bf16[2,4,32,1664]{3,2,1,0:T(8,128)(2,1)} collective-permute-done((bf16[2,4,32,1664]{3,2,1,0:T(8,128)(2,1)S(1)}, bf16[2,4,32,1664]{3,2,1,0:T(8,128)(2,1)}, u32[]{:S(2)}, u32[]{:S(2)}) %collective-permute-start.5) | collective-permute-done | bytes 852000 | tf_op jit(solution)/shard_map/ppermute | solution.py:70
  145.4 10.1 %all-to-all-done.5 = bf16[32,40,1024]{2,1,0:T(8,128)(2,1)} async-done(((bf16[32,40,1024]{2,1,0:T(8,128)(2,1)}), bf16[32,40,1024]{2,1,0:T(8,128)(2,1)}, u32[]{:S(2)}, u32[]{:S(2)}) %all-to-all-start.5) | async-done | bytes 2621472 | tf_op jit(solution)/shard_map/all_to_all | solution.py:89
  163.8 6.8 %fusion.25.qkv_ref = bf16[512,3072]{1,0:T(8,128)(2,1)S(1)} fusion(bf16[1024,3200]{1,0:T(8,128)(2,1)} %bitcast.322, bf16[512,1024]{1,0:T(8,128)(2,1)} %get-tuple-element.352, f32[1024]{0:T(1024)S(1)} %bitcast.409, f32[1024]{0:T(1024)S(1)} %bitcast.401, f32[512]{0:T(512)S(1)} %fusion.155, f32[512]{0:T(512)S(1)} %broadcast_multiply_fusion), kind=kOutput, calls=%fused_computation.45 | convolution fusion | flops 3225944064 | bytes 10498048 | tf_op jit(solution)/shard_map/dot_general | solution.py:42
  178.1 11.6 %all-gather.2.cloned.1.call-done.source_ref = bf16[1024,9216]{1,0:T(8,128)(2,1)} async-done(((bf16[32,9216]{1,0:T(8,128)(2,1)}), bf16[1024,9216]{1,0:T(8,128)(2,1)}) %all-gather.2.cloned.1.call-update) | async-done | bytes 18874384 | tf_op jit(solution)/shard_map/all_gather | solution.py:870
  197.2 8.0 %fusion.19 = f32[64,4096]{1,0:T(8,128)S(1)} fusion(bf16[1024,9216]{1,0:T(8,128)(2,1)} %all-gather.2.cloned.1.call-done.source_ref, f32[64,1024]{1,0:T(8,128)S(1)} %get-tuple-element.724, f32[1024]{0:T(1024)S(1)} %bitcast.413, f32[1024]{0:T(1024)S(1)} %bitcast.392, f32[64]{0:T(128)S(1)} %fusion.156, f32[64]{0:T(128)S(1)} %broadcast_multiply_fusion.2), kind=kOutput, calls=%fused_computation.36 | convolution fusion | flops 537198592 | bytes 9708032 | tf_op jit(solution)/shard_map/dot_general | solution.py:42
  207.9 7.9 %collective-permute-done.10 = bf16[1,64,1024]{2,1,0:T(8,128)(2,1)S(1)} collective-permute-done((bf16[1,64,1024]{2,1,0:T(8,128)(2,1)S(1)}, bf16[1,64,1024]{2,1,0:T(8,128)(2,1)S(1)}, u32[]{:S(2)}, u32[]{:S(2)}) %collective-permute-start.10) | collective-permute-done | bytes 131104 | tf_op jit(solution)/shard_map/ppermute | solution.py:75
  215.9 8.2 %collective-permute-done.11 = bf16[2,64,1024]{2,1,0:T(8,128)(2,1)S(1)} collective-permute-done((bf16[2,64,1024]{2,1,0:T(8,128)(2,1)S(1)}, bf16[2,64,1024]{2,1,0:T(8,128)(2,1)S(1)}, u32[]{:S(2)}, u32[]{:S(2)}) %collective-permute-start.11) | collective-permute-done | bytes 262176 | tf_op jit(solution)/shard_map/ppermute | solution.py:75
  237.4 7.9 %collective-permute-done.13.refs_1_ = bf16[2,4,64,512]{3,2,1,0:T(8,128)(2,1)} collective-permute-done((bf16[2,4,64,512]{3,2,1,0:T(8,128)(2,1)}, bf16[2,4,64,512]{3,2,1,0:T(8,128)(2,1)}, u32[]{:S(2)}, u32[]{:S(2)}) %collective-permute-start.13) | collective-permute-done | bytes 524320 | tf_op jit(solution)/shard_map/ppermute | solution.py:72
  255.8 16.7 %head_logits.1 = (f32[2048,1664]{1,0:T(8,128)}, f32[1,2048]{1,0:T(1,128)}, f32[1,2048]{1,0:T(1,128)}, f32[1,128]{1,0:T(1,128)}) custom-call(s32[1]{0:T(128)} %bitcast.base_ref, bf16[2048,1024]{1,0:T(8,128)(2,1)} %bitcast.318, bf16[1664,1024]{1,0:T(8,128)(2,1)S(1)} %copy-done.19, s32[2048,1]{1,0:T(8,128)} %broadcast_in_dim_reshape.3.targets_ref), custom_call_target="tpu_custom_call" | custom-call | tf_op jit(solution)/shard_map/head_logits/pallas_call | solution.py:509
  294.6 10.1 %head_grads.2 = (bf16[1024,1664]{1,0:T(8,128)(2,1)}, bf16[1024,1024]{1,0:T(8,128)(2,1)}) custom-call(s32[2]{0:T(128)} %pad_add_fusion.place_ref, f32[2048,1664]{1,0:T(8,128)} %get-tuple-element.363.logits_ref, f32[1,2048]{1,0:T(1,128)} %get-tuple-element.703.total_ref, bf16[1664,1024]{1,0:T(8,128)(2,1)} %get-tuple-element.1030, ...), custom_call_target="tpu_custom_call" | custom-call | tf_op jit(solution)/shard_map/head_grads/pallas_call | solution.py:557
  309.2 9.8 %head_grads.3 = (bf16[1024,1664]{1,0:T(8,128)(2,1)}, bf16[1024,1024]{1,0:T(8,128)(2,1)}) custom-call(s32[2]{0:T(128)} %pad_add_fusion.1.place_ref, f32[2048,1664]{1,0:T(8,128)} %get-tuple-element.363.logits_ref, f32[1,2048]{1,0:T(1,128)} %get-tuple-element.703.total_ref, bf16[1664,1024]{1,0:T(8,128)(2,1)S(1)} %copy-done.20, ...), custom_call_target="tpu_custom_call" | custom-call | tf_op jit(solution)/shard_map/head_grads/pallas_call | solution.py:557
  377.8 6.8 %multiply_reduce_fusion.1 = (f32[1024]{0:T(1024)}, f32[64]{0:T(128)S(1)}, f32[1024]{0:T(1024)}, f32[64,1024]{1,0:T(8,128)S(1)}) fusion(f32[64,1024]{1,0:T(8,128)S(1)} %copy-done.26, f32[64]{0:T(128)S(1)} %copy-done.125, f32[64]{0:T(128)S(1)} %copy-done.120, f32[1024]{0:T(1024)S(1)} %bitcast.394, bf16[64,4096]{1,0:T(8,128)(2,1)S(1)} %fusion.81, ...), kind=kOutput, calls=%fused_computation.194 | convolution fusion | flops 537393088 | bytes 9450240 | tf_op jit(solution)/shard_map/dot_general | solution.py:52
  405.5 6.9 %convolution_convert_fusion.1 = bf16[512,3072]{1,0:T(8,128)(2,1)} fusion(bf16[512,3072]{1,0:T(8,128)(2,1)} %copy-done.8, s32[512]{0:T(512)S(1)} %multiply_add_fusion.4, bf16[512,1024]{1,0:T(8,128)(2,1)} %get-tuple-element.352, f32[1024]{0:T(1024)S(1)} %bitcast.410, f32[1024]{0:T(1024)S(1)} %bitcast.402, f32[512]{0:T(512)S(1)} %copy-done.100, ...), kind=kOutput, calls=%fused_computation.46 | convolution fusion | flops 2152988672 | bytes 7354368 | tf_op jit(solution)/shard_map/dot_general | solution.py:46
  413.0 7.6 %fusion.45 = (f32[1024]{0:T(1024)}, f32[512]{0:T(512)S(1)}, f32[1024]{0:T(1024)S(1)}, f32[512,1024]{1,0:T(8,128)S(1)}) fusion(bf16[512,1024]{1,0:T(8,128)(2,1)S(1)} %copy-done.22, f32[512]{0:T(512)S(1)} %copy-done.100, f32[512]{0:T(512)S(1)} %copy-done.86, f32[1024]{0:T(1024)S(1)} %bitcast.403, bf16[512,3072]{1,0:T(8,128)(2,1)} %copy-done.8, ...), kind=kOutput, calls=%fused_computation.72 | convolution fusion | flops 3225941504 | bytes 12601344 | tf_op jit(solution)/shard_map/dot_general | solution.py:52
  445.3 6.9 %add_convert_fusion = bf16[512,3072]{1,0:T(8,128)(2,1)} fusion(bf16[512,3072]{1,0:T(8,128)(2,1)} %collective-permute-done.42, bf16[512,3072]{1,0:T(8,128)(2,1)S(1)} %copy-done.9, s32[512]{0:T(512)S(1)} %multiply_add_fusion.5, bf16[512,1024]{1,0:T(8,128)(2,1)} %get-tuple-element.352, f32[1024]{0:T(1024)S(1)} %bitcast.411, f32[1024]{0:T(1024)S(1)} %bitcast.405, ...), kind=kOutput, calls=%fused_computation.40 | convolution fusion | flops 2156134400 | bytes 10500096 | tf_op jit(solution)/shard_map/dot_general | solution.py:46
  470.8 14.9 %collective-permute-done.50 = bf16[2,4,32,1536]{3,2,1,0:T(8,128)(2,1)S(1)} collective-permute-done((bf16[2,4,32,1536]{3,2,1,0:T(8,128)(2,1)S(1)}, bf16[2,4,32,1536]{3,2,1,0:T(8,128)(2,1)S(1)}, u32[]{:S(2)}, u32[]{:S(2)}) %collective-permute-start.50) | collective-permute-done | bytes 786464 | tf_op jit(solution)/shard_map/ppermute | solution.py:70
  493.1 13.3 %collective-permute-done.49 = bf16[2,32,4096]{2,1,0:T(8,128)(2,1)S(1)} collective-permute-done((bf16[2,32,4096]{2,1,0:T(8,128)(2,1)S(1)}, bf16[2,32,4096]{2,1,0:T(8,128)(2,1)S(1)}, u32[]{:S(2)}, u32[]{:S(2)}) %collective-permute-start.49) | collective-permute-done | bytes 524320 | tf_op jit(solution)/shard_map/ppermute | solution.py:75
  557.5 10.4 %collective-permute-done.55 = bf16[1,32,4096]{2,1,0:T(8,128)(2,1)S(1)} collective-permute-done((bf16[1,32,4096]{2,1,0:T(8,128)(2,1)S(1)}, bf16[1,32,4096]{2,1,0:T(8,128)(2,1)S(1)}, u32[]{:S(2)}, u32[]{:S(2)}) %collective-permute-start.55) | collective-permute-done | bytes 262176 | tf_op jit(solution)/shard_map/ppermute | solution.py:75
  585.9 21.1 %lamb_directions.1 = (f32[1572,1024]{1,0:T(8,128)}, f32[32,3072]{1,0:T(8,128)}, f32[32,1024]{1,0:T(8,128)}, f32[32,4096]{1,0:T(8,128)}, f32[128,1024]{1,0:T(8,12...) custom-call(f32[32,256]{1,0:T(8,128)} %bitcast.360, ...), custom_call_target="tpu_custom_call" | custom-call | tf_op jit(solution)/shard_map/lamb_directions/pallas_call | solution.py:689
  617.3 8.9 %lamb_weights.1 = (f32[1572,1024]{1,0:T(8,128)}, f32[32,3072]{1,0:T(8,128)}, f32[32,1024]{1,0:T(8,128)}, f32[32,4096]{1,0:T(8,128)}, f32[128,1024]{1,0:T(8,128)}, /*index=5*/f32[32,6]{1,0:T(8,128)}, f32[8,128]{1,0:T(8,128)}) custom-call(f32[32,256]{1,0:T(8,128)} %bitcast.361, f32[32,128]{1,0:T(8,128)} %bitcast.375, f32[1572,1024]{1,0:T(8,128)} %get-tuple-element.394.refs_0_, ...), custom_call_target="tpu_custom_call" | custom-call | tf_op jit(solution)/shard_map/lamb_weights/pallas_call | solution.py:731
  (594 shorter events, 346.1 us)
Async XLA Ops:
  7.2 182.4 %all-gather.2.cloned.1.call-start = ((), (), s32[]{:S(2)}) async-start(), calls=%async_computation.10 | async-start | bytes 19464192 | tf_op jit(solution)/shard_map/all_gather | solution.py:870
  11.5 18.9 %collective-permute-start = (bf16[1,32,3200]{2,1,0:T(8,128)(2,1)S(1)}, bf16[1,32,3200]{2,1,0:T(8,128)(2,1)S(1)}, u32[]{:S(2)}, u32[]{:S(2)}) collective-permute-start(bf16[1,32,3200]{2,1,0:T(8,128)(2,1)S(1)} %pad_maximum_fusion.14), channel_id=1, source_target_pairs={{0,16},{4,20},{8,24},{12,28},{16,0},{20,4},{24,8},{28,12},{1,17},{... | collective-permute-start | bytes 614408 | tf_op jit(solution)/shard_map/ppermute | solution.py:75
  30.5 17.4 %collective-permute-start.1 = (bf16[2,32,3200]{2,1,0:T(8,128)(2,1)S(1)}, bf16[2,32,3200]{2,1,0:T(8,128)(2,1)S(1)}, u32[]{:S(2)}, u32[]{:S(2)}) collective-permute-start(bf16[2,32,3200]{2,1,0:T(8,128)(2,1)S(1)} %pad_maximum_fusion.11), channel_id=1, source_target_pairs={{0,8},{4,12},{8,0},{12,4},{16,24},{20,28},{24,16},{28,20},{1,9},{5... | collective-permute-start | bytes 1228808 | tf_op jit(solution)/shard_map/ppermute | solution.py:75
  48.0 107.6 %all-to-all-start.5 = ((bf16[32,40,1024]{2,1,0:T(8,128)(2,1)}), bf16[32,40,1024]{2,1,0:T(8,128)(2,1)}, u32[]{:S(2)}, u32[]{:S(2)}) async-start(bf16[32,40,1024]{2,1,0:T(8,128)(2,1)} %bitcast.330), calls=%async_computation.5 | async-start | bytes 5242880 | tf_op jit(solution)/shard_map/all_to_all | solution.py:89
  52.8 34.2 %collective-permute-start.4 = (bf16[4,32,1664]{2,1,0:T(8,128)(2,1)S(1)}, bf16[4,32,1664]{2,1,0:T(8,128)(2,1)S(1)}, u32[]{:S(2)}, u32[]{:S(2)}) collective-permute-start(bf16[4,32,1664]{2,1,0:T(8,128)(2,1)S(1)} %get-tuple-element.681), channel_id=1, source_target_pairs={{0,2},{1,3},{2,0},{3,1},{4,6},{5,7},{6,4},{7,5},{8,10},{9,11},{10,... | collective-permute-start | bytes 1277960 | tf_op jit(solution)/shard_map/ppermute | solution.py:72
  54.6 45.7 %collective-permute-start.2 = (bf16[4,32,1536]{2,1,0:T(8,128)(2,1)S(1)}, bf16[4,32,1536]{2,1,0:T(8,128)(2,1)S(1)}, u32[]{:S(2)}, u32[]{:S(2)}) collective-permute-start(bf16[4,32,1536]{2,1,0:T(8,128)(2,1)S(1)} %get-tuple-element.683), channel_id=1, source_target_pairs={{0,4},{4,0},{8,12},{12,8},{16,20},{20,16},{24,28},{28,24},{1,5},{5... | collective-permute-start | bytes 1179656 | tf_op jit(solution)/shard_map/ppermute | solution.py:70
  87.1 35.8 %collective-permute-start.5 = (bf16[2,4,32,1664]{3,2,1,0:T(8,128)(2,1)S(1)}, bf16[2,4,32,1664]{3,2,1,0:T(8,128)(2,1)}, u32[]{:S(2)}, u32[]{:S(2)}) collective-permute-start(bf16[2,4,32,1664]{3,2,1,0:T(8,128)(2,1)S(1)} %pad_maximum_fusion.1.refs_2_), channel_id=1, source_target_pairs={{0,4},{4,0},{8,12},{12,8},{16,20},{20,16},{24,28},{28,24},{1,5},{5... | collective-permute-start | bytes 2555912 | tf_op jit(solution)/shard_map/ppermute | solution.py:70
  100.4 34.1 %collective-permute-start.3 = (bf16[2,4,32,1536]{3,2,1,0:T(8,128)(2,1)S(1)}, bf16[2,4,32,1536]{3,2,1,0:T(8,128)(2,1)}, u32[]{:S(2)}, u32[]{:S(2)}) collective-permute-start(bf16[2,4,32,1536]{3,2,1,0:T(8,128)(2,1)S(1)} %pad_maximum_fusion.3.refs_0_), channel_id=1, source_target_pairs={{0,2},{1,3},{2,0},{3,1},{4,6},{5,7},{6,4},{7,5},{8,10},{9,11},{10,... | collective-permute-start | bytes 2359304 | tf_op jit(solution)/shard_map/ppermute | solution.py:72
  102.0 36.1 %collective-permute-start.8 = (bf16[2,4,32,1664]{3,2,1,0:T(8,128)(2,1)S(1)}, bf16[2,4,32,1664]{3,2,1,0:T(8,128)(2,1)}, u32[]{:S(2)}, u32[]{:S(2)}) collective-permute-start(bf16[2,4,32,1664]{3,2,1,0:T(8,128)(2,1)S(1)} %pad_maximum_fusion.1.refs_2_), channel_id=1, source_target_pairs={{0,1},{1,0},{2,3},{3,2},{4,5},{5,4},{6,7},{7,6},{8,9},{9,8},{10,11... | collective-permute-start | bytes 2555912 | tf_op jit(solution)/shard_map/ppermute | solution.py:72
  387.8 35.0 %collective-permute-start.39 = (bf16[64,1024]{1,0:T(8,128)(2,1)}, bf16[64,1024]{1,0:T(8,128)(2,1)}, u32[]{:S(2)}, u32[]{:S(2)}) collective-permute-start(bf16[64,1024]{1,0:T(8,128)(2,1)} %fusion.159), channel_id=1, source_target_pairs={{0,2},{1,3},{2,0},{3,1},{4,6},{5,7},{6,4},{7,5},{8,10},{9,11},{10,... | collective-permute-start | bytes 393224 | tf_op jit(solution)/shard_map/ppermute | solution.py:72
  389.4 39.2 %collective-permute-start.40 = (bf16[64,1024]{1,0:T(8,128)(2,1)}, bf16[64,1024]{1,0:T(8,128)(2,1)}, u32[]{:S(2)}, u32[]{:S(2)}) collective-permute-start(bf16[64,1024]{1,0:T(8,128)(2,1)} %fusion.159), channel_id=1, source_target_pairs={{0,4},{4,0},{8,12},{12,8},{16,20},{20,16},{24,28},{28,24},{1,5},{5... | collective-permute-start | bytes 393224 | tf_op jit(solution)/shard_map/ppermute | solution.py:70
  398.0 35.4 %collective-permute-start.37 = (bf16[2,64,2560]{2,1,0:T(8,128)(2,1)}, bf16[2,64,2560]{2,1,0:T(8,128)(2,1)}, u32[]{:S(2)}, u32[]{:S(2)}) collective-permute-start(bf16[2,64,2560]{2,1,0:T(8,128)(2,1)} %pad_maximum_fusion.5.refs_0_), channel_id=1, source_target_pairs={{0,2},{1,3},{2,0},{3,1},{4,6},{5,7},{6,4},{7,5},{8,10},{9,11},{10,... | collective-permute-start | bytes 1966088 | tf_op jit(solution)/shard_map/ppermute | solution.py:72
  412.4 32.9 %collective-permute-start.42 = (bf16[512,3072]{1,0:T(8,128)(2,1)}, bf16[512,3072]{1,0:T(8,128)(2,1)}, u32[]{:S(2)}, u32[]{:S(2)}) collective-permute-start(bf16[512,3072]{1,0:T(8,128)(2,1)} %convolution_convert_fusion.1), channel_id=1, source_target_pairs={{0,1},{1,0},{2,3},{3,2},{4,5},{5,4},{6,7},{7,6},{8,9},{9,8},{10,11... | collective-permute-start | bytes 9437192 | tf_op jit(solution)/shard_map/ppermute | solution.py:72
  412.5 21.0 %collective-permute-start.38 = (bf16[2,64,2560]{2,1,0:T(8,128)(2,1)S(1)}, bf16[2,64,2560]{2,1,0:T(8,128)(2,1)S(1)}, u32[]{:S(2)}, u32[]{:S(2)}) collective-permute-start(bf16[2,64,2560]{2,1,0:T(8,128)(2,1)S(1)} %pad_maximum_fusion.6.refs_1_), channel_id=1, source_target_pairs={{0,4},{4,0},{8,12},{12,8},{16,20},{20,16},{24,28},{28,24},{1,5},{5... | collective-permute-start | bytes 1966088 | tf_op jit(solution)/shard_map/ppermute | solution.py:70
  434.4 72.2 %all-to-all-start.6 = ((bf16[32,40,1024]{2,1,0:T(8,128)(2,1)}), bf16[32,40,1024]{2,1,0:T(8,128)(2,1)}, u32[]{:S(2)}, u32[]{:S(2)}) async-start(bf16[32,40,1024]{2,1,0:T(8,128)(2,1)} %bitcast.331), calls=%async_computation.6 | async-start | bytes 5242880 | tf_op jit(solution)/shard_map/all_to_all | solution.py:89
  458.2 27.5 %collective-permute-start.50 = (bf16[2,4,32,1536]{3,2,1,0:T(8,128)(2,1)S(1)}, bf16[2,4,32,1536]{3,2,1,0:T(8,128)(2,1)S(1)}, u32[]{:S(2)}, u32[]{:S(2)}) collective-permute-start(bf16[2,4,32,1536]{3,2,1,0:T(8,128)(2,1)S(1)} %dynamic-slice_bitcast_fusion.1), channel_id=1, source_target_pairs={{0,4},{4,0},{8,12},{12,8},{16,20},{20,16},{24,28},{28,24},{1,5},{5... | collective-permute-start | bytes 2359304 | tf_op jit(solution)/shard_map/ppermute | solution.py:70
  459.8 27.9 %collective-permute-start.51 = (bf16[2,4,32,1536]{3,2,1,0:T(8,128)(2,1)S(1)}, bf16[2,4,32,1536]{3,2,1,0:T(8,128)(2,1)S(1)}, u32[]{:S(2)}, u32[]{:S(2)}) collective-permute-start(bf16[2,4,32,1536]{3,2,1,0:T(8,128)(2,1)S(1)} %dynamic-slice_bitcast_fusion), channel_id=1, source_target_pairs={{0,2},{1,3},{2,0},{3,1},{4,6},{5,7},{6,4},{7,5},{8,10},{9,11},{10,... | collective-permute-start | bytes 2359304 | tf_op jit(solution)/shard_map/ppermute | solution.py:72
  467.6 25.3 %collective-permute-start.48 = (bf16[2,128,1024]{2,1,0:T(8,128)(2,1)S(1)}, bf16[2,128,1024]{2,1,0:T(8,128)(2,1)S(1)}, u32[]{:S(2)}, u32[]{:S(2)}) collective-permute-start(bf16[2,128,1024]{2,1,0:T(8,128)(2,1)S(1)} %dynamic-slice_bitcast_fusion.4), channel_id=1, source_target_pairs={{0,8},{4,12},{8,0},{12,4},{16,24},{20,28},{24,16},{28,20},{1,9},{5... | collective-permute-start | bytes 1572872 | tf_op jit(solution)/shard_map/ppermute | solution.py:75
  470.3 36.1 %collective-permute-start.49 = (bf16[2,32,4096]{2,1,0:T(8,128)(2,1)S(1)}, bf16[2,32,4096]{2,1,0:T(8,128)(2,1)S(1)}, u32[]{:S(2)}, u32[]{:S(2)}) collective-permute-start(bf16[2,32,4096]{2,1,0:T(8,128)(2,1)S(1)} %dynamic-slice_bitcast_fusion.3), channel_id=1, source_target_pairs={{0,8},{4,12},{8,0},{12,4},{16,24},{20,28},{24,16},{28,20},{1,9},{5... | collective-permute-start | bytes 1572872 | tf_op jit(solution)/shard_map/ppermute | solution.py:75
  509.9 22.6 %collective-permute-start.53 = (bf16[4,32,1536]{2,1,0:T(8,128)(2,1)}, bf16[4,32,1536]{2,1,0:T(8,128)(2,1)}, u32[]{:S(2)}, u32[]{:S(2)}) collective-permute-start(bf16[4,32,1536]{2,1,0:T(8,128)(2,1)} %dynamic-slice_bitcast_fusion.7), channel_id=1, source_target_pairs={{0,4},{4,0},{8,12},{12,8},{16,20},{20,16},{24,28},{28,24},{1,5},{5... | collective-permute-start | bytes 1179656 | tf_op jit(solution)/shard_map/ppermute | solution.py:70
  511.3 22.3 %collective-permute-start.52 = (bf16[4,32,1536]{2,1,0:T(8,128)(2,1)S(1)}, bf16[4,32,1536]{2,1,0:T(8,128)(2,1)}, u32[]{:S(2)}, u32[]{:S(2)}) collective-permute-start(bf16[4,32,1536]{2,1,0:T(8,128)(2,1)S(1)} %dynamic-slice_bitcast_fusion.8), channel_id=1, source_target_pairs={{0,2},{1,3},{2,0},{3,1},{4,6},{5,7},{6,4},{7,5},{8,10},{9,11},{10,... | collective-permute-start | bytes 1179656 | tf_op jit(solution)/shard_map/ppermute | solution.py:72
  512.9 41.0 %collective-permute-start.56 = (bf16[1,32,4096]{2,1,0:T(8,128)(2,1)}, bf16[1,32,4096]{2,1,0:T(8,128)(2,1)}, u32[]{:S(2)}, u32[]{:S(2)}) collective-permute-start(bf16[1,32,4096]{2,1,0:T(8,128)(2,1)} %dynamic-slice_convert_fusion.1), channel_id=1, source_target_pairs={{0,16},{4,20},{8,24},{12,28},{16,0},{20,4},{24,8},{28,12},{1,17},{... | collective-permute-start | bytes 786440 | tf_op jit(solution)/shard_map/ppermute | solution.py:75
  515.2 40.5 %collective-permute-start.57 = (bf16[1,128,1024]{2,1,0:T(8,128)(2,1)}, bf16[1,128,1024]{2,1,0:T(8,128)(2,1)}, u32[]{:S(2)}, u32[]{:S(2)}) collective-permute-start(bf16[1,128,1024]{2,1,0:T(8,128)(2,1)} %dynamic-slice_convert_fusion.2), channel_id=1, source_target_pairs={{0,16},{4,20},{8,24},{12,28},{16,0},{20,4},{24,8},{28,12},{1,17},{... | collective-permute-start | bytes 786440 | tf_op jit(solution)/shard_map/ppermute | solution.py:75
  536.6 15.6 %collective-permute-start.54 = (bf16[2,32,4096]{2,1,0:T(8,128)(2,1)}, bf16[2,32,4096]{2,1,0:T(8,128)(2,1)}, u32[]{:S(2)}, u32[]{:S(2)}) collective-permute-start(bf16[2,32,4096]{2,1,0:T(8,128)(2,1)} %dynamic-slice_bitcast_fusion.2), channel_id=1, source_target_pairs={{0,8},{4,12},{8,0},{12,4},{16,24},{20,28},{24,16},{28,20},{1,9},{5... | collective-permute-start | bytes 1572872 | tf_op jit(solution)/shard_map/ppermute | solution.py:75
  (175 other events, 1804.9 us)
Sparse Core Ops, SparseCore 0:
  11.4 178.1 all-gather.1

commit v6 on v5

--- a/solution.py
+++ b/solution.py
@@ -995,7 +995,7 @@
     grad_qkv_low = attend_backward(
         qkv_all, pick_rows, queries, probs, grad_context, micro_count
     )
-    late = grad_qkv_low
+    late = after(grad_qkv_low, known, *attn_parts)
     grad_x_one, gain_one, shift_one = norm_backward(
         x_embed, gain_entries[0], gain_entries[1], contract_cols(late, qkv_weight)
     )
@@ -1008,7 +1008,7 @@
     )
     grad_embed_low = grad_x_embed.astype(bf16)
     sent = give(slot_first, grad_embed_low)
-    returned = links.to_all(after(sent, known, *grad_parts, *attn_parts))
+    returned = links.to_all(sent)
     half_place = jnp.arange(model_width // 2)
     half_row = half_place % shard_rows
     half_z = half_place // shard_rows % links.depth
@@ -1019,6 +1019,7 @@
         columns = (jnp.arange(model_width)[:, None] == source[None, :]).astype(bf16)
         return contract_rows(matmul(normed_one, columns).astype(bf16), grad_qkv_low)
 
+    grad_qkv_low = after(grad_qkv_low, sent, *attn_parts, *grad_parts)
     to_core = qkv_part(1 - core).astype(bf16)
     from_core = links.swap(to_core, "c")
     last_mine = (qkv_part(core) + from_core.astype(f32)).astype(bf16)

time: 648 us -> 645 us (level)
    ppermute x28, waiting for transfers between devices: 54.3 us -> 63.3 us  [swap(): lax.ppermute(values, 'narrow', [(i, i ^ step) for i in range(self.narrow)])]
    unnamed x285 -> x275, local copies, waits for them, and re-layouts: 26.2 us -> 26 us
  transfers between devices with their start and end apart: 65 -> 65, of which waited for: 38 -> 38; matrix products, arithmetic and copies ran while one was open for 22% -> 21% of each run, Pallas kernels for 3% -> 3%
where the time goes in v6:
time: 645 us; the launch traced here: 636 us
  waiting for transfers between devices  232 us (36%)
  Pallas kernels  99 us (15%)
  matrix products  87.6 us (14%)
  starting transfers between devices  74.1 us (11%)
  local copies, waits for them, and re-layouts  68.8 us (11%)
  other arithmetic  54 us (8%)
  between operations  20.4 us (3%)
    ppermute x12, waiting for transfers between devices, swap(): return lax.ppermute(values, 'wide', [(i, i ^ 1) for i in range(self.wide)])  64.6 us
    ppermute x28, waiting for transfers between devices, swap(): lax.ppermute(values, 'narrow', [(i, i ^ step) for i in range(self.narrow)])  63.3 us
    ppermute x12, waiting for transfers between devices, cross(): lax.ppermute(values, 'wide', [(i, i ^ 2 * step) for i in range(self.wide)])  55.9 us
    dot_general x10, matrix products, matmul(): return jnp.dot(left_side, right_side, preferred_element_type=f32)  41.2 us
    unnamed x275, local copies, waits for them, and re-layouts  26 us
    all_to_all x6, waiting for transfers between devices, to_all(): return lax.all_to_all(values, ('wide', 'narrow'), 0, 0, tiled=True)  25.8 us
    dot_general x5, matrix products, contract_rows(): lax.dot_general(left_side, right_side, (((0,), (0,)), ((), ())), preferre...  25.2 us
    all_to_all x6, starting transfers between devices, to_all(): return lax.all_to_all(values, ('wide', 'narrow'), 0, 0, tiled=True)  22.2 us
  transfers between devices with their start and end apart: 65, of which 38 were waited for; matrix products, arithmetic and copies ran while one was open for 21% of the time, Pallas kernels for 3%

profile of v6, /device:TPU:0, one launch (start us, length us, event | category | flops | bytes accessed | tf_op | source)
XLA Modules:
  0.0 636.5 jit_solution(9980500599790835721)
XLA Ops:
  31.1 8.3 %fusion.32 = bf16[1280,1024]{1,0:T(8,128)(2,1)} fusion(s32[1280]{0:T(1024)S(1)} %eq.368, bf16[1572,1024]{1,0:T(8,128)(2,1)} %convert.59), kind=kOutput, calls=%fused_computation.53 | convolution fusion | flops 4365516800 | bytes 5846016 | tf_op jit(solution)/shard_map/dot_general | solution.py:42
  39.4 8.5 %collective-permute-done.1 = bf16[2,32,3200]{2,1,0:T(8,128)(2,1)S(1)} collective-permute-done((bf16[2,32,3200]{2,1,0:T(8,128)(2,1)S(1)}, bf16[2,32,3200]{2,1,0:T(8,128)(2,1)S(1)}, u32[]{:S(2)}, u32[]{:S(2)}) %collective-permute-start.1) | collective-permute-done | bytes 409632 | tf_op jit(solution)/shard_map/ppermute | solution.py:75
  56.2 30.8 %collective-permute-done.4 = bf16[4,32,1664]{2,1,0:T(8,128)(2,1)S(1)} collective-permute-done((bf16[4,32,1664]{2,1,0:T(8,128)(2,1)S(1)}, bf16[4,32,1664]{2,1,0:T(8,128)(2,1)S(1)}, u32[]{:S(2)}, u32[]{:S(2)}) %collective-permute-start.4) | collective-permute-done | bytes 426016 | tf_op jit(solution)/shard_map/ppermute | solution.py:72
  89.7 10.7 %collective-permute-done.2 = bf16[4,32,1536]{2,1,0:T(8,128)(2,1)S(1)} collective-permute-done((bf16[4,32,1536]{2,1,0:T(8,128)(2,1)S(1)}, bf16[4,32,1536]{2,1,0:T(8,128)(2,1)S(1)}, u32[]{:S(2)}, u32[]{:S(2)}) %collective-permute-start.2) | collective-permute-done | bytes 393248 | tf_op jit(solution)/shard_map/ppermute | solution.py:70
  102.0 20.9 %collective-permute-done.5.refs_3_ = bf16[2,4,32,1664]{3,2,1,0:T(8,128)(2,1)} collective-permute-done((bf16[2,4,32,1664]{3,2,1,0:T(8,128)(2,1)S(1)}, bf16[2,4,32,1664]{3,2,1,0:T(8,128)(2,1)}, u32[]{:S(2)}, u32[]{:S(2)}) %collective-permute-start.5) | collective-permute-done | bytes 852000 | tf_op jit(solution)/shard_map/ppermute | solution.py:70
  145.4 10.1 %all-to-all-done.5 = bf16[32,40,1024]{2,1,0:T(8,128)(2,1)} async-done(((bf16[32,40,1024]{2,1,0:T(8,128)(2,1)}), bf16[32,40,1024]{2,1,0:T(8,128)(2,1)}, u32[]{:S(2)}, u32[]{:S(2)}) %all-to-all-start.5) | async-done | bytes 2621472 | tf_op jit(solution)/shard_map/all_to_all | solution.py:89
  163.7 6.9 %fusion.25.qkv_ref = bf16[512,3072]{1,0:T(8,128)(2,1)S(1)} fusion(bf16[1024,3200]{1,0:T(8,128)(2,1)} %bitcast.322, bf16[512,1024]{1,0:T(8,128)(2,1)} %get-tuple-element.353, f32[1024]{0:T(1024)S(1)} %bitcast.414, f32[1024]{0:T(1024)S(1)} %bitcast.406, f32[512]{0:T(512)S(1)} %fusion.155, f32[512]{0:T(512)S(1)} %broadcast_multiply_fusion), kind=kOutput, calls=%fused_computation.45 | convolution fusion | flops 3225944064 | bytes 10498048 | tf_op jit(solution)/shard_map/dot_general | solution.py:42
  178.1 11.6 %all-gather.2.cloned.1.call-done.source_ref = bf16[1024,9216]{1,0:T(8,128)(2,1)} async-done(((bf16[32,9216]{1,0:T(8,128)(2,1)}), bf16[1024,9216]{1,0:T(8,128)(2,1)}) %all-gather.2.cloned.1.call-update) | async-done | bytes 18874384 | tf_op jit(solution)/shard_map/all_gather | solution.py:870
  197.2 8.0 %fusion.19 = f32[64,4096]{1,0:T(8,128)S(1)} fusion(bf16[1024,9216]{1,0:T(8,128)(2,1)} %all-gather.2.cloned.1.call-done.source_ref, f32[64,1024]{1,0:T(8,128)S(1)} %get-tuple-element.726, f32[1024]{0:T(1024)S(1)} %bitcast.418, f32[1024]{0:T(1024)S(1)} %bitcast.397, f32[64]{0:T(128)S(1)} %fusion.156, f32[64]{0:T(128)S(1)} %broadcast_multiply_fusion.2), kind=kOutput, calls=%fused_computation.36 | convolution fusion | flops 537198592 | bytes 9708032 | tf_op jit(solution)/shard_map/dot_general | solution.py:42
  208.0 7.9 %collective-permute-done.10 = bf16[1,64,1024]{2,1,0:T(8,128)(2,1)S(1)} collective-permute-done((bf16[1,64,1024]{2,1,0:T(8,128)(2,1)S(1)}, bf16[1,64,1024]{2,1,0:T(8,128)(2,1)S(1)}, u32[]{:S(2)}, u32[]{:S(2)}) %collective-permute-start.10) | collective-permute-done | bytes 131104 | tf_op jit(solution)/shard_map/ppermute | solution.py:75
  216.0 8.2 %collective-permute-done.11 = bf16[2,64,1024]{2,1,0:T(8,128)(2,1)S(1)} collective-permute-done((bf16[2,64,1024]{2,1,0:T(8,128)(2,1)S(1)}, bf16[2,64,1024]{2,1,0:T(8,128)(2,1)S(1)}, u32[]{:S(2)}, u32[]{:S(2)}) %collective-permute-start.11) | collective-permute-done | bytes 262176 | tf_op jit(solution)/shard_map/ppermute | solution.py:75
  237.4 7.9 %collective-permute-done.13.refs_1_ = bf16[2,4,64,512]{3,2,1,0:T(8,128)(2,1)} collective-permute-done((bf16[2,4,64,512]{3,2,1,0:T(8,128)(2,1)}, bf16[2,4,64,512]{3,2,1,0:T(8,128)(2,1)}, u32[]{:S(2)}, u32[]{:S(2)}) %collective-permute-start.13) | collective-permute-done | bytes 524320 | tf_op jit(solution)/shard_map/ppermute | solution.py:72
  255.8 16.7 %head_logits.1 = (f32[2048,1664]{1,0:T(8,128)}, f32[1,2048]{1,0:T(1,128)}, f32[1,2048]{1,0:T(1,128)}, f32[1,128]{1,0:T(1,128)}) custom-call(s32[1]{0:T(128)} %bitcast.base_ref, bf16[2048,1024]{1,0:T(8,128)(2,1)} %bitcast.318, bf16[1664,1024]{1,0:T(8,128)(2,1)S(1)} %copy-done.21, s32[2048,1]{1,0:T(8,128)} %broadcast_in_dim_reshape.3.targets_ref), custom_call_target="tpu_custom_call" | custom-call | tf_op jit(solution)/shard_map/head_logits/pallas_call | solution.py:509
  294.6 10.1 %head_grads.2 = (bf16[1024,1664]{1,0:T(8,128)(2,1)}, bf16[1024,1024]{1,0:T(8,128)(2,1)}) custom-call(s32[2]{0:T(128)} %pad_add_fusion.place_ref, f32[2048,1664]{1,0:T(8,128)} %get-tuple-element.364.logits_ref, f32[1,2048]{1,0:T(1,128)} %get-tuple-element.705.total_ref, bf16[1664,1024]{1,0:T(8,128)(2,1)} %get-tuple-element.1034, ...), custom_call_target="tpu_custom_call" | custom-call | tf_op jit(solution)/shard_map/head_grads/pallas_call | solution.py:557
  309.2 9.8 %head_grads.3 = (bf16[1024,1664]{1,0:T(8,128)(2,1)}, bf16[1024,1024]{1,0:T(8,128)(2,1)}) custom-call(s32[2]{0:T(128)} %pad_add_fusion.1.place_ref, f32[2048,1664]{1,0:T(8,128)} %get-tuple-element.364.logits_ref, f32[1,2048]{1,0:T(1,128)} %get-tuple-element.705.total_ref, bf16[1664,1024]{1,0:T(8,128)(2,1)S(1)} %copy-done.22, ...), custom_call_target="tpu_custom_call" | custom-call | tf_op jit(solution)/shard_map/head_grads/pallas_call | solution.py:557
  331.4 6.4 %collective-permute-done.26 = bf16[2,4,64,512]{3,2,1,0:T(8,128)(2,1)} collective-permute-done((bf16[2,4,64,512]{3,2,1,0:T(8,128)(2,1)}, bf16[2,4,64,512]{3,2,1,0:T(8,128)(2,1)}, u32[]{:S(2)}, u32[]{:S(2)}) %collective-permute-start.26) | collective-permute-done | bytes 524320 | tf_op jit(solution)/shard_map/ppermute | solution.py:70
  377.8 6.8 %multiply_reduce_fusion.1 = (f32[1024]{0:T(1024)}, f32[64]{0:T(128)S(1)}, f32[1024]{0:T(1024)}, f32[64,1024]{1,0:T(8,128)S(1)}) fusion(f32[64,1024]{1,0:T(8,128)S(1)} %copy-done.28, f32[64]{0:T(128)S(1)} %copy-done.118, f32[64]{0:T(128)S(1)} %copy-done.114, f32[1024]{0:T(1024)S(1)} %bitcast.399, bf16[64,4096]{1,0:T(8,128)(2,1)S(1)} %fusion.81, ...), kind=kOutput, calls=%fused_computation.194 | convolution fusion | flops 537393088 | bytes 9450240 | tf_op jit(solution)/shard_map/dot_general | solution.py:52
  415.6 7.0 %collective-permute-done.40.refs_2_ = bf16[2,64,2560]{2,1,0:T(8,128)(2,1)S(1)} collective-permute-done((bf16[2,64,2560]{2,1,0:T(8,128)(2,1)S(1)}, bf16[2,64,2560]{2,1,0:T(8,128)(2,1)S(1)}, u32[]{:S(2)}, u32[]{:S(2)}) %collective-permute-start.40) | collective-permute-done | bytes 655392 | tf_op jit(solution)/shard_map/ppermute | solution.py:72
  444.9 6.9 %add_convert_fusion = bf16[512,3072]{1,0:T(8,128)(2,1)} fusion(bf16[512,3072]{1,0:T(8,128)(2,1)} %collective-permute-done.42, bf16[512,3072]{1,0:T(8,128)(2,1)S(1)} %copy-done.9, s32[512]{0:T(512)} %multiply_add_fusion.5, bf16[512,1024]{1,0:T(8,128)(2,1)} %get-tuple-element.353, f32[1024]{0:T(1024)} %bitcast.415, f32[1024]{0:T(1024)} %bitcast.407, ...), kind=kOutput, calls=%fused_computation.40 | convolution fusion | flops 2156134400 | bytes 10500096 | tf_op jit(solution)/shard_map/dot_general | solution.py:46
  470.2 13.9 %collective-permute-done.50 = bf16[2,4,32,1536]{3,2,1,0:T(8,128)(2,1)S(1)} collective-permute-done((bf16[2,4,32,1536]{3,2,1,0:T(8,128)(2,1)S(1)}, bf16[2,4,32,1536]{3,2,1,0:T(8,128)(2,1)S(1)}, u32[]{:S(2)}, u32[]{:S(2)}) %collective-permute-start.50) | collective-permute-done | bytes 786464 | tf_op jit(solution)/shard_map/ppermute | solution.py:70
  494.3 9.7 %collective-permute-done.49 = bf16[2,32,4096]{2,1,0:T(8,128)(2,1)S(1)} collective-permute-done((bf16[2,32,4096]{2,1,0:T(8,128)(2,1)S(1)}, bf16[2,32,4096]{2,1,0:T(8,128)(2,1)S(1)}, u32[]{:S(2)}, u32[]{:S(2)}) %collective-permute-start.49) | collective-permute-done | bytes 524320 | tf_op jit(solution)/shard_map/ppermute | solution.py:75
  554.0 9.9 %collective-permute-done.55 = bf16[1,32,4096]{2,1,0:T(8,128)(2,1)S(1)} collective-permute-done((bf16[1,32,4096]{2,1,0:T(8,128)(2,1)S(1)}, bf16[1,32,4096]{2,1,0:T(8,128)(2,1)S(1)}, u32[]{:S(2)}, u32[]{:S(2)}) %collective-permute-start.55) | collective-permute-done | bytes 262176 | tf_op jit(solution)/shard_map/ppermute | solution.py:75
  582.5 21.2 %lamb_directions.1 = (f32[1572,1024]{1,0:T(8,128)}, f32[32,3072]{1,0:T(8,128)}, f32[32,1024]{1,0:T(8,128)}, f32[32,4096]{1,0:T(8,128)}, f32[128,1024]{1,0:T(8,12...) custom-call(f32[32,256]{1,0:T(8,128)} %bitcast.363, ...), custom_call_target="tpu_custom_call" | custom-call | tf_op jit(solution)/shard_map/lamb_directions/pallas_call | solution.py:689
  613.9 8.9 %lamb_weights.1 = (f32[1572,1024]{1,0:T(8,128)}, f32[32,3072]{1,0:T(8,128)}, f32[32,1024]{1,0:T(8,128)}, f32[32,4096]{1,0:T(8,128)}, f32[128,1024]{1,0:T(8,128)}, /*index=5*/f32[32,6]{1,0:T(8,128)}, f32[8,128]{1,0:T(8,128)}) custom-call(f32[32,256]{1,0:T(8,128)} %bitcast.364, f32[32,128]{1,0:T(8,128)} %bitcast.380, f32[1572,1024]{1,0:T(8,128)} %get-tuple-element.396.refs_0_, ...), custom_call_target="tpu_custom_call" | custom-call | tf_op jit(solution)/shard_map/lamb_weights/pallas_call | solution.py:731
  (585 shorter events, 349.0 us)
Async XLA Ops:
  7.2 182.4 %all-gather.2.cloned.1.call-start = ((), (), s32[]{:S(2)}) async-start(), calls=%async_computation.10 | async-start | bytes 19464192 | tf_op jit(solution)/shard_map/all_gather | solution.py:870
  11.5 18.9 %collective-permute-start = (bf16[1,32,3200]{2,1,0:T(8,128)(2,1)S(1)}, bf16[1,32,3200]{2,1,0:T(8,128)(2,1)S(1)}, u32[]{:S(2)}, u32[]{:S(2)}) collective-permute-start(bf16[1,32,3200]{2,1,0:T(8,128)(2,1)S(1)} %pad_maximum_fusion.14), channel_id=1, source_target_pairs={{0,16},{4,20},{8,24},{12,28},{16,0},{20,4},{24,8},{28,12},{1,17},{... | collective-permute-start | bytes 614408 | tf_op jit(solution)/shard_map/ppermute | solution.py:75
  30.5 17.4 %collective-permute-start.1 = (bf16[2,32,3200]{2,1,0:T(8,128)(2,1)S(1)}, bf16[2,32,3200]{2,1,0:T(8,128)(2,1)S(1)}, u32[]{:S(2)}, u32[]{:S(2)}) collective-permute-start(bf16[2,32,3200]{2,1,0:T(8,128)(2,1)S(1)} %pad_maximum_fusion.11), channel_id=1, source_target_pairs={{0,8},{4,12},{8,0},{12,4},{16,24},{20,28},{24,16},{28,20},{1,9},{5... | collective-permute-start | bytes 1228808 | tf_op jit(solution)/shard_map/ppermute | solution.py:75
  48.0 107.6 %all-to-all-start.5 = ((bf16[32,40,1024]{2,1,0:T(8,128)(2,1)}), bf16[32,40,1024]{2,1,0:T(8,128)(2,1)}, u32[]{:S(2)}, u32[]{:S(2)}) async-start(bf16[32,40,1024]{2,1,0:T(8,128)(2,1)} %bitcast.332), calls=%async_computation.5 | async-start | bytes 5242880 | tf_op jit(solution)/shard_map/all_to_all | solution.py:89
  52.8 34.2 %collective-permute-start.4 = (bf16[4,32,1664]{2,1,0:T(8,128)(2,1)S(1)}, bf16[4,32,1664]{2,1,0:T(8,128)(2,1)S(1)}, u32[]{:S(2)}, u32[]{:S(2)}) collective-permute-start(bf16[4,32,1664]{2,1,0:T(8,128)(2,1)S(1)} %get-tuple-element.683), channel_id=1, source_target_pairs={{0,2},{1,3},{2,0},{3,1},{4,6},{5,7},{6,4},{7,5},{8,10},{9,11},{10,... | collective-permute-start | bytes 1277960 | tf_op jit(solution)/shard_map/ppermute | solution.py:72
  54.6 45.7 %collective-permute-start.2 = (bf16[4,32,1536]{2,1,0:T(8,128)(2,1)S(1)}, bf16[4,32,1536]{2,1,0:T(8,128)(2,1)S(1)}, u32[]{:S(2)}, u32[]{:S(2)}) collective-permute-start(bf16[4,32,1536]{2,1,0:T(8,128)(2,1)S(1)} %get-tuple-element.685), channel_id=1, source_target_pairs={{0,4},{4,0},{8,12},{12,8},{16,20},{20,16},{24,28},{28,24},{1,5},{5... | collective-permute-start | bytes 1179656 | tf_op jit(solution)/shard_map/ppermute | solution.py:70
  87.1 35.8 %collective-permute-start.5 = (bf16[2,4,32,1664]{3,2,1,0:T(8,128)(2,1)S(1)}, bf16[2,4,32,1664]{3,2,1,0:T(8,128)(2,1)}, u32[]{:S(2)}, u32[]{:S(2)}) collective-permute-start(bf16[2,4,32,1664]{3,2,1,0:T(8,128)(2,1)S(1)} %pad_maximum_fusion.1.refs_2_), channel_id=1, source_target_pairs={{0,4},{4,0},{8,12},{12,8},{16,20},{20,16},{24,28},{28,24},{1,5},{5... | collective-permute-start | bytes 2555912 | tf_op jit(solution)/shard_map/ppermute | solution.py:70
  100.4 34.1 %collective-permute-start.3 = (bf16[2,4,32,1536]{3,2,1,0:T(8,128)(2,1)S(1)}, bf16[2,4,32,1536]{3,2,1,0:T(8,128)(2,1)}, u32[]{:S(2)}, u32[]{:S(2)}) collective-permute-start(bf16[2,4,32,1536]{3,2,1,0:T(8,128)(2,1)S(1)} %pad_maximum_fusion.3.refs_0_), channel_id=1, source_target_pairs={{0,2},{1,3},{2,0},{3,1},{4,6},{5,7},{6,4},{7,5},{8,10},{9,11},{10,... | collective-permute-start | bytes 2359304 | tf_op jit(solution)/shard_map/ppermute | solution.py:72
  102.0 36.1 %collective-permute-start.8 = (bf16[2,4,32,1664]{3,2,1,0:T(8,128)(2,1)S(1)}, bf16[2,4,32,1664]{3,2,1,0:T(8,128)(2,1)}, u32[]{:S(2)}, u32[]{:S(2)}) collective-permute-start(bf16[2,4,32,1664]{3,2,1,0:T(8,128)(2,1)S(1)} %pad_maximum_fusion.1.refs_2_), channel_id=1, source_target_pairs={{0,1},{1,0},{2,3},{3,2},{4,5},{5,4},{6,7},{7,6},{8,9},{9,8},{10,11... | collective-permute-start | bytes 2555912 | tf_op jit(solution)/shard_map/ppermute | solution.py:72
  122.9 15.2 %collective-permute-start.9 = (bf16[2,4,32,1664]{3,2,1,0:T(8,128)(2,1)}, bf16[2,4,32,1664]{3,2,1,0:T(8,128)(2,1)}, u32[]{:S(2)}, u32[]{:S(2)}) collective-permute-start(bf16[2,4,32,1664]{3,2,1,0:T(8,128)(2,1)} %collective-permute-done.5.refs_3_), channel_id=1, source_target_pairs={{0,1},{1,0},{2,3},{3,2},{4,5},{5,4},{6,7},{7,6},{8,9},{9,8},{10,11... | collective-permute-start | bytes 2555912 | tf_op jit(solution)/shard_map/ppermute | solution.py:72
  322.8 15.1 %collective-permute-start.26 = (bf16[2,4,64,512]{3,2,1,0:T(8,128)(2,1)}, bf16[2,4,64,512]{3,2,1,0:T(8,128)(2,1)}, u32[]{:S(2)}, u32[]{:S(2)}) collective-permute-start(bf16[2,4,64,512]{3,2,1,0:T(8,128)(2,1)} %dynamic-slice_bitcast_fusion.6), channel_id=1, source_target_pairs={{0,4},{4,0},{8,12},{12,8},{16,20},{20,16},{24,28},{28,24},{1,5},{5... | collective-permute-start | bytes 1572872 | tf_op jit(solution)/shard_map/ppermute | solution.py:70
  329.1 14.9 %collective-permute-start.28 = (bf16[2,4,64,512]{3,2,1,0:T(8,128)(2,1)S(1)}, bf16[2,4,64,512]{3,2,1,0:T(8,128)(2,1)S(1)}, u32[]{:S(2)}, u32[]{:S(2)}) collective-permute-start(bf16[2,4,64,512]{3,2,1,0:T(8,128)(2,1)S(1)} %dynamic-slice_bitcast_fusion.5), channel_id=1, source_target_pairs={{0,2},{1,3},{2,0},{3,1},{4,6},{5,7},{6,4},{7,5},{8,10},{9,11},{10,... | collective-permute-start | bytes 1572872 | tf_op jit(solution)/shard_map/ppermute | solution.py:72
  331.0 15.1 %collective-permute-start.34 = (bf16[2,2,64,768]{3,2,1,0:T(8,128)(2,1)S(1)}, bf16[2,2,64,768]{3,2,1,0:T(8,128)(2,1)S(1)}, u32[]{:S(2)}, u32[]{:S(2)}) collective-permute-start(bf16[2,2,64,768]{3,2,1,0:T(8,128)(2,1)S(1)} %get-tuple-element.690), channel_id=1, source_target_pairs={{0,4},{4,0},{8,12},{12,8},{16,20},{20,16},{24,28},{28,24},{1,5},{5... | collective-permute-start | bytes 1179656 | tf_op jit(solution)/shard_map/ppermute | solution.py:70
  387.2 16.4 %collective-permute-start.37 = (bf16[64,1024]{1,0:T(8,128)(2,1)S(1)}, bf16[64,1024]{1,0:T(8,128)(2,1)S(1)}, u32[]{:S(2)}, u32[]{:S(2)}) collective-permute-start(bf16[64,1024]{1,0:T(8,128)(2,1)S(1)} %fusion.159), channel_id=1, source_target_pairs={{0,2},{1,3},{2,0},{3,1},{4,6},{5,7},{6,4},{7,5},{8,10},{9,11},{10,... | collective-permute-start | bytes 393224 | tf_op jit(solution)/shard_map/ppermute | solution.py:72
  429.1 15.8 %collective-permute-start.42 = (bf16[512,3072]{1,0:T(8,128)(2,1)}, bf16[512,3072]{1,0:T(8,128)(2,1)}, u32[]{:S(2)}, u32[]{:S(2)}) collective-permute-start(bf16[512,3072]{1,0:T(8,128)(2,1)} %convolution_convert_fusion.1), channel_id=1, source_target_pairs={{0,1},{1,0},{2,3},{3,2},{4,5},{5,4},{6,7},{7,6},{8,9},{9,8},{10,11... | collective-permute-start | bytes 9437192 | tf_op jit(solution)/shard_map/ppermute | solution.py:72
  429.1 75.0 %all-to-all-start.6 = ((bf16[32,40,1024]{2,1,0:T(8,128)(2,1)}), bf16[32,40,1024]{2,1,0:T(8,128)(2,1)}, u32[]{:S(2)}, u32[]{:S(2)}) async-start(bf16[32,40,1024]{2,1,0:T(8,128)(2,1)} %bitcast.333), calls=%async_computation.6 | async-start | bytes 5242880 | tf_op jit(solution)/shard_map/all_to_all | solution.py:89
  457.7 26.3 %collective-permute-start.50 = (bf16[2,4,32,1536]{3,2,1,0:T(8,128)(2,1)S(1)}, bf16[2,4,32,1536]{3,2,1,0:T(8,128)(2,1)S(1)}, u32[]{:S(2)}, u32[]{:S(2)}) collective-permute-start(bf16[2,4,32,1536]{3,2,1,0:T(8,128)(2,1)S(1)} %dynamic-slice_bitcast_fusion.1), channel_id=1, source_target_pairs={{0,4},{4,0},{8,12},{12,8},{16,20},{20,16},{24,28},{28,24},{1,5},{5... | collective-permute-start | bytes 2359304 | tf_op jit(solution)/shard_map/ppermute | solution.py:70
  459.4 27.6 %collective-permute-start.51 = (bf16[2,4,32,1536]{3,2,1,0:T(8,128)(2,1)S(1)}, bf16[2,4,32,1536]{3,2,1,0:T(8,128)(2,1)S(1)}, u32[]{:S(2)}, u32[]{:S(2)}) collective-permute-start(bf16[2,4,32,1536]{3,2,1,0:T(8,128)(2,1)S(1)} %dynamic-slice_bitcast_fusion), channel_id=1, source_target_pairs={{0,2},{1,3},{2,0},{3,1},{4,6},{5,7},{6,4},{7,5},{8,10},{9,11},{10,... | collective-permute-start | bytes 2359304 | tf_op jit(solution)/shard_map/ppermute | solution.py:72
  466.9 27.2 %collective-permute-start.48 = (bf16[2,128,1024]{2,1,0:T(8,128)(2,1)S(1)}, bf16[2,128,1024]{2,1,0:T(8,128)(2,1)S(1)}, u32[]{:S(2)}, u32[]{:S(2)}) collective-permute-start(bf16[2,128,1024]{2,1,0:T(8,128)(2,1)S(1)} %dynamic-slice_bitcast_fusion.4), channel_id=1, source_target_pairs={{0,8},{4,12},{8,0},{12,4},{16,24},{20,28},{24,16},{28,20},{1,9},{5... | collective-permute-start | bytes 1572872 | tf_op jit(solution)/shard_map/ppermute | solution.py:75
  469.6 34.3 %collective-permute-start.49 = (bf16[2,32,4096]{2,1,0:T(8,128)(2,1)S(1)}, bf16[2,32,4096]{2,1,0:T(8,128)(2,1)S(1)}, u32[]{:S(2)}, u32[]{:S(2)}) collective-permute-start(bf16[2,32,4096]{2,1,0:T(8,128)(2,1)S(1)} %dynamic-slice_bitcast_fusion.3), channel_id=1, source_target_pairs={{0,8},{4,12},{8,0},{12,4},{16,24},{20,28},{24,16},{28,20},{1,9},{5... | collective-permute-start | bytes 1572872 | tf_op jit(solution)/shard_map/ppermute | solution.py:75
  507.5 22.1 %collective-permute-start.53 = (bf16[4,32,1536]{2,1,0:T(8,128)(2,1)}, bf16[4,32,1536]{2,1,0:T(8,128)(2,1)}, u32[]{:S(2)}, u32[]{:S(2)}) collective-permute-start(bf16[4,32,1536]{2,1,0:T(8,128)(2,1)} %dynamic-slice_bitcast_fusion.7), channel_id=1, source_target_pairs={{0,4},{4,0},{8,12},{12,8},{16,20},{20,16},{24,28},{28,24},{1,5},{5... | collective-permute-start | bytes 1179656 | tf_op jit(solution)/shard_map/ppermute | solution.py:70
  507.5 23.2 %collective-permute-start.52 = (bf16[4,32,1536]{2,1,0:T(8,128)(2,1)S(1)}, bf16[4,32,1536]{2,1,0:T(8,128)(2,1)}, u32[]{:S(2)}, u32[]{:S(2)}) collective-permute-start(bf16[4,32,1536]{2,1,0:T(8,128)(2,1)S(1)} %dynamic-slice_bitcast_fusion.8), channel_id=1, source_target_pairs={{0,2},{1,3},{2,0},{3,1},{4,6},{5,7},{6,4},{7,5},{8,10},{9,11},{10,... | collective-permute-start | bytes 1179656 | tf_op jit(solution)/shard_map/ppermute | solution.py:72
  510.0 40.4 %collective-permute-start.56 = (bf16[1,32,4096]{2,1,0:T(8,128)(2,1)}, bf16[1,32,4096]{2,1,0:T(8,128)(2,1)}, u32[]{:S(2)}, u32[]{:S(2)}) collective-permute-start(bf16[1,32,4096]{2,1,0:T(8,128)(2,1)} %dynamic-slice_convert_fusion.1), channel_id=1, source_target_pairs={{0,16},{4,20},{8,24},{12,28},{16,0},{20,4},{24,8},{28,12},{1,17},{... | collective-permute-start | bytes 786440 | tf_op jit(solution)/shard_map/ppermute | solution.py:75
  510.0 42.2 %collective-permute-start.57 = (bf16[1,128,1024]{2,1,0:T(8,128)(2,1)}, bf16[1,128,1024]{2,1,0:T(8,128)(2,1)}, u32[]{:S(2)}, u32[]{:S(2)}) collective-permute-start(bf16[1,128,1024]{2,1,0:T(8,128)(2,1)} %dynamic-slice_convert_fusion.2), channel_id=1, source_target_pairs={{0,16},{4,20},{8,24},{12,28},{16,0},{20,4},{24,8},{28,12},{1,17},{... | collective-permute-start | bytes 786440 | tf_op jit(solution)/shard_map/ppermute | solution.py:75
  (170 other events, 1785.8 us)
Sparse Core Ops, SparseCore 0:
  11.4 178.1 all-gather.1

commit v7 on v6

--- a/solution.py
+++ b/solution.py
@@ -873,9 +873,9 @@
     first_parts = links.plane_first(first_near)
     found = after(find(asked_first), first_near)
     landed = links.to_all(found)
+    weight_row = weight_squares(tie(*masters, found)[:6])
+    first_parts = [after(part, weight_row, table_low) for part in first_parts]
     first_pieces = links.plane_second(*first_parts)
-    weight_row = weight_squares(tie(*masters, found)[:6])
-    first_pieces[0] = after(first_pieces[0], weight_row, table_low)
     first_whole = links.assemble(links.plane_core(first_pieces))
     qkv_weight = first_whole[:, :qkv_width]
     gain_entries = first_whole[:, qkv_width : qkv_width + 6].astype(f32).T

time: 645 us -> 645 us (level)
  waiting for transfers between devices: 232 us -> 240 us
    ppermute x28, waiting for transfers between devices: 63.3 us -> 33 us  [swap(): lax.ppermute(values, 'narrow', [(i, i ^ step) for i in range(self.narrow)])]
    ppermute x12, waiting for transfers between devices: 64.6 us -> 92.3 us  [swap(): return lax.ppermute(values, 'wide', [(i, i ^ 1) for i in range(self.wide)])]
    all_to_all x6, waiting for transfers between devices: 25.8 us -> 34.9 us  [to_all(): return lax.all_to_all(values, ('wide', 'narrow'), 0, 0, tiled=True)]
    unnamed x275 -> x247, local copies, waits for them, and re-layouts: 26 us -> 23 us
  transfers between devices with their start and end apart: 65 -> 65, of which waited for: 38 -> 39; matrix products, arithmetic and copies ran while one was open for 21% -> 20% of each run, Pallas kernels for 3% -> 3%
where the time goes in v7:
time: 645 us; the launch traced here: 637 us
  waiting for transfers between devices  240 us (37%)
  Pallas kernels  98.7 us (15%)
  matrix products  87.3 us (14%)
  starting transfers between devices  70.9 us (11%)
  local copies, waits for them, and re-layouts  64 us (10%)
  other arithmetic  54.9 us (9%)
  between operations  20.3 us (3%)
    ppermute x12, waiting for transfers between devices, swap(): return lax.ppermute(values, 'wide', [(i, i ^ 1) for i in range(self.wide)])  92.3 us
    ppermute x12, waiting for transfers between devices, cross(): lax.ppermute(values, 'wide', [(i, i ^ 2 * step) for i in range(self.wide)])  56.4 us
    dot_general x10, matrix products, matmul(): return jnp.dot(left_side, right_side, preferred_element_type=f32)  41 us
    all_to_all x6, waiting for transfers between devices, to_all(): return lax.all_to_all(values, ('wide', 'narrow'), 0, 0, tiled=True)  34.9 us
    ppermute x28, waiting for transfers between devices, swap(): lax.ppermute(values, 'narrow', [(i, i ^ step) for i in range(self.narrow)])  33 us
    dot_general x5, matrix products, contract_rows(): lax.dot_general(left_side, right_side, (((0,), (0,)), ((), ())), preferre...  25.1 us
    unnamed x247, local copies, waits for them, and re-layouts  23 us
    all_to_all x6, starting transfers between devices, to_all(): return lax.all_to_all(values, ('wide', 'narrow'), 0, 0, tiled=True)  22.5 us
  transfers between devices with their start and end apart: 65, of which 39 were waited for; matrix products, arithmetic and copies ran while one was open for 20% of the time, Pallas kernels for 3%

profile of v7, /device:TPU:0, one launch (start us, length us, event | category | flops | bytes accessed | tf_op | source)
XLA Modules:
  0.0 636.7 jit_solution(361178685948056663)
XLA Ops:
  30.5 8.3 %fusion.32 = bf16[1280,1024]{1,0:T(8,128)(2,1)} fusion(s32[1280]{0:T(1024)S(1)} %eq.368, bf16[1572,1024]{1,0:T(8,128)(2,1)} %convert.59), kind=kOutput, calls=%fused_computation.53 | convolution fusion | flops 4365516800 | bytes 5846016 | tf_op jit(solution)/shard_map/dot_general | solution.py:42
  38.8 9.0 %collective-permute-done.1 = bf16[2,32,3200]{2,1,0:T(8,128)(2,1)S(1)} collective-permute-done((bf16[2,32,3200]{2,1,0:T(8,128)(2,1)S(1)}, bf16[2,32,3200]{2,1,0:T(8,128)(2,1)S(1)}, u32[]{:S(2)}, u32[]{:S(2)}) %collective-permute-start.1) | collective-permute-done | bytes 409632 | tf_op jit(solution)/shard_map/ppermute | solution.py:75
  64.8 35.7 %collective-permute-done.2 = bf16[4,32,1536]{2,1,0:T(8,128)(2,1)S(1)} collective-permute-done((bf16[4,32,1536]{2,1,0:T(8,128)(2,1)S(1)}, bf16[4,32,1536]{2,1,0:T(8,128)(2,1)S(1)}, u32[]{:S(2)}, u32[]{:S(2)}) %collective-permute-start.2) | collective-permute-done | bytes 393248 | tf_op jit(solution)/shard_map/ppermute | solution.py:70
  102.5 22.2 %collective-permute-done.5.refs_3_ = bf16[2,4,32,1664]{3,2,1,0:T(8,128)(2,1)S(1)} collective-permute-done((bf16[2,4,32,1664]{3,2,1,0:T(8,128)(2,1)S(1)}, bf16[2,4,32,1664]{3,2,1,0:T(8,128)(2,1)S(1)}, u32[]{:S(2)}, u32[]{:S(2)}) %collective-permute-start.5) | collective-permute-done | bytes 852000 | tf_op jit(solution)/shard_map/ppermute | solution.py:70
  136.1 19.5 %all-to-all-done.5 = bf16[32,40,1024]{2,1,0:T(8,128)(2,1)} async-done(((bf16[32,40,1024]{2,1,0:T(8,128)(2,1)}), bf16[32,40,1024]{2,1,0:T(8,128)(2,1)}, u32[]{:S(2)}, u32[]{:S(2)}) %all-to-all-start.5) | async-done | bytes 2621472 | tf_op jit(solution)/shard_map/all_to_all | solution.py:89
  163.2 6.7 %fusion.25.qkv_ref = bf16[512,3072]{1,0:T(8,128)(2,1)S(1)} fusion(bf16[1024,3200]{1,0:T(8,128)(2,1)} %bitcast.320, bf16[512,1024]{1,0:T(8,128)(2,1)} %get-tuple-element.356, f32[1024]{0:T(1024)S(1)} %bitcast.414, f32[1024]{0:T(1024)S(1)} %bitcast.406, f32[512]{0:T(512)S(1)} %fusion.155, f32[512]{0:T(512)S(1)} %broadcast_multiply_fusion), kind=kOutput, calls=%fused_computation.45 | convolution fusion | flops 3225944064 | bytes 10498048 | tf_op jit(solution)/shard_map/dot_general | solution.py:42
  178.0 12.1 %all-gather.2.cloned.1.call-done.source_ref = bf16[1024,9216]{1,0:T(8,128)(2,1)} async-done(((bf16[32,9216]{1,0:T(8,128)(2,1)}), bf16[1024,9216]{1,0:T(8,128)(2,1)}) %all-gather.2.cloned.1.call-update) | async-done | bytes 18874384 | tf_op jit(solution)/shard_map/all_gather | solution.py:870
  197.1 8.0 %fusion.19 = f32[64,4096]{1,0:T(8,128)S(1)} fusion(bf16[1024,9216]{1,0:T(8,128)(2,1)} %all-gather.2.cloned.1.call-done.source_ref, f32[64,1024]{1,0:T(8,128)S(1)} %get-tuple-element.728, f32[1024]{0:T(1024)S(1)} %bitcast.417, f32[1024]{0:T(1024)S(1)} %bitcast.397, f32[64]{0:T(128)S(1)} %fusion.156, f32[64]{0:T(128)S(1)} %broadcast_multiply_fusion.2), kind=kOutput, calls=%fused_computation.36 | convolution fusion | flops 537198592 | bytes 9708032 | tf_op jit(solution)/shard_map/dot_general | solution.py:42
  207.3 7.9 %collective-permute-done.10 = bf16[1,64,1024]{2,1,0:T(8,128)(2,1)S(1)} collective-permute-done((bf16[1,64,1024]{2,1,0:T(8,128)(2,1)S(1)}, bf16[1,64,1024]{2,1,0:T(8,128)(2,1)S(1)}, u32[]{:S(2)}, u32[]{:S(2)}) %collective-permute-start.10) | collective-permute-done | bytes 131104 | tf_op jit(solution)/shard_map/ppermute | solution.py:75
  215.3 8.2 %collective-permute-done.11 = bf16[2,64,1024]{2,1,0:T(8,128)(2,1)S(1)} collective-permute-done((bf16[2,64,1024]{2,1,0:T(8,128)(2,1)S(1)}, bf16[2,64,1024]{2,1,0:T(8,128)(2,1)S(1)}, u32[]{:S(2)}, u32[]{:S(2)}) %collective-permute-start.11) | collective-permute-done | bytes 262176 | tf_op jit(solution)/shard_map/ppermute | solution.py:75
  236.9 8.0 %collective-permute-done.13.refs_1_ = bf16[2,4,64,512]{3,2,1,0:T(8,128)(2,1)} collective-permute-done((bf16[2,4,64,512]{3,2,1,0:T(8,128)(2,1)}, bf16[2,4,64,512]{3,2,1,0:T(8,128)(2,1)}, u32[]{:S(2)}, u32[]{:S(2)}) %collective-permute-start.13) | collective-permute-done | bytes 524320 | tf_op jit(solution)/shard_map/ppermute | solution.py:72
  255.6 16.7 %head_logits.1 = (f32[2048,1664]{1,0:T(8,128)}, f32[1,2048]{1,0:T(1,128)}, f32[1,2048]{1,0:T(1,128)}, f32[1,128]{1,0:T(1,128)}) custom-call(s32[1]{0:T(128)} %bitcast.base_ref, bf16[2048,1024]{1,0:T(8,128)(2,1)} %bitcast.316, bf16[1664,1024]{1,0:T(8,128)(2,1)S(1)} %copy-done.23, s32[2048,1]{1,0:T(8,128)} %broadcast_in_dim_reshape.3.targets_ref), custom_call_target="tpu_custom_call" | custom-call | tf_op jit(solution)/shard_map/head_logits/pallas_call | solution.py:509
  294.4 10.1 %head_grads.2 = (bf16[1024,1664]{1,0:T(8,128)(2,1)}, bf16[1024,1024]{1,0:T(8,128)(2,1)}) custom-call(s32[2]{0:T(128)} %pad_add_fusion.place_ref, f32[2048,1664]{1,0:T(8,128)} %get-tuple-element.370.logits_ref, f32[1,2048]{1,0:T(1,128)} %get-tuple-element.707.total_ref, bf16[1664,1024]{1,0:T(8,128)(2,1)} %get-tuple-element.1038, ...), custom_call_target="tpu_custom_call" | custom-call | tf_op jit(solution)/shard_map/head_grads/pallas_call | solution.py:557
  309.0 9.8 %head_grads.3 = (bf16[1024,1664]{1,0:T(8,128)(2,1)}, bf16[1024,1024]{1,0:T(8,128)(2,1)}) custom-call(s32[2]{0:T(128)} %pad_add_fusion.1.place_ref, f32[2048,1664]{1,0:T(8,128)} %get-tuple-element.370.logits_ref, f32[1,2048]{1,0:T(1,128)} %get-tuple-element.707.total_ref, bf16[1664,1024]{1,0:T(8,128)(2,1)S(1)} %copy-done.24, ...), custom_call_target="tpu_custom_call" | custom-call | tf_op jit(solution)/shard_map/head_grads/pallas_call | solution.py:557
  330.9 6.7 %collective-permute-done.26 = bf16[2,4,64,512]{3,2,1,0:T(8,128)(2,1)} collective-permute-done((bf16[2,4,64,512]{3,2,1,0:T(8,128)(2,1)}, bf16[2,4,64,512]{3,2,1,0:T(8,128)(2,1)}, u32[]{:S(2)}, u32[]{:S(2)}) %collective-permute-start.26) | collective-permute-done | bytes 524320 | tf_op jit(solution)/shard_map/ppermute | solution.py:70
  371.9 6.3 fusion.81
  378.4 6.8 %multiply_reduce_fusion.1 = (f32[1024]{0:T(1024)}, f32[64]{0:T(128)S(1)}, f32[1024]{0:T(1024)}, f32[64,1024]{1,0:T(8,128)S(1)}) fusion(f32[64,1024]{1,0:T(8,128)S(1)} %copy-done.30, f32[64]{0:T(128)S(1)} %copy-done.104, f32[64]{0:T(128)S(1)} %copy-done.100, f32[1024]{0:T(1024)S(1)} %bitcast.399, bf16[64,4096]{1,0:T(8,128)(2,1)S(1)} %fusion.81, ...), kind=kOutput, calls=%fused_computation.194 | convolution fusion | flops 537393088 | bytes 9450240 | tf_op jit(solution)/shard_map/dot_general | solution.py:52
  415.6 7.1 %collective-permute-done.40.refs_2_ = bf16[2,64,2560]{2,1,0:T(8,128)(2,1)S(1)} collective-permute-done((bf16[2,64,2560]{2,1,0:T(8,128)(2,1)S(1)}, bf16[2,64,2560]{2,1,0:T(8,128)(2,1)S(1)}, u32[]{:S(2)}, u32[]{:S(2)}) %collective-permute-start.40) | collective-permute-done | bytes 655392 | tf_op jit(solution)/shard_map/ppermute | solution.py:72
  445.1 6.9 %add_convert_fusion = bf16[512,3072]{1,0:T(8,128)(2,1)} fusion(bf16[512,3072]{1,0:T(8,128)(2,1)} %collective-permute-done.42, bf16[512,3072]{1,0:T(8,128)(2,1)S(1)} %copy-done.9, s32[512]{0:T(512)} %multiply_add_fusion.5, bf16[512,1024]{1,0:T(8,128)(2,1)} %get-tuple-element.356, f32[1024]{0:T(1024)} %bitcast.415, f32[1024]{0:T(1024)} %bitcast.410, ...), kind=kOutput, calls=%fused_computation.40 | convolution fusion | flops 2156134400 | bytes 10500096 | tf_op jit(solution)/shard_map/dot_general | solution.py:46
  470.5 13.9 %collective-permute-done.50 = bf16[2,4,32,1536]{3,2,1,0:T(8,128)(2,1)S(1)} collective-permute-done((bf16[2,4,32,1536]{3,2,1,0:T(8,128)(2,1)S(1)}, bf16[2,4,32,1536]{3,2,1,0:T(8,128)(2,1)S(1)}, u32[]{:S(2)}, u32[]{:S(2)}) %collective-permute-start.50) | collective-permute-done | bytes 786464 | tf_op jit(solution)/shard_map/ppermute | solution.py:70
  494.5 9.7 %collective-permute-done.49 = bf16[2,32,4096]{2,1,0:T(8,128)(2,1)S(1)} collective-permute-done((bf16[2,32,4096]{2,1,0:T(8,128)(2,1)S(1)}, bf16[2,32,4096]{2,1,0:T(8,128)(2,1)S(1)}, u32[]{:S(2)}, u32[]{:S(2)}) %collective-permute-start.49) | collective-permute-done | bytes 524320 | tf_op jit(solution)/shard_map/ppermute | solution.py:75
  554.1 10.0 %collective-permute-done.55 = bf16[1,32,4096]{2,1,0:T(8,128)(2,1)S(1)} collective-permute-done((bf16[1,32,4096]{2,1,0:T(8,128)(2,1)S(1)}, bf16[1,32,4096]{2,1,0:T(8,128)(2,1)S(1)}, u32[]{:S(2)}, u32[]{:S(2)}) %collective-permute-start.55) | collective-permute-done | bytes 262176 | tf_op jit(solution)/shard_map/ppermute | solution.py:75
  582.6 21.2 %lamb_directions.1 = (f32[1572,1024]{1,0:T(8,128)}, f32[32,3072]{1,0:T(8,128)}, f32[32,1024]{1,0:T(8,128)}, f32[32,4096]{1,0:T(8,128)}, f32[128,1024]{1,0:T(8,12...) custom-call(f32[32,256]{1,0:T(8,128)} %bitcast.363, ...), custom_call_target="tpu_custom_call" | custom-call | tf_op jit(solution)/shard_map/lamb_directions/pallas_call | solution.py:689
  614.0 8.9 %lamb_weights.1 = (f32[1572,1024]{1,0:T(8,128)}, f32[32,3072]{1,0:T(8,128)}, f32[32,1024]{1,0:T(8,128)}, f32[32,4096]{1,0:T(8,128)}, f32[128,1024]{1,0:T(8,128)}, /*index=5*/f32[32,6]{1,0:T(8,128)}, f32[8,128]{1,0:T(8,128)}) custom-call(f32[32,256]{1,0:T(8,128)} %bitcast.364, f32[32,128]{1,0:T(8,128)} %bitcast.380, f32[1572,1024]{1,0:T(8,128)} %get-tuple-element.402.refs_0_, ...), custom_call_target="tpu_custom_call" | custom-call | tf_op jit(solution)/shard_map/lamb_weights/pallas_call | solution.py:731
  (557 shorter events, 336.7 us)
Async XLA Ops:
  7.2 182.9 %all-gather.2.cloned.1.call-start = ((), (), s32[]{:S(2)}) async-start(), calls=%async_computation.10 | async-start | bytes 19464192 | tf_op jit(solution)/shard_map/all_gather | solution.py:870
  11.5 18.3 %collective-permute-start = (bf16[1,32,3200]{2,1,0:T(8,128)(2,1)S(1)}, bf16[1,32,3200]{2,1,0:T(8,128)(2,1)S(1)}, u32[]{:S(2)}, u32[]{:S(2)}) collective-permute-start(bf16[1,32,3200]{2,1,0:T(8,128)(2,1)S(1)} %pad_maximum_fusion.14), channel_id=1, source_target_pairs={{0,16},{4,20},{8,24},{12,28},{16,0},{20,4},{24,8},{28,12},{1,17},{... | collective-permute-start | bytes 614408 | tf_op jit(solution)/shard_map/ppermute | solution.py:75
  29.9 17.9 %collective-permute-start.1 = (bf16[2,32,3200]{2,1,0:T(8,128)(2,1)S(1)}, bf16[2,32,3200]{2,1,0:T(8,128)(2,1)S(1)}, u32[]{:S(2)}, u32[]{:S(2)}) collective-permute-start(bf16[2,32,3200]{2,1,0:T(8,128)(2,1)S(1)} %pad_maximum_fusion.11), channel_id=1, source_target_pairs={{0,8},{4,12},{8,0},{12,4},{16,24},{20,28},{24,16},{28,20},{1,9},{5... | collective-permute-start | bytes 1228808 | tf_op jit(solution)/shard_map/ppermute | solution.py:75
  47.8 107.8 %all-to-all-start.5 = ((bf16[32,40,1024]{2,1,0:T(8,128)(2,1)}), bf16[32,40,1024]{2,1,0:T(8,128)(2,1)}, u32[]{:S(2)}, u32[]{:S(2)}) async-start(bf16[32,40,1024]{2,1,0:T(8,128)(2,1)} %bitcast.330), calls=%async_computation.5 | async-start | bytes 5242880 | tf_op jit(solution)/shard_map/all_to_all | solution.py:89
  52.8 47.7 %collective-permute-start.4 = (bf16[4,32,1664]{2,1,0:T(8,128)(2,1)S(1)}, bf16[4,32,1664]{2,1,0:T(8,128)(2,1)S(1)}, u32[]{:S(2)}, u32[]{:S(2)}) collective-permute-start(bf16[4,32,1664]{2,1,0:T(8,128)(2,1)S(1)} %slice.225), channel_id=1, source_target_pairs={{0,2},{1,3},{2,0},{3,1},{4,6},{5,7},{6,4},{7,5},{8,10},{9,11},{10,... | collective-permute-start | bytes 1277960 | tf_op jit(solution)/shard_map/ppermute | solution.py:72
  54.6 45.9 %collective-permute-start.2 = (bf16[4,32,1536]{2,1,0:T(8,128)(2,1)S(1)}, bf16[4,32,1536]{2,1,0:T(8,128)(2,1)S(1)}, u32[]{:S(2)}, u32[]{:S(2)}) collective-permute-start(bf16[4,32,1536]{2,1,0:T(8,128)(2,1)S(1)} %slice.224), channel_id=1, source_target_pairs={{0,4},{4,0},{8,12},{12,8},{16,20},{20,16},{24,28},{28,24},{1,5},{5... | collective-permute-start | bytes 1179656 | tf_op jit(solution)/shard_map/ppermute | solution.py:70
  100.6 24.1 %collective-permute-start.5 = (bf16[2,4,32,1664]{3,2,1,0:T(8,128)(2,1)S(1)}, bf16[2,4,32,1664]{3,2,1,0:T(8,128)(2,1)S(1)}, u32[]{:S(2)}, u32[]{:S(2)}) collective-permute-start(bf16[2,4,32,1664]{3,2,1,0:T(8,128)(2,1)S(1)} %pad_maximum_fusion.1.refs_2_), channel_id=1, source_target_pairs={{0,4},{4,0},{8,12},{12,8},{16,20},{20,16},{24,28},{28,24},{1,5},{5... | collective-permute-start | bytes 2555912 | tf_op jit(solution)/shard_map/ppermute | solution.py:70
  101.9 23.8 %collective-permute-start.3 = (bf16[2,4,32,1536]{3,2,1,0:T(8,128)(2,1)S(1)}, bf16[2,4,32,1536]{3,2,1,0:T(8,128)(2,1)}, u32[]{:S(2)}, u32[]{:S(2)}) collective-permute-start(bf16[2,4,32,1536]{3,2,1,0:T(8,128)(2,1)S(1)} %pad_maximum_fusion.3.refs_0_), channel_id=1, source_target_pairs={{0,2},{1,3},{2,0},{3,1},{4,6},{5,7},{6,4},{7,5},{8,10},{9,11},{10,... | collective-permute-start | bytes 2359304 | tf_op jit(solution)/shard_map/ppermute | solution.py:72
  102.5 27.0 %collective-permute-start.8 = (bf16[2,4,32,1664]{3,2,1,0:T(8,128)(2,1)S(1)}, bf16[2,4,32,1664]{3,2,1,0:T(8,128)(2,1)S(1)}, u32[]{:S(2)}, u32[]{:S(2)}) collective-permute-start(bf16[2,4,32,1664]{3,2,1,0:T(8,128)(2,1)S(1)} %pad_maximum_fusion.1.refs_2_), channel_id=1, source_target_pairs={{0,1},{1,0},{2,3},{3,2},{4,5},{5,4},{6,7},{7,6},{8,9},{9,8},{10,11... | collective-permute-start | bytes 2555912 | tf_op jit(solution)/shard_map/ppermute | solution.py:72
  322.5 15.1 %collective-permute-start.26 = (bf16[2,4,64,512]{3,2,1,0:T(8,128)(2,1)}, bf16[2,4,64,512]{3,2,1,0:T(8,128)(2,1)}, u32[]{:S(2)}, u32[]{:S(2)}) collective-permute-start(bf16[2,4,64,512]{3,2,1,0:T(8,128)(2,1)} %dynamic-slice_bitcast_fusion.6), channel_id=1, source_target_pairs={{0,4},{4,0},{8,12},{12,8},{16,20},{20,16},{24,28},{28,24},{1,5},{5... | collective-permute-start | bytes 1572872 | tf_op jit(solution)/shard_map/ppermute | solution.py:70
  328.4 14.9 %collective-permute-start.28 = (bf16[2,4,64,512]{3,2,1,0:T(8,128)(2,1)S(1)}, bf16[2,4,64,512]{3,2,1,0:T(8,128)(2,1)S(1)}, u32[]{:S(2)}, u32[]{:S(2)}) collective-permute-start(bf16[2,4,64,512]{3,2,1,0:T(8,128)(2,1)S(1)} %dynamic-slice_bitcast_fusion.5), channel_id=1, source_target_pairs={{0,2},{1,3},{2,0},{3,1},{4,6},{5,7},{6,4},{7,5},{8,10},{9,11},{10,... | collective-permute-start | bytes 1572872 | tf_op jit(solution)/shard_map/ppermute | solution.py:72
  330.3 15.6 %collective-permute-start.34 = (bf16[2,2,64,768]{3,2,1,0:T(8,128)(2,1)S(1)}, bf16[2,2,64,768]{3,2,1,0:T(8,128)(2,1)S(1)}, u32[]{:S(2)}, u32[]{:S(2)}) collective-permute-start(bf16[2,2,64,768]{3,2,1,0:T(8,128)(2,1)S(1)} %get-tuple-element.692), channel_id=1, source_target_pairs={{0,4},{4,0},{8,12},{12,8},{16,20},{20,16},{24,28},{28,24},{1,5},{5... | collective-permute-start | bytes 1179656 | tf_op jit(solution)/shard_map/ppermute | solution.py:70
  387.4 16.2 %collective-permute-start.37 = (bf16[64,1024]{1,0:T(8,128)(2,1)S(1)}, bf16[64,1024]{1,0:T(8,128)(2,1)S(1)}, u32[]{:S(2)}, u32[]{:S(2)}) collective-permute-start(bf16[64,1024]{1,0:T(8,128)(2,1)S(1)} %fusion.159), channel_id=1, source_target_pairs={{0,2},{1,3},{2,0},{3,1},{4,6},{5,7},{6,4},{7,5},{8,10},{9,11},{10,... | collective-permute-start | bytes 393224 | tf_op jit(solution)/shard_map/ppermute | solution.py:72
  429.1 15.9 %collective-permute-start.42 = (bf16[512,3072]{1,0:T(8,128)(2,1)}, bf16[512,3072]{1,0:T(8,128)(2,1)}, u32[]{:S(2)}, u32[]{:S(2)}) collective-permute-start(bf16[512,3072]{1,0:T(8,128)(2,1)} %convolution_convert_fusion.1), channel_id=1, source_target_pairs={{0,1},{1,0},{2,3},{3,2},{4,5},{5,4},{6,7},{7,6},{8,9},{9,8},{10,11... | collective-permute-start | bytes 9437192 | tf_op jit(solution)/shard_map/ppermute | solution.py:72
  429.2 75.2 %all-to-all-start.6 = ((bf16[32,40,1024]{2,1,0:T(8,128)(2,1)}), bf16[32,40,1024]{2,1,0:T(8,128)(2,1)}, u32[]{:S(2)}, u32[]{:S(2)}) async-start(bf16[32,40,1024]{2,1,0:T(8,128)(2,1)} %bitcast.331), calls=%async_computation.6 | async-start | bytes 5242880 | tf_op jit(solution)/shard_map/all_to_all | solution.py:89
  457.9 26.5 %collective-permute-start.50 = (bf16[2,4,32,1536]{3,2,1,0:T(8,128)(2,1)S(1)}, bf16[2,4,32,1536]{3,2,1,0:T(8,128)(2,1)S(1)}, u32[]{:S(2)}, u32[]{:S(2)}) collective-permute-start(bf16[2,4,32,1536]{3,2,1,0:T(8,128)(2,1)S(1)} %dynamic-slice_bitcast_fusion.1), channel_id=1, source_target_pairs={{0,4},{4,0},{8,12},{12,8},{16,20},{20,16},{24,28},{28,24},{1,5},{5... | collective-permute-start | bytes 2359304 | tf_op jit(solution)/shard_map/ppermute | solution.py:70
  459.7 27.7 %collective-permute-start.51 = (bf16[2,4,32,1536]{3,2,1,0:T(8,128)(2,1)S(1)}, bf16[2,4,32,1536]{3,2,1,0:T(8,128)(2,1)S(1)}, u32[]{:S(2)}, u32[]{:S(2)}) collective-permute-start(bf16[2,4,32,1536]{3,2,1,0:T(8,128)(2,1)S(1)} %dynamic-slice_bitcast_fusion), channel_id=1, source_target_pairs={{0,2},{1,3},{2,0},{3,1},{4,6},{5,7},{6,4},{7,5},{8,10},{9,11},{10,... | collective-permute-start | bytes 2359304 | tf_op jit(solution)/shard_map/ppermute | solution.py:72
  467.2 27.1 %collective-permute-start.48 = (bf16[2,128,1024]{2,1,0:T(8,128)(2,1)S(1)}, bf16[2,128,1024]{2,1,0:T(8,128)(2,1)S(1)}, u32[]{:S(2)}, u32[]{:S(2)}) collective-permute-start(bf16[2,128,1024]{2,1,0:T(8,128)(2,1)S(1)} %dynamic-slice_bitcast_fusion.4), channel_id=1, source_target_pairs={{0,8},{4,12},{8,0},{12,4},{16,24},{20,28},{24,16},{28,20},{1,9},{5... | collective-permute-start | bytes 1572872 | tf_op jit(solution)/shard_map/ppermute | solution.py:75
  469.9 34.4 %collective-permute-start.49 = (bf16[2,32,4096]{2,1,0:T(8,128)(2,1)S(1)}, bf16[2,32,4096]{2,1,0:T(8,128)(2,1)S(1)}, u32[]{:S(2)}, u32[]{:S(2)}) collective-permute-start(bf16[2,32,4096]{2,1,0:T(8,128)(2,1)S(1)} %dynamic-slice_bitcast_fusion.3), channel_id=1, source_target_pairs={{0,8},{4,12},{8,0},{12,4},{16,24},{20,28},{24,16},{28,20},{1,9},{5... | collective-permute-start | bytes 1572872 | tf_op jit(solution)/shard_map/ppermute | solution.py:75
  507.7 22.0 %collective-permute-start.53 = (bf16[4,32,1536]{2,1,0:T(8,128)(2,1)}, bf16[4,32,1536]{2,1,0:T(8,128)(2,1)}, u32[]{:S(2)}, u32[]{:S(2)}) collective-permute-start(bf16[4,32,1536]{2,1,0:T(8,128)(2,1)} %dynamic-slice_bitcast_fusion.7), channel_id=1, source_target_pairs={{0,4},{4,0},{8,12},{12,8},{16,20},{20,16},{24,28},{28,24},{1,5},{5... | collective-permute-start | bytes 1179656 | tf_op jit(solution)/shard_map/ppermute | solution.py:70
  507.7 23.1 %collective-permute-start.52 = (bf16[4,32,1536]{2,1,0:T(8,128)(2,1)S(1)}, bf16[4,32,1536]{2,1,0:T(8,128)(2,1)}, u32[]{:S(2)}, u32[]{:S(2)}) collective-permute-start(bf16[4,32,1536]{2,1,0:T(8,128)(2,1)S(1)} %dynamic-slice_bitcast_fusion.8), channel_id=1, source_target_pairs={{0,2},{1,3},{2,0},{3,1},{4,6},{5,7},{6,4},{7,5},{8,10},{9,11},{10,... | collective-permute-start | bytes 1179656 | tf_op jit(solution)/shard_map/ppermute | solution.py:72
  510.1 40.3 %collective-permute-start.56 = (bf16[1,32,4096]{2,1,0:T(8,128)(2,1)}, bf16[1,32,4096]{2,1,0:T(8,128)(2,1)}, u32[]{:S(2)}, u32[]{:S(2)}) collective-permute-start(bf16[1,32,4096]{2,1,0:T(8,128)(2,1)} %dynamic-slice_convert_fusion.1), channel_id=1, source_target_pairs={{0,16},{4,20},{8,24},{12,28},{16,0},{20,4},{24,8},{28,12},{1,17},{... | collective-permute-start | bytes 786440 | tf_op jit(solution)/shard_map/ppermute | solution.py:75
  510.1 42.1 %collective-permute-start.57 = (bf16[1,128,1024]{2,1,0:T(8,128)(2,1)}, bf16[1,128,1024]{2,1,0:T(8,128)(2,1)}, u32[]{:S(2)}, u32[]{:S(2)}) collective-permute-start(bf16[1,128,1024]{2,1,0:T(8,128)(2,1)} %dynamic-slice_convert_fusion.2), channel_id=1, source_target_pairs={{0,16},{4,20},{8,24},{12,28},{16,0},{20,4},{24,8},{28,12},{1,17},{... | collective-permute-start | bytes 786440 | tf_op jit(solution)/shard_map/ppermute | solution.py:75
  549.2 14.8 %collective-permute-start.55 = (bf16[1,32,4096]{2,1,0:T(8,128)(2,1)S(1)}, bf16[1,32,4096]{2,1,0:T(8,128)(2,1)S(1)}, u32[]{:S(2)}, u32[]{:S(2)}) collective-permute-start(bf16[1,32,4096]{2,1,0:T(8,128)(2,1)S(1)} %dynamic-slice_convert_fusion), channel_id=1, source_target_pairs={{0,16},{4,20},{8,24},{12,28},{16,0},{20,4},{24,8},{28,12},{1,17},{... | collective-permute-start | bytes 786440 | tf_op jit(solution)/shard_map/ppermute | solution.py:75
  (156 other events, 2271.1 us)
Sparse Core Ops, SparseCore 0:
  11.4 178.6 all-gather.1
